TPU v7x, 32 devices: a whole 2x2x4 slice. The times are simulated.
32 devices in a mesh: chan: 4 (over x, core), filt: 8 (over z, y).
Axes of the slice: x: 2, y: 2, z: 4, core: 2. Of those that a mesh axis runs over, the one named last changes fastest.
Arguments:
- inputs: bfloat16 [1, 64, 128, 1024], P(None, 'filt', None, 'chan'), may hold values from -6 to 6
- weights: bfloat16 [3, 3, 1024, 1024], P(None, None, 'filt', 'chan'), may hold values from -0.0625 to 0.0625
- cotangent: bfloat16 [1, 64, 1024, 128], P(None, 'chan', 'filt'), may hold values from -6 to 6
Outputs:
- outputs: bfloat16 [1, 64, 1024, 128], P(None, 'chan', 'filt')
- input_grad: bfloat16 [1, 64, 128, 1024], P(None, 'filt', None, 'chan')
- weight_grad: float32 [3, 3, 1024, 1024], P(None, None, 'filt', 'chan')
All inputs are finite; a program needn't handle non-finite values.
Results may differ from a plain program's by a relative error of at most 0.001.
Values may be sent and summed in bfloat16 or wider, within the bound.
No kernel may reach another device: no remote copies, remote signals or barrier semaphores. Data moves between devices by JAX's collectives and lax.ppermute only.
A program may use at most 128 MiB of HBM per device.

v0:
```python
import functools
import math

import jax
import jax.numpy as jnp
from jax import lax
from jax.experimental import pallas as pl
from jax.experimental.pallas import tpu as pltpu
from jax.sharding import PartitionSpec as P

F32 = jnp.float32
BF16 = jnp.bfloat16
NT = (((1,), (1,)), ((), ()))
HBM = pl.BlockSpec(memory_space=pltpu.HBM)
VMEM = pl.BlockSpec(memory_space=pltpu.VMEM)
SMEM = pl.BlockSpec(memory_space=pltpu.SMEM)
PAIR = 2


def params(mib):
    return pltpu.CompilerParams(vmem_limit_bytes=mib << 20)


def cost(flops, moved):
    return pl.CostEstimate(flops=int(flops), bytes_accessed=int(moved), transcendentals=0)


def lane_shift(value, by):
    size = value.shape[1]
    lane = lax.broadcasted_iota(jnp.int32, value.shape, 1)
    keep = lane >= by if by > 0 else lane < size + by
    return jnp.where(keep, pltpu.roll(value, by % size, 1), 0.0)


def after(value, *others):
    return lax.optimization_barrier((value,) + others)[0]


def arrivals(depth, line):
    steps = [way for step in range(1, depth) for way in (-step, step)]
    return [way for way in steps if 0 <= line + way < depth]


def arrival(along, depth, line, place):
    picked = None
    for z in range(depth):
        way = arrivals(depth, z)[place]
        value = along[2 * abs(way) - (way < 0)]
        picked = value if picked is None or value is picked else jnp.where(line == z, value, picked)
    return picked


def load_rows(at, parts, rows, sems, first, last):
    height = parts[0][0].shape[0]

    def place(spot):
        return rows.at[pl.ds(1 + spot * height, height)]

    for half in range(PAIR):
        of_side = lax.rem(at[1] + half, PAIR)
        for index, part in enumerate(parts[half]):
            spot = at[4 + index] * PAIR + of_side

            @pl.when(jnp.logical_and(spot >= first, spot <= last))
            def _():
                pltpu.make_async_copy(part, place(spot), sems.at[spot]).start()

    rows[0] = jnp.zeros(rows.shape[1:], rows.dtype)
    rows[rows.shape[0] - 1] = jnp.zeros(rows.shape[1:], rows.dtype)
    return lambda spot: pltpu.make_async_copy(parts[0][0], place(spot), sems.at[spot]).wait()


def forward_kernel(depth, chans, which, at, weights, *refs):
    count = (len(refs) - 5) // 2
    parts = (refs[:count], refs[count : 2 * count])
    keep, send, rows, taps, sems = refs[2 * count :]
    filters, chans_in = weights.shape[2], weights.shape[3]
    width = rows.shape[1]
    block = keep.shape[0]
    height = parts[0][0].shape[0]
    far, core = at[2], at[3]
    top = lax.rem(far + which, chans // 2) * 2 * block
    first, spots = top // height, max(1, 2 * block // height)
    wait = load_rows(at, parts, rows, sems, first - 1, first + spots)
    for tap_row in range(3):
        for tap_col in range(3):
            taps[pl.ds(tap_col * filters, filters), pl.ds(tap_row * chans_in, chans_in)] = weights[tap_row, tap_col]
    for spot in range(-1, spots + 1):

        @pl.when(jnp.logical_and(first + spot >= 0, first + spot < depth * PAIR))
        def _():
            wait(first + spot)

    group = min(4, block)

    @pl.loop(0, block // group)
    def _(step):
        for target, of_core in ((send, 1 - core), (keep, core)):
            start = top + of_core * block + step * group
            window = jnp.concatenate(
                [rows[pl.ds(start + i, group)].reshape(group * width, chans_in) for i in range(3)], axis=1
            )
            product = lax.dot_general(taps[...], window, NT, preferred_element_type=F32)
            for row in range(group):
                part = [
                    product[j * filters : (j + 1) * filters, row * width : (row + 1) * width] for j in range(3)
                ]
                target[step * group + row] = part[1] + lane_shift(part[0], 1) + lane_shift(part[2], -1)


def forward_partial(depth, chans, which, at, weights, own, other):
    height, width, chans_in = own[0].shape
    filters = weights.shape[2]
    rows = height * depth * PAIR
    half = jax.ShapeDtypeStruct((rows // chans, filters, width), F32)
    return pl.pallas_call(
        functools.partial(forward_kernel, depth, chans, which),
        out_shape=(half, half),
        in_specs=[SMEM, VMEM] + [HBM] * (len(own) + len(other)),
        out_specs=(VMEM, VMEM),
        scratch_shapes=[
            pltpu.VMEM((rows + 2, width, chans_in), BF16),
            pltpu.VMEM((3 * filters, 3 * chans_in), BF16),
            pltpu.SemaphoreType.DMA((depth * PAIR,)),
        ],
        compiler_params=params(58),
        cost_estimate=cost(
            36 * rows // chans * width * chans_in * filters, 8 * rows // chans * width * (filters + chans_in)
        ),
        name="forward",
    )(at, weights, *own, *other)


def weight_kernel(depth, scale, at, cot, *refs):
    count = (len(refs) - 4) // 2
    parts = (refs[:count], refs[count : 2 * count])
    out, rows, moved, sems = refs[2 * count :]
    wait = load_rows(at, parts, rows, sems, 0, depth * PAIR - 1)
    filters, width = cot.shape[1], cot.shape[2]
    total = cot.shape[0] - 2
    chans_in = rows.shape[2]
    chunk = min(8, total)
    for spot in range(depth * PAIR):
        wait(spot)
    out[...] = jnp.zeros(out.shape, F32)

    @pl.loop(0, total // chunk)
    def _(step):
        first = step * chunk
        for row in range(chunk):
            value = cot[1 + first + row]
            wide = value.astype(F32)
            lanes = pl.ds(row * width, width)
            moved[0:filters, lanes] = lane_shift(wide, -1).astype(BF16)
            moved[filters : 2 * filters, lanes] = value
            moved[2 * filters :, lanes] = lane_shift(wide, 1).astype(BF16)
        for tap_row in range(3):
            window = rows[pl.ds(first + tap_row, chunk)].reshape(chunk * width, chans_in)
            out[tap_row] += jnp.dot(moved[...], window, preferred_element_type=F32)

    out[...] = out[...] * scale


def weight_gradient(depth, at, scale, cot, own, other):
    width, chans_in = own[0].shape[1:]
    rows, filters = cot.shape[0] - 2, cot.shape[1]
    return pl.pallas_call(
        functools.partial(weight_kernel, depth, scale),
        out_shape=jax.ShapeDtypeStruct((3, 3 * filters, chans_in), F32),
        in_specs=[SMEM, VMEM] + [HBM] * (len(own) + len(other)),
        out_specs=VMEM,
        scratch_shapes=[
            pltpu.VMEM((rows + 2, width, chans_in), BF16),
            pltpu.VMEM((3 * filters, min(8, rows) * width), BF16),
            pltpu.SemaphoreType.DMA((depth * PAIR,)),
        ],
        compiler_params=params(58),
        cost_estimate=cost(18 * rows * width * chans_in * filters, 2 * rows * width * (filters + chans_in)),
        name="weight_gradient",
    )(at, cot, *own, *other)


def turn_kernel(same, cross, out):
    fars, _, rows = same.shape[:3]
    unroll = max(n for n in (1, 2, 3, 6) if rows % n == 0)

    @pl.loop(0, rows // unroll)
    def _(step):
        for n in range(unroll):
            row = step * unroll + n
            out[0, row] = jnp.concatenate([part[far, 0, row] for far in range(fars) for part in (same, cross)], axis=0).T


def turned(same, cross):
    fars, depth, rows, part, width = same.shape
    filters = 2 * fars * part
    spec = pl.BlockSpec((fars, 1, rows, part, width), lambda d: (0, d, 0, 0, 0))
    return pl.pallas_call(
        turn_kernel,
        grid=(depth,),
        out_shape=jax.ShapeDtypeStruct((depth, rows, width, filters), BF16),
        in_specs=[spec, spec],
        out_specs=pl.BlockSpec((1, rows, width, filters), lambda d: (d, 0, 0, 0)),
        compiler_params=params(58),
        cost_estimate=cost(0, 4 * depth * rows * width * filters),
        name="turned",
    )(same, cross)


def input_kernel(chans, index, at, cot, kernels, keep, send, source, taps, stacked, sems):
    side, far, core = at[1], at[2], at[3]
    depth, rows, width, filters = source.shape
    rows = rows - 2
    chans_in = taps.shape[3]
    copies = []
    for n in range(depth):
        copies.append(
            (
                pltpu.make_async_copy(
                    kernels.at[n, :, :, pl.ds(index * chans_in, chans_in)], taps.at[n], sems.at[n, 0]
                ),
                pltpu.make_async_copy(cot.at[n], source.at[n], sems.at[n, 1]),
            )
        )
        for copy in copies[n]:
            copy.start()
    part = filters // chans
    places = chans if part % 16 == 0 else 1
    size = filters // places
    for n in range(depth):
        copies[n][0].wait()
        for place in range(places):
            chan = lax.rem(far - place // 2 + chans // 2, chans // 2) * 2 + lax.rem(core + place, 2)
            of_chan = pl.ds(0 if places == 1 else pl.multiple_of(chan * size, size), size)
            for i in range(3):
                for j in range(3):
                    stacked[
                        pl.ds((n * 3 + i) * filters + place * size, size), pl.ds(j * chans_in, chans_in)
                    ] = taps[n, 3 * i + j, of_chan]
    for n in range(depth):
        copies[n][1].wait()
    half = rows // PAIR
    chunk = min(8, half)
    lanes = lax.broadcasted_iota(jnp.int32, (width, chans_in), 0)

    for out, of_side in ((send, 1 - side), (keep, side)):

        @pl.loop(0, half // chunk)
        def _(step):
            first = of_side * half + step * chunk
            window = [
                source[n, pl.ds(first + 2 - i, chunk)].reshape(chunk * width, filters)
                for n in range(depth)
                for i in range(3)
            ]
            if filters % 128 == 0:
                product = jnp.dot(jnp.concatenate(window, axis=1), stacked[...], preferred_element_type=F32)
            else:
                product = sum(
                    jnp.dot(value, stacked[n * filters : (n + 1) * filters], preferred_element_type=F32)
                    for n, value in enumerate(window)
                )
            for row in range(chunk):
                here = [
                    product[row * width : (row + 1) * width, j * chans_in : (j + 1) * chans_in] for j in range(3)
                ]
                before_it = jnp.where(lanes < width - 1, pltpu.roll(here[0], width - 1, 0), 0.0)
                behind_it = jnp.where(lanes >= 1, pltpu.roll(here[2], 1, 0), 0.0)
                out[step * chunk + row] = here[1] + before_it + behind_it


def input_partial(chans, at, cot, kernels, index, halves):
    depth, rows, width, filters = cot.shape
    rows = rows - 2
    chans_in = kernels.shape[3] // halves
    half = jax.ShapeDtypeStruct((rows // PAIR, width, chans_in), F32)
    return pl.pallas_call(
        functools.partial(input_kernel, chans, index),
        out_shape=(half, half),
        in_specs=[SMEM, HBM, HBM],
        out_specs=(VMEM, VMEM),
        scratch_shapes=[
            pltpu.VMEM(cot.shape, BF16),
            pltpu.VMEM(kernels.shape[:3] + (chans_in,), BF16),
            pltpu.VMEM((depth * 3 * filters, 3 * chans_in), BF16),
            pltpu.SemaphoreType.DMA((depth, 2)),
        ],
        compiler_params=params(58),
        cost_estimate=cost(
            18 * rows * width * chans_in * filters * depth, 2 * depth * filters * ((rows + 2) * width + 9 * chans_in)
        ),
        name="input_gradient",
    )(at, cot, kernels)


def fars_gather(value, chans):
    got = [value]
    for step in range(1, chans // 2):
        got.append(lax.ppermute(value, "chan", [(c, (c + 2 * step) % chans) for c in range(chans)]))
    return jnp.stack(got)


def lines(depth):
    return [[z * PAIR + y for z in range(depth)] for y in range(PAIR)]


def line_steps(step, depth):
    up = [(z * PAIR + y, (z + 1) * PAIR + y) for z in range(step - 1, depth - 1) for y in range(PAIR)]
    down = [(z * PAIR + y, (z - 1) * PAIR + y) for z in range(1, depth - step + 1) for y in range(PAIR)]
    return up, down


def line_step(along, step, depth):
    up, down = line_steps(step, depth)
    below, above = along[0 if step == 1 else -2], along[0 if step == 1 else -1]
    return [lax.ppermute(below, "filt", up), lax.ppermute(above, "filt", down)]


def core_swap(value, chans):
    return lax.ppermute(value, "chan", [(c, c ^ 1) for c in range(chans)])


def pair_swap(value, depth):
    pairs = [(z * PAIR + y, z * PAIR + 1 - y) for z in range(depth) for y in range(PAIR)]
    return lax.ppermute(value, "filt", pairs)


def body(inputs, weights, cotangent):
    chans, filts = lax.axis_size("chan"), lax.axis_size("filt")
    depth = filts // PAIR
    chan, filt = lax.axis_index("chan"), lax.axis_index("filt")
    line, side = filt // PAIR, filt % PAIR
    far, core = chan // 2, chan % 2
    spots = jnp.asarray([[z] + [z + way for way in arrivals(depth, z)] for z in range(depth)], jnp.int32)
    at = jnp.concatenate([jnp.stack([line, side, far, core]).astype(jnp.int32), spots[line]])
    own_rows, width, chans_in = inputs.shape[1:]
    block, filters = cotangent.shape[1], cotangent.shape[2]
    height = own_rows * filts
    scale = 1.0 / math.sqrt(inputs.shape[0] * height * width)

    part = filters // chans
    line_rows = own_rows * PAIR

    def all_rows(same):
        cross = core_swap(same, chans)
        padded = jnp.zeros((height + 2, filters, width), BF16)
        for step in range(chans // 2):
            at_far = lax.rem(far - step + chans // 2, chans // 2) * 2
            padded = lax.dynamic_update_slice(padded, same[step], (1 + (at_far + core) * block, 0, 0))
            padded = lax.dynamic_update_slice(padded, cross[step], (1 + (at_far + 1 - core) * block, 0, 0))
        return padded

    def line_pieces(padded):
        own_part = lax.dynamic_slice_in_dim(padded, chan * part, part, axis=1)
        return jnp.stack([own_part[z * line_rows : (z + 1) * line_rows + 2] for z in range(depth)])

    def exchange(pieces):
        return lax.all_to_all(pieces, "filt", 0, 0, axis_index_groups=lines(depth), tiled=True)

    along, mine, theirs = [inputs[0]], [inputs[0]], [pair_swap(inputs[0], depth)]
    same, gate = fars_gather(cotangent[0], chans), []
    padded = pieces = None
    kernels = weights
    for step in range(1, depth + 1):
        along = list(lax.optimization_barrier(tuple(along + gate)))[: len(along)]
        if step < depth:
            along += line_step(along, step, depth)
        if step == 1:
            gate = along[1:] + theirs + [same]
            continue
        mine.append(arrival(along, depth, line, step - 2))
        theirs.append(pair_swap(mine[-1], depth))
        before, gate = gate, along[-2:] + theirs[-1:]
        if step == 2:
            padded = all_rows(after(same, *before))
            pieces = exchange(line_pieces(padded))
            gate.append(pieces)
        elif step == 3:
            kernels = after(weights, *before)
            same = fars_gather(after(pieces, *before), chans)
            gate.append(same)
    kernels = lax.all_gather(kernels, "filt", axis=0, axis_index_groups=lines(depth))
    kernels = kernels.reshape((depth, 9) + weights.shape[2:])
    if depth < 3:
        same = fars_gather(pieces, chans)
    sources = turned(same, core_swap(same, chans))

    if part % 16:
        order = [(far - c // 2 + chans // 2) % (chans // 2) * 2 + (core + c) % 2 for c in range(chans)]
        split = kernels.reshape((depth, 9, chans, part, chans_in))
        kernels = jnp.take(split, jnp.stack(order), axis=2).reshape(kernels.shape)

    halves = PAIR if chans_in % (PAIR * 128) == 0 else 1
    fars = chans // 2
    at_next = after(at, sources, kernels)
    outputs, input_grad = None, []
    for n, which in enumerate([*range(1, fars), 0]):
        keep, send = forward_partial(depth, chans, which, at_next, weights, mine, theirs)
        at_next = after(at, send)
        moving = keep + core_swap(send, chans)
        if which:
            if not input_grad:
                kept, sent = input_partial(chans, at_next, sources, kernels, 0, halves)
                at_next = after(at, sent)
                input_grad.append((kept + pair_swap(sent, depth)).astype(BF16))
            at_next = after(at_next, moving)
            moving = lax.ppermute(moving, "chan", [(c, (c + 2 * which) % chans) for c in range(chans)])
        outputs = moving if outputs is None else outputs + moving
    outputs = outputs.astype(BF16)[None]
    for index in range(len(input_grad), halves):
        kept, sent = input_partial(chans, at_next, sources, kernels, index, halves)
        at_next = after(at, sent)
        input_grad.append((kept + pair_swap(sent, depth)).astype(BF16))
    input_grad = jnp.concatenate(input_grad, axis=2)[None]

    weight_grad = weight_gradient(depth, at_next, scale, padded, mine, theirs)
    weight_grad = weight_grad.reshape((3, 3, filters, chans_in))
    return (outputs, input_grad, weight_grad)


def solution(mesh):
    return jax.shard_map(
        body,
        mesh=mesh,
        in_specs=(
            P(None, "filt", None, "chan"),
            P(None, None, "filt", "chan"),
            P(None, "chan", "filt", None),
        ),
        out_specs=(
            P(None, "chan", "filt", None),
            P(None, "filt", None, "chan"),
            P(None, None, "filt", "chan"),
        ),
        check_vma=False,
    )
```

profile of v0, /device:TPU:0, one launch (start us, length us, event | category | flops | bytes accessed | tf_op | source)
XLA Modules:
  0.0 179.2 jit_solution(17815697645333535239)
XLA Ops:
  7.2 3.0 %collective-permute-start = (bf16[16,128,128]{2,1,0:T(8,128)(2,1)}, bf16[16,128,128]{2,1,0:T(8,128)(2,1)S(1)}, u32[]{:S(2)}, u32[]{:S(2)}) collective-permute-start(bf16[16,128,128]{2,1,0:T(8,128)(2,1)} %bitcast.39), channel_id=1, source_target_pairs={{0,16},{8,24},{16,0},{24,8},{1,17},{9,25},{17,1},{25,9},{2,18},{10... | collective-permute-start | bytes 1572872 | tf_op jit(solution)/shard_map/ppermute | solution.py:299
  10.2 1.3 collective-permute-start.2
  11.5 5.4 %collective-permute-start.1 = (bf16[8,128,256]{2,1,0:T(8,128)(2,1)}, bf16[8,128,256]{2,1,0:T(8,128)(2,1)}, u32[]{:S(2)}, u32[]{:S(2)}) collective-permute-start(bf16[8,128,256]{2,1,0:T(8,128)(2,1)} %bitcast.44), channel_id=1, source_target_pairs={{0,2},{1,3},{2,4},{3,5},{4,6},{5,7},{8,10},{9,11},{10,12},{11,13},... | collective-permute-start | bytes 1572872 | tf_op jit(solution)/shard_map/ppermute | solution.py:316
  16.8 1.5 collective-permute-start.3
  18.3 4.0 %collective-permute-done = bf16[16,128,128]{2,1,0:T(8,128)(2,1)S(1)} collective-permute-done((bf16[16,128,128]{2,1,0:T(8,128)(2,1)}, bf16[16,128,128]{2,1,0:T(8,128)(2,1)S(1)}, u32[]{:S(2)}, u32[]{:S(2)}) %collective-permute-start) | collective-permute-done | bytes 524320 | tf_op jit(solution)/shard_map/ppermute | solution.py:299
  22.3 1.1 pad_maximum_fusion.1
  23.4 2.2 %collective-permute-done.2 = bf16[8,128,256]{2,1,0:T(8,128)(2,1)S(1)} collective-permute-done((bf16[8,128,256]{2,1,0:T(8,128)(2,1)}, bf16[8,128,256]{2,1,0:T(8,128)(2,1)S(1)}, u32[]{:S(2)}, u32[]{:S(2)}) %collective-permute-start.2) | collective-permute-done | bytes 524320 | tf_op jit(solution)/shard_map/ppermute | solution.py:316
  25.6 1.3 collective-permute-done.1
  26.9 2.9 %collective-permute-done.3.refs_4_ = bf16[8,128,256]{2,1,0:T(8,128)(2,1)S(1)} collective-permute-done((bf16[8,128,256]{2,1,0:T(8,128)(2,1)}, bf16[8,128,256]{2,1,0:T(8,128)(2,1)S(1)}, u32[]{:S(2)}, u32[]{:S(2)}) %collective-permute-start.3) | collective-permute-done | bytes 524320 | tf_op jit(solution)/shard_map/ppermute | solution.py:325
  31.3 2.2 %collective-permute-done.4 = bf16[2,16,128,128]{3,2,1,0:T(8,128)(2,1)} collective-permute-done((bf16[2,16,128,128]{3,2,1,0:T(8,128)(2,1)S(1)}, bf16[2,16,128,128]{3,2,1,0:T(8,128)(2,1)}, u32[]{:S(2)}, u32[]{:S(2)}) %collective-permute-start.4) | collective-permute-done | bytes 1048608 | tf_op jit(solution)/shard_map/ppermute | solution.py:320
  33.4 1.1 fusion.3
  34.7 1.1 fusion.2.cot
  37.0 3.5 %all-to-all-start = ((bf16[4,18,32,128]{3,2,1,0:T(8,128)(2,1)}), bf16[4,18,32,128]{3,2,1,0:T(8,128)(2,1)S(1)}, u32[]{:S(2)}, u32[]{:S(2)}) async-start(bf16[4,18,32,128]{3,2,1,0:T(8,128)(2,1)} %pad_maximum_fusion.2), calls=%async_computation | async-start | bytes 1179648 | tf_op jit(solution)/shard_map/all_to_all | solution.py:358
  40.5 1.3 select_select_fusion.1.refs_1_
  41.8 1.6 collective-permute-start.7
  44.1 1.3 collective-permute-start.6
  45.4 10.5 %collective-permute-done.7.refs_5_ = bf16[8,128,256]{2,1,0:T(8,128)(2,1)S(1)} collective-permute-done((bf16[8,128,256]{2,1,0:T(8,128)(2,1)S(1)}, bf16[8,128,256]{2,1,0:T(8,128)(2,1)S(1)}, u32[]{:S(2)}, u32[]{:S(2)}) %collective-permute-start.7) | collective-permute-done | bytes 524320 | tf_op jit(solution)/shard_map/ppermute | solution.py:325
  56.7 8.2 %collective-permute-done.6 = bf16[8,128,256]{2,1,0:T(8,128)(2,1)S(1)} collective-permute-done((bf16[8,128,256]{2,1,0:T(8,128)(2,1)}, bf16[8,128,256]{2,1,0:T(8,128)(2,1)S(1)}, u32[]{:S(2)}, u32[]{:S(2)}) %collective-permute-start.6) | collective-permute-done | bytes 524320 | tf_op jit(solution)/shard_map/ppermute | solution.py:316
  65.4 1.1 fusion.refs_2_
  68.2 1.3 collective-permute-start.11
  69.5 9.7 %collective-permute-done.8 = bf16[4,18,32,128]{3,2,1,0:T(8,128)(2,1)S(1)} collective-permute-done((bf16[4,18,32,128]{3,2,1,0:T(8,128)(2,1)S(1)}, bf16[4,18,32,128]{3,2,1,0:T(8,128)(2,1)S(1)}, u32[]{:S(2)}, u32[]{:S(2)}) %collective-permute-start.8) | collective-permute-done | bytes 589856 | tf_op jit(solution)/shard_map/ppermute | solution.py:299
  79.3 1.2 pad_maximum_fusion.same
  80.6 32.5 %collective-permute-done.11 = bf16[8,128,256]{2,1,0:T(8,128)(2,1)S(1)} collective-permute-done((bf16[8,128,256]{2,1,0:T(8,128)(2,1)S(1)}, bf16[8,128,256]{2,1,0:T(8,128)(2,1)S(1)}, u32[]{:S(2)}, u32[]{:S(2)}) %collective-permute-start.11) | collective-permute-done | bytes 524320 | tf_op jit(solution)/shard_map/ppermute | solution.py:316
  116.6 4.4 %turned.1.cot = bf16[4,18,128,128]{3,2,1,0:T(8,128)(2,1)} custom-call(bf16[2,4,18,32,128]{4,3,2,1,0:T(8,128)(2,1)} %copy-done, bf16[2,4,18,32,128]{4,3,2,1,0:T(8,128)(2,1)} %copy-done.4), custom_call_target="tpu_custom_call" | custom-call | bytes 4718592 | tf_op jit(solution)/shard_map/turned/pallas_call | solution.py:198
  121.0 2.2 %all-gather.3.cloned.1.call-done = bf16[12,3,128,256]{3,2,1,0:T(8,128)(2,1)} async-done(((bf16[3,3,128,256]{3,2,1,0:T(8,128)(2,1)}), bf16[12,3,128,256]{3,2,1,0:T(8,128)(2,1)}) %all-gather.3.cloned.1.call-update) | async-done | bytes 2359312 | tf_op jit(solution)/shard_map/all_gather | solution.py:382
  124.2 7.5 %forward.2 = (f32[16,128,128]{2,1,0:T(8,128)}, f32[16,128,128]{2,1,0:T(8,128)}) custom-call(s32[8]{0:T(128)} %concatenate.6.at, bf16[3,3,128,256]{3,2,1,0:T(8,128)(2,1)} %weights.3, bf16[8,128,256]{2,1,0:T(8,128)(2,1)} %bitcast.46, bf16[8,128,256]{2,1,0:T(8,128)(2,1)} %copy-done.7, bf16[8,128,256]{2,1,0:T(8,128)(2,1)} %copy-done.10, ...), custom_call_target="tpu_custom_call" | custom-call | flops 2415919104 | bytes 6291456 | tf_op jit(solution)/shard_map/forward/pallas_call | solution.py:116
  131.7 7.0 %input_gradient.2 = (f32[8,128,128]{2,1,0:T(8,128)}, f32[8,128,128]{2,1,0:T(8,128)}) custom-call(s32[8]{0:T(128)} %concatenate.6.at, bf16[4,18,128,128]{3,2,1,0:T(8,128)(2,1)} %turned.1.cot, bf16[4,9,128,256]{3,2,1,0:T(8,128)(2,1)} %bitcast.41), custom_call_target="tpu_custom_call" | custom-call | flops 2415919104 | bytes 3538944 | tf_op jit(solution)/shard_map/input_gradient/pallas_call | solution.py:277
  139.3 1.7 collective-permute-start.15
  141.0 7.5 %forward.3 = (f32[16,128,128]{2,1,0:T(8,128)}, f32[16,128,128]{2,1,0:T(8,128)}) custom-call(s32[8]{0:T(128)} %concatenate.6.at, bf16[3,3,128,256]{3,2,1,0:T(8,128)(2,1)} %weights.3, bf16[8,128,256]{2,1,0:T(8,128)(2,1)} %bitcast.47, bf16[8,128,256]{2,1,0:T(8,128)(2,1)} %copy-done.7, bf16[8,128,256]{2,1,0:T(8,128)(2,1)} %copy-done.10, ...), custom_call_target="tpu_custom_call" | custom-call | flops 2415919104 | bytes 6291456 | tf_op jit(solution)/shard_map/forward/pallas_call | solution.py:116
  148.7 7.0 %input_gradient.3 = (f32[8,128,128]{2,1,0:T(8,128)}, f32[8,128,128]{2,1,0:T(8,128)}) custom-call(s32[8]{0:T(128)} %concatenate.6.at, bf16[4,18,128,128]{3,2,1,0:T(8,128)(2,1)} %turned.1.cot, bf16[4,9,128,256]{3,2,1,0:T(8,128)(2,1)} %bitcast.42), custom_call_target="tpu_custom_call" | custom-call | flops 2415919104 | bytes 3538944 | tf_op jit(solution)/shard_map/input_gradient/pallas_call | solution.py:277
  155.7 2.0 %collective-permute-start.18 = (f32[8,128,128]{2,1,0:T(8,128)}, f32[8,128,128]{2,1,0:T(8,128)S(1)}, u32[]{:S(2)}, u32[]{:S(2)}) collective-permute-start(f32[8,128,128]{2,1,0:T(8,128)} %get-tuple-element.53), channel_id=1, source_target_pairs={{0,1},{1,0},{2,3},{3,2},{4,5},{5,4},{6,7},{7,6},{8,9},{9,8},{10,11... | collective-permute-start | bytes 1572872 | tf_op jit(solution)/shard_map/ppermute | solution.py:325
  157.8 11.8 %weight_gradient.1 = f32[3,384,256]{2,1,0:T(8,128)} custom-call(s32[8]{0:T(128)} %concatenate.6.at, bf16[66,128,128]{2,1,0:T(8,128)(2,1)} %copy-done.1, bf16[8,128,256]{2,1,0:T(8,128)(2,1)} %bitcast.48, bf16[8,128,256]{2,1,0:T(8,128)(2,1)} %copy-done.7, bf16[8,128,256]{2,1,0:T(8,128)(2,1)} %copy-done.10, bf16[8,128,256]{2,1,0:T(8,128)(2,1)} %select_select_fusion.2.refs_3_, ...), custom_call_target="tpu_custom_call" | custom-call | flops 4831838208 | bytes 6291456 | tf_op jit(solution)/shard_map/weight_gradient/pallas_call | solution.py:167
  (66 shorter events, 14.6 us)
Async XLA Ops:
  7.2 15.1 %collective-permute-start = (bf16[16,128,128]{2,1,0:T(8,128)(2,1)}, bf16[16,128,128]{2,1,0:T(8,128)(2,1)S(1)}, u32[]{:S(2)}, u32[]{:S(2)}) collective-permute-start(bf16[16,128,128]{2,1,0:T(8,128)(2,1)} %bitcast.39), channel_id=1, source_target_pairs={{0,16},{8,24},{16,0},{24,8},{1,17},{9,25},{17,1},{25,9},{2,18},{10... | collective-permute-start | bytes 1572872 | tf_op jit(solution)/shard_map/ppermute | solution.py:299
  10.2 15.5 %collective-permute-start.2 = (bf16[8,128,256]{2,1,0:T(8,128)(2,1)}, bf16[8,128,256]{2,1,0:T(8,128)(2,1)S(1)}, u32[]{:S(2)}, u32[]{:S(2)}) collective-permute-start(bf16[8,128,256]{2,1,0:T(8,128)(2,1)} %bitcast.43), channel_id=1, source_target_pairs={{2,0},{3,1},{4,2},{5,3},{6,4},{7,5},{10,8},{11,9},{12,10},{13,11},... | collective-permute-start | bytes 1572872 | tf_op jit(solution)/shard_map/ppermute | solution.py:316
  11.5 15.5 %collective-permute-start.1 = (bf16[8,128,256]{2,1,0:T(8,128)(2,1)}, bf16[8,128,256]{2,1,0:T(8,128)(2,1)}, u32[]{:S(2)}, u32[]{:S(2)}) collective-permute-start(bf16[8,128,256]{2,1,0:T(8,128)(2,1)} %bitcast.44), channel_id=1, source_target_pairs={{0,2},{1,3},{2,4},{3,5},{4,6},{5,7},{8,10},{9,11},{10,12},{11,13},... | collective-permute-start | bytes 1572872 | tf_op jit(solution)/shard_map/ppermute | solution.py:316
  16.8 13.0 %collective-permute-start.3 = (bf16[8,128,256]{2,1,0:T(8,128)(2,1)}, bf16[8,128,256]{2,1,0:T(8,128)(2,1)S(1)}, u32[]{:S(2)}, u32[]{:S(2)}) collective-permute-start(bf16[8,128,256]{2,1,0:T(8,128)(2,1)} %bitcast.45), channel_id=1, source_target_pairs={{0,1},{1,0},{2,3},{3,2},{4,5},{5,4},{6,7},{7,6},{8,9},{9,8},{10,11... | collective-permute-start | bytes 1572872 | tf_op jit(solution)/shard_map/ppermute | solution.py:325
  25.6 1.3 copy-start.3
  30.6 2.8 %collective-permute-start.4 = (bf16[2,16,128,128]{3,2,1,0:T(8,128)(2,1)S(1)}, bf16[2,16,128,128]{3,2,1,0:T(8,128)(2,1)}, u32[]{:S(2)}, u32[]{:S(2)}) collective-permute-start(bf16[2,16,128,128]{3,2,1,0:T(8,128)(2,1)S(1)} %pad_maximum_fusion.1), channel_id=1, source_target_pairs={{0,8},{8,0},{16,24},{24,16},{1,9},{9,1},{17,25},{25,17},{2,10},{10... | collective-permute-start | bytes 3145736 | tf_op jit(solution)/shard_map/ppermute | solution.py:320
  35.8 6.0 %copy-start.1 = (bf16[66,128,128]{2,1,0:T(8,128)(2,1)}, bf16[66,128,128]{2,1,0:T(8,128)(2,1)S(1)}, u32[]{:S(2)}) copy-start(bf16[66,128,128]{2,1,0:T(8,128)(2,1)S(1)} %fusion.2.cot) | copy-start | bytes 6488068
  37.0 27.9 %all-to-all-start = ((bf16[4,18,32,128]{3,2,1,0:T(8,128)(2,1)}), bf16[4,18,32,128]{3,2,1,0:T(8,128)(2,1)S(1)}, u32[]{:S(2)}, u32[]{:S(2)}) async-start(bf16[4,18,32,128]{3,2,1,0:T(8,128)(2,1)} %pad_maximum_fusion.2), calls=%async_computation | async-start | bytes 1179648 | tf_op jit(solution)/shard_map/all_to_all | solution.py:358
  40.5 82.7 %all-gather.3.cloned.1.call-start = ((), (), s32[]{:S(2)}) async-start(), calls=%async_computation.1 | async-start | bytes 2949120 | tf_op jit(solution)/shard_map/all_gather | solution.py:382
  41.8 14.1 %copy-start.7 = (bf16[8,128,256]{2,1,0:T(8,128)(2,1)}, bf16[8,128,256]{2,1,0:T(8,128)(2,1)S(1)}, u32[]{:S(2)}) copy-start(bf16[8,128,256]{2,1,0:T(8,128)(2,1)S(1)} %select_select_fusion.1.refs_1_) | copy-start | bytes 1572868
  41.8 14.0 %collective-permute-start.7 = (bf16[8,128,256]{2,1,0:T(8,128)(2,1)S(1)}, bf16[8,128,256]{2,1,0:T(8,128)(2,1)S(1)}, u32[]{:S(2)}, u32[]{:S(2)}) collective-permute-start(bf16[8,128,256]{2,1,0:T(8,128)(2,1)S(1)} %select_select_fusion.1.refs_1_), channel_id=1, source_target_pairs={{0,1},{1,0},{2,3},{3,2},{4,5},{5,4},{6,7},{7,6},{8,9},{9,8},{10,11... | collective-permute-start | bytes 1572872 | tf_op jit(solution)/shard_map/ppermute | solution.py:325
  43.4 12.5 %collective-permute-start.5 = (bf16[8,128,256]{2,1,0:T(8,128)(2,1)}, bf16[8,128,256]{2,1,0:T(8,128)(2,1)S(1)}, u32[]{:S(2)}, u32[]{:S(2)}) collective-permute-start(bf16[8,128,256]{2,1,0:T(8,128)(2,1)} %collective-permute-done.1), channel_id=1, source_target_pairs={{2,4},{3,5},{4,6},{5,7},{10,12},{11,13},{12,14},{13,15},{18,20},{1... | collective-permute-start | bytes 1572872 | tf_op jit(solution)/shard_map/ppermute | solution.py:316
  44.1 20.7 %collective-permute-start.6 = (bf16[8,128,256]{2,1,0:T(8,128)(2,1)}, bf16[8,128,256]{2,1,0:T(8,128)(2,1)S(1)}, u32[]{:S(2)}, u32[]{:S(2)}) collective-permute-start(bf16[8,128,256]{2,1,0:T(8,128)(2,1)} %copy-done.3), channel_id=1, source_target_pairs={{2,0},{3,1},{4,2},{5,3},{10,8},{11,9},{12,10},{13,11},{18,16},{19,... | collective-permute-start | bytes 1572872 | tf_op jit(solution)/shard_map/ppermute | solution.py:316
  64.8 14.4 %copy-start.2 = (bf16[4,18,32,128]{3,2,1,0:T(8,128)(2,1)}, bf16[4,18,32,128]{3,2,1,0:T(8,128)(2,1)S(1)}, u32[]{:S(2)}) copy-start(bf16[4,18,32,128]{3,2,1,0:T(8,128)(2,1)S(1)} %all-to-all-done) | copy-start | bytes 1769476
  64.9 14.4 %collective-permute-start.8 = (bf16[4,18,32,128]{3,2,1,0:T(8,128)(2,1)S(1)}, bf16[4,18,32,128]{3,2,1,0:T(8,128)(2,1)S(1)}, u32[]{:S(2)}, u32[]{:S(2)}) collective-permute-start(bf16[4,18,32,128]{3,2,1,0:T(8,128)(2,1)S(1)} %all-to-all-done), channel_id=1, source_target_pairs={{0,16},{8,24},{16,0},{24,8},{1,17},{9,25},{17,1},{25,9},{2,18},{10... | collective-permute-start | bytes 1769480 | tf_op jit(solution)/shard_map/ppermute | solution.py:299
  66.6 47.4 %copy-start.10 = (bf16[8,128,256]{2,1,0:T(8,128)(2,1)}, bf16[8,128,256]{2,1,0:T(8,128)(2,1)S(1)}, u32[]{:S(2)}) copy-start(bf16[8,128,256]{2,1,0:T(8,128)(2,1)S(1)} %fusion.refs_2_) | copy-start | bytes 1572868
  66.6 13.9 %collective-permute-start.12 = (bf16[8,128,256]{2,1,0:T(8,128)(2,1)S(1)}, bf16[8,128,256]{2,1,0:T(8,128)(2,1)S(1)}, u32[]{:S(2)}, u32[]{:S(2)}) collective-permute-start(bf16[8,128,256]{2,1,0:T(8,128)(2,1)S(1)} %fusion.refs_2_), channel_id=1, source_target_pairs={{0,1},{1,0},{2,3},{3,2},{4,5},{5,4},{6,7},{7,6},{8,9},{9,8},{10,11... | collective-permute-start | bytes 1572872 | tf_op jit(solution)/shard_map/ppermute | solution.py:325
  67.5 13.0 %collective-permute-start.10 = (bf16[8,128,256]{2,1,0:T(8,128)(2,1)S(1)}, bf16[8,128,256]{2,1,0:T(8,128)(2,1)S(1)}, u32[]{:S(2)}, u32[]{:S(2)}) collective-permute-start(bf16[8,128,256]{2,1,0:T(8,128)(2,1)S(1)} %collective-permute-done.5), channel_id=1, source_target_pairs={{4,6},{5,7},{12,14},{13,15},{20,22},{21,23},{28,30},{29,31}} | collective-permute-start | bytes 1572872 | tf_op jit(solution)/shard_map/ppermute | solution.py:316
  68.2 44.8 %collective-permute-start.11 = (bf16[8,128,256]{2,1,0:T(8,128)(2,1)S(1)}, bf16[8,128,256]{2,1,0:T(8,128)(2,1)S(1)}, u32[]{:S(2)}, u32[]{:S(2)}) collective-permute-start(bf16[8,128,256]{2,1,0:T(8,128)(2,1)S(1)} %collective-permute-done.6), channel_id=1, source_target_pairs={{2,0},{3,1},{10,8},{11,9},{18,16},{19,17},{26,24},{27,25}} | collective-permute-start | bytes 1572872 | tf_op jit(solution)/shard_map/ppermute | solution.py:316
  80.4 35.1 %copy-start = (bf16[2,4,18,32,128]{4,3,2,1,0:T(8,128)(2,1)}, bf16[2,4,18,32,128]{4,3,2,1,0:T(8,128)(2,1)S(1)}, u32[]{:S(2)}) copy-start(bf16[2,4,18,32,128]{4,3,2,1,0:T(8,128)(2,1)S(1)} %pad_maximum_fusion.same) | copy-start | bytes 3538948
  80.4 35.0 %collective-permute-start.9 = (bf16[2,4,18,32,128]{4,3,2,1,0:T(8,128)(2,1)S(1)}, bf16[2,4,18,32,128]{4,3,2,1,0:T(8,128)(2,1)S(1)}, u32[]{:S(2)}, u32[]{:S(2)}) collective-permute-start(bf16[2,4,18,32,128]{4,3,2,1,0:T(8,128)(2,1)S(1)} %pad_maximum_fusion.same), channel_id=1, source_target_pairs={{0,8},{8,0},{16,24},{24,16},{1,9},{9,1},{17,25},{25,17},{2,10},{10... | collective-permute-start | bytes 3538952 | tf_op jit(solution)/shard_map/ppermute | solution.py:320
  80.5 33.4 %copy-start.13 = (bf16[8,128,256]{2,1,0:T(8,128)(2,1)}, bf16[8,128,256]{2,1,0:T(8,128)(2,1)S(1)}, u32[]{:S(2)}) copy-start(bf16[8,128,256]{2,1,0:T(8,128)(2,1)S(1)} %collective-permute-done.12.refs_6_) | copy-start | bytes 1572868
  114.0 9.4 %collective-permute-start.13 = (bf16[8,128,256]{2,1,0:T(8,128)(2,1)}, bf16[8,128,256]{2,1,0:T(8,128)(2,1)S(1)}, u32[]{:S(2)}, u32[]{:S(2)}) collective-permute-start(bf16[8,128,256]{2,1,0:T(8,128)(2,1)} %select_select_fusion.2.refs_3_), channel_id=1, source_target_pairs={{0,1},{1,0},{2,3},{3,2},{4,5},{5,4},{6,7},{7,6},{8,9},{9,8},{10,11... | collective-permute-start | bytes 1572872 | tf_op jit(solution)/shard_map/ppermute | solution.py:325
  131.7 7.5 %copy-start.6 = (f32[16,128,128]{2,1,0:T(8,128)S(1)}, f32[16,128,128]{2,1,0:T(8,128)}, u32[]{:S(2)}) copy-start(f32[16,128,128]{2,1,0:T(8,128)} %get-tuple-element.42) | copy-start | bytes 3145732
  131.7 7.5 %collective-permute-start.14 = (f32[16,128,128]{2,1,0:T(8,128)}, f32[16,128,128]{2,1,0:T(8,128)S(1)}, u32[]{:S(2)}, u32[]{:S(2)}) collective-permute-start(f32[16,128,128]{2,1,0:T(8,128)} %get-tuple-element.43), channel_id=1, source_target_pairs={{0,8},{8,0},{16,24},{24,16},{1,9},{9,1},{17,25},{25,17},{2,10},{10... | collective-permute-start | bytes 3145736 | tf_op jit(solution)/shard_map/ppermute | solution.py:320
  138.8 18.9 %collective-permute-start.17 = (f32[8,128,128]{2,1,0:T(8,128)}, f32[8,128,128]{2,1,0:T(8,128)S(1)}, u32[]{:S(2)}, u32[]{:S(2)}) collective-permute-start(f32[8,128,128]{2,1,0:T(8,128)} %get-tuple-element.45), channel_id=1, source_target_pairs={{0,1},{1,0},{2,3},{3,2},{4,5},{5,4},{6,7},{7,6},{8,9},{9,8},{10,11... | collective-permute-start | bytes 1572872 | tf_op jit(solution)/shard_map/ppermute | solution.py:325
  139.3 32.0 %collective-permute-start.15 = (f32[16,128,128]{2,1,0:T(8,128)S(1)}, f32[16,128,128]{2,1,0:T(8,128)S(1)}, u32[]{:S(2)}, u32[]{:S(2)}) collective-permute-start(f32[16,128,128]{2,1,0:T(8,128)S(1)} %add.101), channel_id=1, source_target_pairs={{0,16},{8,24},{16,0},{24,8},{1,17},{9,25},{17,1},{25,9},{2,18},{10... | collective-permute-start | bytes 3145736 | tf_op jit(solution)/shard_map/ppermute | solution.py:407
  148.5 9.2 %copy-start.8 = (f32[8,128,128]{2,1,0:T(8,128)S(1)}, f32[8,128,128]{2,1,0:T(8,128)}, u32[]{:S(2)}) copy-start(f32[8,128,128]{2,1,0:T(8,128)} %get-tuple-element.50) | copy-start | bytes 1572868
  148.5 22.8 %collective-permute-start.16 = (f32[16,128,128]{2,1,0:T(8,128)}, f32[16,128,128]{2,1,0:T(8,128)S(1)}, u32[]{:S(2)}, u32[]{:S(2)}) collective-permute-start(f32[16,128,128]{2,1,0:T(8,128)} %get-tuple-element.49), channel_id=1, source_target_pairs={{0,8},{8,0},{16,24},{24,16},{1,9},{9,1},{17,25},{25,17},{2,10},{10... | collective-permute-start | bytes 3145736 | tf_op jit(solution)/shard_map/ppermute | solution.py:320
  155.7 14.7 %collective-permute-start.18 = (f32[8,128,128]{2,1,0:T(8,128)}, f32[8,128,128]{2,1,0:T(8,128)S(1)}, u32[]{:S(2)}, u32[]{:S(2)}) collective-permute-start(f32[8,128,128]{2,1,0:T(8,128)} %get-tuple-element.53), channel_id=1, source_target_pairs={{0,1},{1,0},{2,3},{3,2},{4,5},{5,4},{6,7},{7,6},{8,9},{9,8},{10,11... | collective-permute-start | bytes 1572872 | tf_op jit(solution)/shard_map/ppermute | solution.py:325
  157.8 12.6 %copy-start.9 = (f32[8,128,128]{2,1,0:T(8,128)S(1)}, f32[8,128,128]{2,1,0:T(8,128)}, u32[]{:S(2)}) copy-start(f32[8,128,128]{2,1,0:T(8,128)} %get-tuple-element.52) | copy-start | bytes 1572868
  169.6 1.7 copy-start.5
  (4 other events, 3.5 us)
Sparse Core Ops, SparseCore 0:
  65.0 58.1 all-gather.2
where the time goes:
time: 180 us; the launch traced here: 179 us
  waiting for transfers between devices  76.5 us (42%)
  Pallas kernels  45.3 us (25%)
  starting transfers between devices  26.3 us (15%)
  between operations  14.4 us (8%)
  other arithmetic  8.89 us (5%)
  local copies, waits for them, and re-layouts  7.89 us (4%)
    ppermute x6, waiting for transfers between devices, line_step(): return [lax.ppermute(below, 'filt', up), lax.ppermute(above, 'filt', down)]  44.1 us
    pallas_call x2, Pallas kernels, forward_partial(): pl.pallas_call(functools.partial(forward_kernel, depth, chans, which), ou...  15 us
    ppermute x6, waiting for transfers between devices, pair_swap(): return lax.ppermute(value, 'filt', pairs)  14.3 us
    pallas_call x2, Pallas kernels, input_partial(): pl.pallas_call(functools.partial(input_kernel, chans, index), out_shape=(...  14.1 us
    ppermute x2, waiting for transfers between devices, fars_gather(): lax.ppermute(value, 'chan', [(c, (c + 2 * step) % chans) for c in range(c...  13.7 us
    pallas_call x1, Pallas kernels, weight_gradient(): pl.pallas_call(functools.partial(weight_kernel, depth, scale), out_shape=...  11.8 us
    ppermute x6, starting transfers between devices, line_step(): return [lax.ppermute(below, 'filt', up), lax.ppermute(above, 'filt', down)]  10.6 us
    ppermute x6, starting transfers between devices, pair_swap(): return lax.ppermute(value, 'filt', pairs)  6.59 us
  transfers between devices with their start and end apart: 21, of which 12 were waited for; matrix products, arithmetic and copies ran while one was open for 5% of the time, Pallas kernels for 21%

commit v1 on v0

--- a/solution.py
+++ b/solution.py
@@ -37,15 +37,16 @@
 
 
 def arrivals(depth, line):
-    steps = [way for step in range(1, depth) for way in (-step, step)]
-    return [way for way in steps if 0 <= line + way < depth]
+    ways = sorted((way for way in range(-line, depth - line) if way), key=abs)
+    if abs(ways[-1]) == depth - 1:
+        ways.insert(1, ways.pop())
+    return ways
 
 
 def arrival(along, depth, line, place):
     picked = None
     for z in range(depth):
-        way = arrivals(depth, z)[place]
-        value = along[2 * abs(way) - (way < 0)]
+        value = along[arrivals(depth, z)[place]]
         picked = value if picked is None or value is picked else jnp.where(line == z, value, picked)
     return picked
 
@@ -207,7 +208,7 @@
     )(same, cross)
 
 
-def input_kernel(chans, index, at, cot, kernels, keep, send, source, taps, stacked, sems):
+def input_kernel(chans, at, cot, kernels, keep, send, source, taps, stacked, sems):
     side, far, core = at[1], at[2], at[3]
     depth, rows, width, filters = source.shape
     rows = rows - 2
@@ -216,9 +217,7 @@
     for n in range(depth):
         copies.append(
             (
-                pltpu.make_async_copy(
-                    kernels.at[n, :, :, pl.ds(index * chans_in, chans_in)], taps.at[n], sems.at[n, 0]
-                ),
+                pltpu.make_async_copy(kernels.at[n], taps.at[n], sems.at[n, 0]),
                 pltpu.make_async_copy(cot.at[n], source.at[n], sems.at[n, 1]),
             )
         )
@@ -269,19 +268,19 @@
                 out[step * chunk + row] = here[1] + before_it + behind_it
 
 
-def input_partial(chans, at, cot, kernels, index, halves):
+def input_partial(chans, at, cot, kernels):
     depth, rows, width, filters = cot.shape
     rows = rows - 2
-    chans_in = kernels.shape[3] // halves
+    chans_in = kernels.shape[3]
     half = jax.ShapeDtypeStruct((rows // PAIR, width, chans_in), F32)
     return pl.pallas_call(
-        functools.partial(input_kernel, chans, index),
+        functools.partial(input_kernel, chans),
         out_shape=(half, half),
         in_specs=[SMEM, HBM, HBM],
         out_specs=(VMEM, VMEM),
         scratch_shapes=[
             pltpu.VMEM(cot.shape, BF16),
-            pltpu.VMEM(kernels.shape[:3] + (chans_in,), BF16),
+            pltpu.VMEM(kernels.shape, BF16),
             pltpu.VMEM((depth * 3 * filters, 3 * chans_in), BF16),
             pltpu.SemaphoreType.DMA((depth, 2)),
         ],
@@ -304,16 +303,17 @@
     return [[z * PAIR + y for z in range(depth)] for y in range(PAIR)]
 
 
-def line_steps(step, depth):
+def line_step(along, step, depth):
     up = [(z * PAIR + y, (z + 1) * PAIR + y) for z in range(step - 1, depth - 1) for y in range(PAIR)]
     down = [(z * PAIR + y, (z - 1) * PAIR + y) for z in range(1, depth - step + 1) for y in range(PAIR)]
-    return up, down
-
-
-def line_step(along, step, depth):
-    up, down = line_steps(step, depth)
-    below, above = along[0 if step == 1 else -2], along[0 if step == 1 else -1]
-    return [lax.ppermute(below, "filt", up), lax.ppermute(above, "filt", down)]
+    along = dict(along)
+    along[-step] = lax.ppermute(along[1 - step], "filt", up)
+    along[step] = lax.ppermute(along[step - 1], "filt", down)
+    if step == 1 and depth > 2:
+        ends = (0, depth - 1)
+        across = [(z * PAIR + y, (depth - 1 - z) * PAIR + y) for z in ends for y in range(PAIR)]
+        along[depth - 1] = along[1 - depth] = lax.ppermute(along[0], "filt", across)
+    return along
 
 
 def core_swap(value, chans):
@@ -357,62 +357,63 @@
     def exchange(pieces):
         return lax.all_to_all(pieces, "filt", 0, 0, axis_index_groups=lines(depth), tiled=True)
 
-    along, mine, theirs = [inputs[0]], [inputs[0]], [pair_swap(inputs[0], depth)]
-    same, gate = fars_gather(cotangent[0], chans), []
-    padded = pieces = None
-    kernels = weights
-    for step in range(1, depth + 1):
-        along = list(lax.optimization_barrier(tuple(along + gate)))[: len(along)]
-        if step < depth:
-            along += line_step(along, step, depth)
-        if step == 1:
-            gate = along[1:] + theirs + [same]
-            continue
-        mine.append(arrival(along, depth, line, step - 2))
-        theirs.append(pair_swap(mine[-1], depth))
-        before, gate = gate, along[-2:] + theirs[-1:]
-        if step == 2:
-            padded = all_rows(after(same, *before))
-            pieces = exchange(line_pieces(padded))
-            gate.append(pieces)
-        elif step == 3:
-            kernels = after(weights, *before)
-            same = fars_gather(after(pieces, *before), chans)
-            gate.append(same)
-    kernels = lax.all_gather(kernels, "filt", axis=0, axis_index_groups=lines(depth))
-    kernels = kernels.reshape((depth, 9) + weights.shape[2:])
-    if depth < 3:
-        same = fars_gather(pieces, chans)
+    halves = PAIR if chans_in % (PAIR * 128) == 0 else 1
+    kernels = []
+    for half in jnp.split(weights, halves, axis=3):
+        half = half.reshape((9,) + half.shape[2:])
+        kernels.append(lax.all_gather(half, "filt", axis=0, axis_index_groups=lines(depth)))
+
+    mine, theirs = [inputs[0]], [pair_swap(inputs[0], depth)]
+    same = fars_gather(cotangent[0], chans)
+    along = line_step({0: inputs[0]}, 1, depth)
+    fresh = theirs + [same]
+    stages = max(2, depth - 1)
+    for stage in range(2, stages + 1):
+        ways = list(along)
+        ready = lax.optimization_barrier([along[way] for way in ways] + fresh)
+        along = dict(zip(ways, ready))
+        if stage == 2:
+            padded = all_rows(ready[-1])
+            pieces = line_pieces(padded)
+        elif stage == 3:
+            pieces = exchange(ready[-1])
+        fresh = []
+        if stage < stages:
+            along = line_step(along, stage, depth)
+        while len(theirs) < min(depth, stage + 1):
+            mine.append(arrival(along, depth, line, len(theirs) - 1))
+            theirs.append(pair_swap(mine[-1], depth))
+            fresh.append(theirs[-1])
+        fresh.append(pieces)
+    if stages < 3:
+        pieces = exchange(pieces)
+    same = fars_gather(pieces, chans)
     sources = turned(same, core_swap(same, chans))
 
     if part % 16:
         order = [(far - c // 2 + chans // 2) % (chans // 2) * 2 + (core + c) % 2 for c in range(chans)]
-        split = kernels.reshape((depth, 9, chans, part, chans_in))
-        kernels = jnp.take(split, jnp.stack(order), axis=2).reshape(kernels.shape)
-
-    halves = PAIR if chans_in % (PAIR * 128) == 0 else 1
-    fars = chans // 2
-    at_next = after(at, sources, kernels)
-    outputs, input_grad = None, []
-    for n, which in enumerate([*range(1, fars), 0]):
+        split = [half.reshape((depth, 9, chans, part, -1)) for half in kernels]
+        kernels = [jnp.take(half, jnp.stack(order), axis=2).reshape(kernels[0].shape) for half in split]
+
+    outputs, came, at_next = None, [], after(at, kernels[0], pieces)
+    for which in [*range(1, chans // 2), 0]:
         keep, send = forward_partial(depth, chans, which, at_next, weights, mine, theirs)
         at_next = after(at, send)
         moving = keep + core_swap(send, chans)
         if which:
-            if not input_grad:
-                kept, sent = input_partial(chans, at_next, sources, kernels, 0, halves)
-                at_next = after(at, sent)
-                input_grad.append((kept + pair_swap(sent, depth)).astype(BF16))
             at_next = after(at_next, moving)
             moving = lax.ppermute(moving, "chan", [(c, (c + 2 * which) % chans) for c in range(chans)])
+            came.append(moving)
         outputs = moving if outputs is None else outputs + moving
     outputs = outputs.astype(BF16)[None]
-    for index in range(len(input_grad), halves):
-        kept, sent = input_partial(chans, at_next, sources, kernels, index, halves)
-        at_next = after(at, sent)
+
+    input_grad = []
+    for half in kernels:
+        kept, sent = input_partial(chans, at_next, sources, half)
+        at_next = after(at_next, sent, *came)
         input_grad.append((kept + pair_swap(sent, depth)).astype(BF16))
+    at_next = after(at_next, *input_grad[:-1])
     input_grad = jnp.concatenate(input_grad, axis=2)[None]
-
     weight_grad = weight_gradient(depth, at_next, scale, padded, mine, theirs)
     weight_grad = weight_grad.reshape((3, 3, filters, chans_in))
     return (outputs, input_grad, weight_grad)

time: 180 us -> 173 us (0.961)
  waiting for transfers between devices: 76.5 us -> 64.9 us
  starting transfers between devices: 26.3 us -> 30.5 us
    ppermute x6, waiting for transfers between devices: 14.3 us -> 0.03 us  [pair_swap(): return lax.ppermute(value, 'filt', pairs)]
    all_to_all x1, waiting for transfers between devices: 0.01 us -> 11 us  [exchange(): lax.all_to_all(pieces, 'filt', 0, 0, axis_index_groups=lines(depth), tile...]
    ppermute x2, waiting for transfers between devices: 13.7 us -> 6.66 us  [fars_gather(): lax.ppermute(value, 'chan', [(c, (c + 2 * step) % chans) for c in range(c...]
    ppermute x6 -> x5, starting transfers between devices: 10.6 us -> 14.9 us  [the longest x1 6.58 us: line_step(): along[depth - 1] = along[1 - depth] = lax.ppermute(along[0], 'filt', across)]
    ppermute x1, waiting for transfers between devices: 0.01 us -> 3.48 us  [body(): lax.ppermute(moving, 'chan', [(c, (c + 2 * which) % chans) for c in range...]
    ppermute x4, waiting for transfers between devices: 2.19 us -> 0.01 us  [core_swap(): return lax.ppermute(value, 'chan', [(c, c ^ 1) for c in range(chans)])]
    all_gather x1 -> x2, waiting for transfers between devices: 2.17 us -> 0.01 us  [body(): lax.all_gather(half, 'filt', axis=0, axis_index_groups=lines(depth))]
    ppermute x6, starting transfers between devices: 6.59 us -> 8.41 us  [pair_swap(): return lax.ppermute(value, 'filt', pairs)]
  transfers between devices with their start and end apart: 21 -> 21, of which waited for: 12 -> 7; matrix products, arithmetic and copies ran while one was open for 5% -> 8% of each run, Pallas kernels for 21% -> 26%
where the time goes in v1:
time: 173 us; the launch traced here: 172 us
  waiting for transfers between devices  64.9 us (38%)
  Pallas kernels  45.1 us (26%)
  starting transfers between devices  30.5 us (18%)
  between operations  14.4 us (8%)
  other arithmetic  9.94 us (6%)
  local copies, waits for them, and re-layouts  7.27 us (4%)
    ppermute x2, waiting for transfers between devices, line_step(): along[step] = lax.ppermute(along[step - 1], 'filt', down)  30.6 us
    pallas_call x2, Pallas kernels, forward_partial(): pl.pallas_call(functools.partial(forward_kernel, depth, chans, which), ou...  15.1 us
    pallas_call x2, Pallas kernels, input_partial(): pl.pallas_call(functools.partial(input_kernel, chans), out_shape=(half, h...  13.8 us
    ppermute x1, waiting for transfers between devices, line_step(): along[depth - 1] = along[1 - depth] = lax.ppermute(along[0], 'filt', across)  11.8 us
    pallas_call x1, Pallas kernels, weight_gradient(): pl.pallas_call(functools.partial(weight_kernel, depth, scale), out_shape=...  11.8 us
    all_to_all x1, waiting for transfers between devices, exchange(): lax.all_to_all(pieces, 'filt', 0, 0, axis_index_groups=lines(depth), tile...  11 us
    ppermute x6, starting transfers between devices, pair_swap(): return lax.ppermute(value, 'filt', pairs)  8.41 us
    ppermute x2, waiting for transfers between devices, fars_gather(): lax.ppermute(value, 'chan', [(c, (c + 2 * step) % chans) for c in range(c...  6.66 us
  transfers between devices with their start and end apart: 21, of which 7 were waited for; matrix products, arithmetic and copies ran while one was open for 8% of the time, Pallas kernels for 26%

profile of v1, /device:TPU:0, one launch (start us, length us, event | category | flops | bytes accessed | tf_op | source)
XLA Modules:
  0.0 172.1 jit_solution(1489467911463768467)
XLA Ops:
  7.2 3.0 %collective-permute-start.4 = (bf16[16,128,128]{2,1,0:T(8,128)(2,1)}, bf16[16,128,128]{2,1,0:T(8,128)(2,1)S(1)}, u32[]{:S(2)}, u32[]{:S(2)}) collective-permute-start(bf16[16,128,128]{2,1,0:T(8,128)(2,1)} %bitcast.42), channel_id=1, source_target_pairs={{0,16},{8,24},{16,0},{24,8},{1,17},{9,25},{17,1},{25,9},{2,18},{10... | collective-permute-start | bytes 1572872 | tf_op jit(solution)/shard_map/ppermute | solution.py:298
  10.2 4.3 %collective-permute-start = (bf16[8,128,256]{2,1,0:T(8,128)(2,1)}, bf16[8,128,256]{2,1,0:T(8,128)(2,1)}, u32[]{:S(2)}, u32[]{:S(2)}) collective-permute-start(bf16[8,128,256]{2,1,0:T(8,128)(2,1)} %bitcast.44), channel_id=1, source_target_pairs={{0,2},{1,3},{2,4},{3,5},{4,6},{5,7},{8,10},{9,11},{10,12},{11,13},... | collective-permute-start | bytes 1572872 | tf_op jit(solution)/shard_map/ppermute | solution.py:310
  14.5 1.3 collective-permute-start.1
  15.8 6.6 %collective-permute-start.2 = (bf16[8,128,256]{2,1,0:T(8,128)(2,1)}, bf16[8,128,256]{2,1,0:T(8,128)(2,1)S(1)}, u32[]{:S(2)}, u32[]{:S(2)}) collective-permute-start(bf16[8,128,256]{2,1,0:T(8,128)(2,1)} %bitcast.46), channel_id=1, source_target_pairs={{0,6},{1,7},{6,0},{7,1},{8,14},{9,15},{14,8},{15,9},{16,22},{17,23... | collective-permute-start | bytes 1572872 | tf_op jit(solution)/shard_map/ppermute | solution.py:315
  22.4 1.6 collective-permute-start.3
  24.0 1.1 pad_maximum_fusion.1
  25.1 1.2 collective-permute-done
  26.4 4.0 %collective-permute-done.1 = bf16[8,128,256]{2,1,0:T(8,128)(2,1)} collective-permute-done((bf16[8,128,256]{2,1,0:T(8,128)(2,1)}, bf16[8,128,256]{2,1,0:T(8,128)(2,1)}, u32[]{:S(2)}, u32[]{:S(2)}) %collective-permute-start.1) | collective-permute-done | bytes 524320 | tf_op jit(solution)/shard_map/ppermute | solution.py:311
  30.3 11.8 %collective-permute-done.2 = bf16[8,128,256]{2,1,0:T(8,128)(2,1)S(1)} collective-permute-done((bf16[8,128,256]{2,1,0:T(8,128)(2,1)}, bf16[8,128,256]{2,1,0:T(8,128)(2,1)S(1)}, u32[]{:S(2)}, u32[]{:S(2)}) %collective-permute-start.2) | collective-permute-done | bytes 524320 | tf_op jit(solution)/shard_map/ppermute | solution.py:315
  43.3 1.5 collective-permute-start.5
  44.8 1.3 collective-permute-start.6
  46.1 1.3 fusion
  47.5 1.6 collective-permute-start.7
  50.2 1.1 fusion.3
  51.4 1.1 fusion.2.cot
  53.6 26.6 %collective-permute-done.6 = bf16[8,128,256]{2,1,0:T(8,128)(2,1)} collective-permute-done((bf16[8,128,256]{2,1,0:T(8,128)(2,1)}, bf16[8,128,256]{2,1,0:T(8,128)(2,1)}, u32[]{:S(2)}, u32[]{:S(2)}) %collective-permute-start.6) | collective-permute-done | bytes 524320 | tf_op jit(solution)/shard_map/ppermute | solution.py:311
  81.1 3.5 %all-to-all-start = ((bf16[4,18,32,128]{3,2,1,0:T(8,128)(2,1)}), bf16[4,18,32,128]{3,2,1,0:T(8,128)(2,1)S(1)}, u32[]{:S(2)}, u32[]{:S(2)}) async-start(bf16[4,18,32,128]{3,2,1,0:T(8,128)(2,1)} %pad_maximum_fusion.2), calls=%async_computation | async-start | bytes 1179648 | tf_op jit(solution)/shard_map/all_to_all | solution.py:358
  84.6 2.0 %select_select_fusion.refs_3_ = bf16[8,128,256]{2,1,0:T(8,128)(2,1)} fusion(bf16[8,128,256]{2,1,0:T(8,128)(2,1)} %collective-permute-done.5, bf16[8,128,256]{2,1,0:T(8,128)(2,1)} %collective-permute-done.6, pred[]{:T(512)S(6)} %eq.18, pred[]{:T(512)S(6)} %eq.9), kind=kLoop, calls=%fused_computation.3 | loop fusion | flops 524288 | bytes 1572866 | tf_op jit(solution)/shard_map/jit(_where)/select_n | solution.py:50
  86.7 1.5 collective-permute-start.10
  89.5 11.0 %all-to-all-done = bf16[4,18,32,128]{3,2,1,0:T(8,128)(2,1)S(1)} async-done(((bf16[4,18,32,128]{3,2,1,0:T(8,128)(2,1)}), bf16[4,18,32,128]{3,2,1,0:T(8,128)(2,1)S(1)}, u32[]{:S(2)}, u32[]{:S(2)}) %all-to-all-start) | async-done | bytes 589856 | tf_op jit(solution)/shard_map/all_to_all | solution.py:358
  100.5 7.5 %forward.2 = (f32[16,128,128]{2,1,0:T(8,128)}, f32[16,128,128]{2,1,0:T(8,128)}) custom-call(s32[8]{0:T(128)} %concatenate.6.at, bf16[3,3,128,256]{3,2,1,0:T(8,128)(2,1)} %weights.3, bf16[8,128,256]{2,1,0:T(8,128)(2,1)} %bitcast.48, bf16[8,128,256]{2,1,0:T(8,128)(2,1)} %copy-done.9, bf16[8,128,256]{2,1,0:T(8,128)(2,1)} %copy-done.8, ...), custom_call_target="tpu_custom_call" | custom-call | flops 2415919104 | bytes 6291456 | tf_op jit(solution)/shard_map/forward/pallas_call | solution.py:117
  108.2 6.7 %collective-permute-done.14 = bf16[4,18,32,128]{3,2,1,0:T(8,128)(2,1)S(1)} collective-permute-done((bf16[4,18,32,128]{3,2,1,0:T(8,128)(2,1)S(1)}, bf16[4,18,32,128]{3,2,1,0:T(8,128)(2,1)S(1)}, u32[]{:S(2)}, u32[]{:S(2)}) %collective-permute-start.14) | collective-permute-done | bytes 589856 | tf_op jit(solution)/shard_map/ppermute | solution.py:298
  115.0 1.3 add.101
  116.6 7.6 %forward.3 = (f32[16,128,128]{2,1,0:T(8,128)}, f32[16,128,128]{2,1,0:T(8,128)}) custom-call(s32[8]{0:T(128)} %concatenate.6.at, bf16[3,3,128,256]{3,2,1,0:T(8,128)(2,1)} %weights.3, bf16[8,128,256]{2,1,0:T(8,128)(2,1)} %bitcast.49, bf16[8,128,256]{2,1,0:T(8,128)(2,1)} %copy-done.9, bf16[8,128,256]{2,1,0:T(8,128)(2,1)} %copy-done.8, ...), custom_call_target="tpu_custom_call" | custom-call | flops 2415919104 | bytes 6291456 | tf_op jit(solution)/shard_map/forward/pallas_call | solution.py:117
  125.4 4.4 %turned.1.cot = bf16[4,18,128,128]{3,2,1,0:T(8,128)(2,1)} custom-call(bf16[2,4,18,32,128]{4,3,2,1,0:T(8,128)(2,1)} %copy-done, bf16[2,4,18,32,128]{4,3,2,1,0:T(8,128)(2,1)} %copy-done.2), custom_call_target="tpu_custom_call" | custom-call | bytes 4718592 | tf_op jit(solution)/shard_map/turned/pallas_call | solution.py:199
  129.9 6.9 %input_gradient.2 = (f32[8,128,128]{2,1,0:T(8,128)}, f32[8,128,128]{2,1,0:T(8,128)}) custom-call(s32[8]{0:T(128)} %concatenate.6.at, bf16[4,18,128,128]{3,2,1,0:T(8,128)(2,1)} %turned.1.cot, bf16[4,9,128,128]{3,2,1,0:T(8,128)(2,1)} %all-gather.3.cloned.1.call-done.kernels), custom_call_target="tpu_custom_call" | custom-call | flops 2415919104 | bytes 3538944 | tf_op jit(solution)/shard_map/input_gradient/pallas_call | solution.py:276
  136.8 1.6 collective-permute-start.16
  138.4 3.5 %collective-permute-done.12 = f32[16,128,128]{2,1,0:T(8,128)S(1)} collective-permute-done((f32[16,128,128]{2,1,0:T(8,128)}, f32[16,128,128]{2,1,0:T(8,128)S(1)}, u32[]{:S(2)}, u32[]{:S(2)}) %collective-permute-start.12) | collective-permute-done | bytes 1048608 | tf_op jit(solution)/shard_map/ppermute | solution.py:405
  141.9 6.9 %input_gradient.3 = (f32[8,128,128]{2,1,0:T(8,128)}, f32[8,128,128]{2,1,0:T(8,128)}) custom-call(s32[8]{0:T(128)} %concatenate.6.at, bf16[4,18,128,128]{3,2,1,0:T(8,128)(2,1)} %turned.1.cot, bf16[4,9,128,128]{3,2,1,0:T(8,128)(2,1)} %all-gather.5.cloned.1.call-done.kernels), custom_call_target="tpu_custom_call" | custom-call | flops 2415919104 | bytes 3538944 | tf_op jit(solution)/shard_map/input_gradient/pallas_call | solution.py:276
  148.8 1.6 collective-permute-start.17
  151.4 1.1 add_convert_fusion.2
  152.6 11.8 %weight_gradient.1 = f32[3,384,256]{2,1,0:T(8,128)} custom-call(s32[8]{0:T(128)} %concatenate.6.at, bf16[66,128,128]{2,1,0:T(8,128)(2,1)} %copy-done.1, bf16[8,128,256]{2,1,0:T(8,128)(2,1)} %bitcast.50, bf16[8,128,256]{2,1,0:T(8,128)(2,1)} %copy-done.9, bf16[8,128,256]{2,1,0:T(8,128)(2,1)} %copy-done.8, bf16[8,128,256]{2,1,0:T(8,128)(2,1)} %select_select_fusion.refs_3_, ...), custom_call_target="tpu_custom_call" | custom-call | flops 4831838208 | bytes 6291456 | tf_op jit(solution)/shard_map/weight_gradient/pallas_call | solution.py:168
  (61 shorter events, 9.3 us)
Async XLA Ops:
  7.2 35.0 %copy-start.5 = (bf16[3,3,128,256]{3,2,1,0:T(8,128)(2,1)S(1)}, bf16[3,3,128,256]{3,2,1,0:T(8,128)(2,1)}, u32[]{:S(2)}) copy-start(bf16[3,3,128,256]{3,2,1,0:T(8,128)(2,1)} %weights.3) | copy-start | bytes 1769476
  7.2 82.3 %all-gather.3.cloned.1.call-start = ((), (), s32[]{:S(2)}) async-start(), calls=%async_computation.1 | async-start | bytes 1474560 | tf_op jit(solution)/shard_map/all_gather | solution.py:364
  7.2 16.8 %collective-permute-start.4 = (bf16[16,128,128]{2,1,0:T(8,128)(2,1)}, bf16[16,128,128]{2,1,0:T(8,128)(2,1)S(1)}, u32[]{:S(2)}, u32[]{:S(2)}) collective-permute-start(bf16[16,128,128]{2,1,0:T(8,128)(2,1)} %bitcast.42), channel_id=1, source_target_pairs={{0,16},{8,24},{16,0},{24,8},{1,17},{9,25},{17,1},{25,9},{2,18},{10... | collective-permute-start | bytes 1572872 | tf_op jit(solution)/shard_map/ppermute | solution.py:298
  10.2 16.1 %collective-permute-start = (bf16[8,128,256]{2,1,0:T(8,128)(2,1)}, bf16[8,128,256]{2,1,0:T(8,128)(2,1)}, u32[]{:S(2)}, u32[]{:S(2)}) collective-permute-start(bf16[8,128,256]{2,1,0:T(8,128)(2,1)} %bitcast.44), channel_id=1, source_target_pairs={{0,2},{1,3},{2,4},{3,5},{4,6},{5,7},{8,10},{9,11},{10,12},{11,13},... | collective-permute-start | bytes 1572872 | tf_op jit(solution)/shard_map/ppermute | solution.py:310
  14.5 15.8 %collective-permute-start.1 = (bf16[8,128,256]{2,1,0:T(8,128)(2,1)}, bf16[8,128,256]{2,1,0:T(8,128)(2,1)}, u32[]{:S(2)}, u32[]{:S(2)}) collective-permute-start(bf16[8,128,256]{2,1,0:T(8,128)(2,1)} %bitcast.45), channel_id=1, source_target_pairs={{2,0},{3,1},{4,2},{5,3},{6,4},{7,5},{10,8},{11,9},{12,10},{13,11},... | collective-permute-start | bytes 1572872 | tf_op jit(solution)/shard_map/ppermute | solution.py:311
  15.8 26.4 %collective-permute-start.2 = (bf16[8,128,256]{2,1,0:T(8,128)(2,1)}, bf16[8,128,256]{2,1,0:T(8,128)(2,1)S(1)}, u32[]{:S(2)}, u32[]{:S(2)}) collective-permute-start(bf16[8,128,256]{2,1,0:T(8,128)(2,1)} %bitcast.46), channel_id=1, source_target_pairs={{0,6},{1,7},{6,0},{7,1},{8,14},{9,15},{14,8},{15,9},{16,22},{17,23... | collective-permute-start | bytes 1572872 | tf_op jit(solution)/shard_map/ppermute | solution.py:315
  22.4 19.8 %collective-permute-start.3 = (bf16[8,128,256]{2,1,0:T(8,128)(2,1)}, bf16[8,128,256]{2,1,0:T(8,128)(2,1)S(1)}, u32[]{:S(2)}, u32[]{:S(2)}) collective-permute-start(bf16[8,128,256]{2,1,0:T(8,128)(2,1)} %bitcast.47), channel_id=1, source_target_pairs={{0,1},{1,0},{2,3},{3,2},{4,5},{5,4},{6,7},{7,6},{8,9},{9,8},{10,11... | collective-permute-start | bytes 1572872 | tf_op jit(solution)/shard_map/ppermute | solution.py:325
  42.2 1.0 copy-start.10
  42.2 8.0 %collective-permute-start.9 = (bf16[2,16,128,128]{3,2,1,0:T(8,128)(2,1)S(1)}, bf16[2,16,128,128]{3,2,1,0:T(8,128)(2,1)}, u32[]{:S(2)}, u32[]{:S(2)}) collective-permute-start(bf16[2,16,128,128]{3,2,1,0:T(8,128)(2,1)S(1)} %pad_maximum_fusion.1), channel_id=1, source_target_pairs={{0,8},{8,0},{16,24},{24,16},{1,9},{9,1},{17,25},{25,17},{2,10},{10... | collective-permute-start | bytes 3145736 | tf_op jit(solution)/shard_map/ppermute | solution.py:320
  43.3 10.3 %collective-permute-start.5 = (bf16[8,128,256]{2,1,0:T(8,128)(2,1)}, bf16[8,128,256]{2,1,0:T(8,128)(2,1)}, u32[]{:S(2)}, u32[]{:S(2)}) collective-permute-start(bf16[8,128,256]{2,1,0:T(8,128)(2,1)} %collective-permute-done), channel_id=1, source_target_pairs={{2,4},{3,5},{4,6},{5,7},{10,12},{11,13},{12,14},{13,15},{18,20},{1... | collective-permute-start | bytes 1572872 | tf_op jit(solution)/shard_map/ppermute | solution.py:310
  44.8 35.5 %collective-permute-start.6 = (bf16[8,128,256]{2,1,0:T(8,128)(2,1)}, bf16[8,128,256]{2,1,0:T(8,128)(2,1)}, u32[]{:S(2)}, u32[]{:S(2)}) collective-permute-start(bf16[8,128,256]{2,1,0:T(8,128)(2,1)} %collective-permute-done.1), channel_id=1, source_target_pairs={{2,0},{3,1},{4,2},{5,3},{10,8},{11,9},{12,10},{13,11},{18,16},{19,... | collective-permute-start | bytes 1572872 | tf_op jit(solution)/shard_map/ppermute | solution.py:311
  47.4 3.9 %copy-start.8 = (bf16[8,128,256]{2,1,0:T(8,128)(2,1)}, bf16[8,128,256]{2,1,0:T(8,128)(2,1)S(1)}, u32[]{:S(2)}) copy-start(bf16[8,128,256]{2,1,0:T(8,128)(2,1)S(1)} %get-tuple-element.55.refs_2_) | copy-start | bytes 1572868
  47.4 3.9 %copy-start.9 = (bf16[8,128,256]{2,1,0:T(8,128)(2,1)}, bf16[8,128,256]{2,1,0:T(8,128)(2,1)S(1)}, u32[]{:S(2)}) copy-start(bf16[8,128,256]{2,1,0:T(8,128)(2,1)S(1)} %get-tuple-element.56.refs_1_) | copy-start | bytes 1572868
  47.5 32.8 %collective-permute-start.7 = (bf16[8,128,256]{2,1,0:T(8,128)(2,1)S(1)}, bf16[8,128,256]{2,1,0:T(8,128)(2,1)S(1)}, u32[]{:S(2)}, u32[]{:S(2)}) collective-permute-start(bf16[8,128,256]{2,1,0:T(8,128)(2,1)S(1)} %get-tuple-element.56.refs_1_), channel_id=1, source_target_pairs={{0,1},{1,0},{2,3},{3,2},{4,5},{5,4},{6,7},{7,6},{8,9},{9,8},{10,11... | collective-permute-start | bytes 1572872 | tf_op jit(solution)/shard_map/ppermute | solution.py:325
  49.0 32.1 %collective-permute-start.8 = (bf16[8,128,256]{2,1,0:T(8,128)(2,1)S(1)}, bf16[8,128,256]{2,1,0:T(8,128)(2,1)}, u32[]{:S(2)}, u32[]{:S(2)}) collective-permute-start(bf16[8,128,256]{2,1,0:T(8,128)(2,1)S(1)} %get-tuple-element.55.refs_2_), channel_id=1, source_target_pairs={{0,1},{1,0},{2,3},{3,2},{4,5},{5,4},{6,7},{7,6},{8,9},{9,8},{10,11... | collective-permute-start | bytes 1572872 | tf_op jit(solution)/shard_map/ppermute | solution.py:325
  52.5 34.1 %copy-start.1 = (bf16[66,128,128]{2,1,0:T(8,128)(2,1)}, bf16[66,128,128]{2,1,0:T(8,128)(2,1)S(1)}, u32[]{:S(2)}) copy-start(bf16[66,128,128]{2,1,0:T(8,128)(2,1)S(1)} %fusion.2.cot) | copy-start | bytes 6488068
  81.1 19.4 %all-to-all-start = ((bf16[4,18,32,128]{3,2,1,0:T(8,128)(2,1)}), bf16[4,18,32,128]{3,2,1,0:T(8,128)(2,1)S(1)}, u32[]{:S(2)}, u32[]{:S(2)}) async-start(bf16[4,18,32,128]{3,2,1,0:T(8,128)(2,1)} %pad_maximum_fusion.2), calls=%async_computation | async-start | bytes 1179648 | tf_op jit(solution)/shard_map/all_to_all | solution.py:358
  84.6 57.3 %all-gather.5.cloned.1.call-start = ((), (), s32[]{:S(2)}) async-start(), calls=%async_computation.2 | async-start | bytes 1474560 | tf_op jit(solution)/shard_map/all_gather | solution.py:364
  86.7 13.9 %collective-permute-start.10 = (bf16[8,128,256]{2,1,0:T(8,128)(2,1)}, bf16[8,128,256]{2,1,0:T(8,128)(2,1)}, u32[]{:S(2)}, u32[]{:S(2)}) collective-permute-start(bf16[8,128,256]{2,1,0:T(8,128)(2,1)} %select_select_fusion.refs_3_), channel_id=1, source_target_pairs={{0,1},{1,0},{2,3},{3,2},{4,5},{5,4},{6,7},{7,6},{8,9},{9,8},{10,11... | collective-permute-start | bytes 1572872 | tf_op jit(solution)/shard_map/ppermute | solution.py:325
  100.5 14.3 %collective-permute-start.14 = (bf16[4,18,32,128]{3,2,1,0:T(8,128)(2,1)S(1)}, bf16[4,18,32,128]{3,2,1,0:T(8,128)(2,1)S(1)}, u32[]{:S(2)}, u32[]{:S(2)}) collective-permute-start(bf16[4,18,32,128]{3,2,1,0:T(8,128)(2,1)S(1)} %all-to-all-done), channel_id=1, source_target_pairs={{0,16},{8,24},{16,0},{24,8},{1,17},{9,25},{17,1},{25,9},{2,18},{10... | collective-permute-start | bytes 1769480 | tf_op jit(solution)/shard_map/ppermute | solution.py:298
  108.0 7.0 %copy-start.4 = (f32[16,128,128]{2,1,0:T(8,128)S(1)}, f32[16,128,128]{2,1,0:T(8,128)}, u32[]{:S(2)}) copy-start(f32[16,128,128]{2,1,0:T(8,128)} %get-tuple-element.35) | copy-start | bytes 3145732
  108.1 7.0 %collective-permute-start.11 = (f32[16,128,128]{2,1,0:T(8,128)}, f32[16,128,128]{2,1,0:T(8,128)S(1)}, u32[]{:S(2)}, u32[]{:S(2)}) collective-permute-start(f32[16,128,128]{2,1,0:T(8,128)} %get-tuple-element.36), channel_id=1, source_target_pairs={{0,8},{8,0},{16,24},{24,16},{1,9},{9,1},{17,25},{25,17},{2,10},{10... | collective-permute-start | bytes 3145736 | tf_op jit(solution)/shard_map/ppermute | solution.py:320
  114.9 9.3 %copy-start = (bf16[2,4,18,32,128]{4,3,2,1,0:T(8,128)(2,1)}, bf16[2,4,18,32,128]{4,3,2,1,0:T(8,128)(2,1)S(1)}, u32[]{:S(2)}) copy-start(bf16[2,4,18,32,128]{4,3,2,1,0:T(8,128)(2,1)S(1)} %pad_maximum_fusion.same) | copy-start | bytes 3538948
  114.9 9.4 %collective-permute-start.15 = (bf16[2,4,18,32,128]{4,3,2,1,0:T(8,128)(2,1)S(1)}, bf16[2,4,18,32,128]{4,3,2,1,0:T(8,128)(2,1)S(1)}, u32[]{:S(2)}, u32[]{:S(2)}) collective-permute-start(bf16[2,4,18,32,128]{4,3,2,1,0:T(8,128)(2,1)S(1)} %pad_maximum_fusion.same), channel_id=1, source_target_pairs={{0,8},{8,0},{16,24},{24,16},{1,9},{9,1},{17,25},{25,17},{2,10},{10... | collective-permute-start | bytes 3538952 | tf_op jit(solution)/shard_map/ppermute | solution.py:320
  116.3 25.6 %collective-permute-start.12 = (f32[16,128,128]{2,1,0:T(8,128)}, f32[16,128,128]{2,1,0:T(8,128)S(1)}, u32[]{:S(2)}, u32[]{:S(2)}) collective-permute-start(f32[16,128,128]{2,1,0:T(8,128)} %add.101), channel_id=1, source_target_pairs={{0,16},{8,24},{16,0},{24,8},{1,17},{9,25},{17,1},{25,9},{2,18},{10... | collective-permute-start | bytes 3145736 | tf_op jit(solution)/shard_map/ppermute | solution.py:405
  124.2 26.2 %collective-permute-start.13 = (f32[16,128,128]{2,1,0:T(8,128)}, f32[16,128,128]{2,1,0:T(8,128)S(1)}, u32[]{:S(2)}, u32[]{:S(2)}) collective-permute-start(f32[16,128,128]{2,1,0:T(8,128)} %get-tuple-element.40), channel_id=1, source_target_pairs={{0,8},{8,0},{16,24},{24,16},{1,9},{9,1},{17,25},{25,17},{2,10},{10... | collective-permute-start | bytes 3145736 | tf_op jit(solution)/shard_map/ppermute | solution.py:320
  124.3 1.1 copy-start.2
  136.8 13.7 %copy-start.3 = (f32[16,128,128]{2,1,0:T(8,128)S(1)}, f32[16,128,128]{2,1,0:T(8,128)}, u32[]{:S(2)}) copy-start(f32[16,128,128]{2,1,0:T(8,128)} %get-tuple-element.39) | copy-start | bytes 3145732
  136.8 14.6 %collective-permute-start.16 = (f32[8,128,128]{2,1,0:T(8,128)}, f32[8,128,128]{2,1,0:T(8,128)}, u32[]{:S(2)}, u32[]{:S(2)}) collective-permute-start(f32[8,128,128]{2,1,0:T(8,128)} %get-tuple-element.43), channel_id=1, source_target_pairs={{0,1},{1,0},{2,3},{3,2},{4,5},{5,4},{6,7},{7,6},{8,9},{9,8},{10,11... | collective-permute-start | bytes 1572872 | tf_op jit(solution)/shard_map/ppermute | solution.py:325
  148.8 2.6 %copy-start.7 = (f32[8,128,128]{2,1,0:T(8,128)S(1)}, f32[8,128,128]{2,1,0:T(8,128)}, u32[]{:S(2)}) copy-start(f32[8,128,128]{2,1,0:T(8,128)} %get-tuple-element.42) | copy-start | bytes 1572868
  148.8 15.5 %collective-permute-start.17 = (f32[8,128,128]{2,1,0:T(8,128)}, f32[8,128,128]{2,1,0:T(8,128)S(1)}, u32[]{:S(2)}, u32[]{:S(2)}) collective-permute-start(f32[8,128,128]{2,1,0:T(8,128)} %get-tuple-element.46), channel_id=1, source_target_pairs={{0,1},{1,0},{2,3},{3,2},{4,5},{5,4},{6,7},{7,6},{8,9},{9,8},{10,11... | collective-permute-start | bytes 1572872 | tf_op jit(solution)/shard_map/ppermute | solution.py:325
  152.5 11.8 %copy-start.6 = (f32[8,128,128]{2,1,0:T(8,128)S(1)}, f32[8,128,128]{2,1,0:T(8,128)}, u32[]{:S(2)}) copy-start(f32[8,128,128]{2,1,0:T(8,128)} %get-tuple-element.45) | copy-start | bytes 1572868
  (1 other events, 0.8 us)
Sparse Core Ops, SparseCore 0:
  43.3 36.4 all-gather.2
  108.3 30.6 all-gather.4

commit v2 on v1

--- a/solution.py
+++ b/solution.py
@@ -72,9 +72,9 @@
 
 
 def forward_kernel(depth, chans, which, at, weights, *refs):
-    count = (len(refs) - 5) // 2
+    count = (len(refs) - 8) // 2
     parts = (refs[:count], refs[count : 2 * count])
-    keep, send, rows, taps, sems = refs[2 * count :]
+    keep, send, rows, taps, made, sems, tap_sems, out_sems = refs[2 * count :]
     filters, chans_in = weights.shape[2], weights.shape[3]
     width = rows.shape[1]
     block = keep.shape[0]
@@ -83,9 +83,19 @@
     top = lax.rem(far + which, chans // 2) * 2 * block
     first, spots = top // height, max(1, 2 * block // height)
     wait = load_rows(at, parts, rows, sems, first - 1, first + spots)
-    for tap_row in range(3):
-        for tap_col in range(3):
-            taps[pl.ds(tap_col * filters, filters), pl.ds(tap_row * chans_in, chans_in)] = weights[tap_row, tap_col]
+    fetches = [
+        pltpu.make_async_copy(
+            weights.at[tap_row, tap_col],
+            taps.at[pl.ds(tap_col * filters, filters), pl.ds(tap_row * chans_in, chans_in)],
+            tap_sems.at[tap_row, tap_col],
+        )
+        for tap_row in range(3)
+        for tap_col in range(3)
+    ]
+    for fetch in fetches:
+        fetch.start()
+    for fetch in fetches:
+        fetch.wait()
     for spot in range(-1, spots + 1):
 
         @pl.when(jnp.logical_and(first + spot >= 0, first + spot < depth * PAIR))
@@ -94,9 +104,13 @@
 
     group = min(4, block)
 
+    def result(step, place):
+        chosen = pl.ds(step * group, group)
+        return pltpu.make_async_copy(made.at[place, chosen], (send, keep)[place].at[chosen], out_sems.at[place, step])
+
     @pl.loop(0, block // group)
     def _(step):
-        for target, of_core in ((send, 1 - core), (keep, core)):
+        for place, of_core in enumerate((1 - core, core)):
             start = top + of_core * block + step * group
             window = jnp.concatenate(
                 [rows[pl.ds(start + i, group)].reshape(group * width, chans_in) for i in range(3)], axis=1
@@ -106,7 +120,12 @@
                 part = [
                     product[j * filters : (j + 1) * filters, row * width : (row + 1) * width] for j in range(3)
                 ]
-                target[step * group + row] = part[1] + lane_shift(part[0], 1) + lane_shift(part[2], -1)
+                made[place, step * group + row] = part[1] + lane_shift(part[0], 1) + lane_shift(part[2], -1)
+            result(step, place).start()
+
+    for step in range(block // group):
+        for place in range(2):
+            result(step, place).wait()
 
 
 def forward_partial(depth, chans, which, at, weights, own, other):
@@ -117,12 +136,15 @@
     return pl.pallas_call(
         functools.partial(forward_kernel, depth, chans, which),
         out_shape=(half, half),
-        in_specs=[SMEM, VMEM] + [HBM] * (len(own) + len(other)),
-        out_specs=(VMEM, VMEM),
+        in_specs=[SMEM, HBM] + [HBM] * (len(own) + len(other)),
+        out_specs=(HBM, HBM),
         scratch_shapes=[
             pltpu.VMEM((rows + 2, width, chans_in), BF16),
             pltpu.VMEM((3 * filters, 3 * chans_in), BF16),
+            pltpu.VMEM((2, rows // chans, filters, width), F32),
             pltpu.SemaphoreType.DMA((depth * PAIR,)),
+            pltpu.SemaphoreType.DMA((3, 3)),
+            pltpu.SemaphoreType.DMA((2, rows // chans // min(4, rows // chans))),
         ],
         compiler_params=params(58),
         cost_estimate=cost(
@@ -133,23 +155,36 @@
 
 
 def weight_kernel(depth, scale, at, cot, *refs):
-    count = (len(refs) - 4) // 2
+    count = (len(refs) - 7) // 2
     parts = (refs[:count], refs[count : 2 * count])
-    out, rows, moved, sems = refs[2 * count :]
+    out, rows, cots, moved, total, sems, cot_sems = refs[2 * count :]
     wait = load_rows(at, parts, rows, sems, 0, depth * PAIR - 1)
     filters, width = cot.shape[1], cot.shape[2]
-    total = cot.shape[0] - 2
     chans_in = rows.shape[2]
-    chunk = min(8, total)
-    for spot in range(depth * PAIR):
-        wait(spot)
-    out[...] = jnp.zeros(out.shape, F32)
-
-    @pl.loop(0, total // chunk)
+    height = parts[0][0].shape[0]
+    steps, chunk = cots.shape[0], cots.shape[1]
+
+    def fetch(step):
+        return pltpu.make_async_copy(cot.at[pl.ds(1 + step * chunk, chunk)], cots.at[step], cot_sems.at[step])
+
+    for step in range(steps):
+        fetch(step).start()
+    total[...] = jnp.zeros(total.shape, F32)
+    wait(0)
+
+    @pl.loop(0, steps)
     def _(step):
         first = step * chunk
+        fetch(step).wait()
+        for spot in range(max(1, chunk // height)):
+            after_it = first // height + spot + 1
+
+            @pl.when(after_it < depth * PAIR)
+            def _():
+                wait(after_it)
+
         for row in range(chunk):
-            value = cot[1 + first + row]
+            value = cots[step, row]
             wide = value.astype(F32)
             lanes = pl.ds(row * width, width)
             moved[0:filters, lanes] = lane_shift(wide, -1).astype(BF16)
@@ -157,23 +192,35 @@
             moved[2 * filters :, lanes] = lane_shift(wide, 1).astype(BF16)
         for tap_row in range(3):
             window = rows[pl.ds(first + tap_row, chunk)].reshape(chunk * width, chans_in)
-            out[tap_row] += jnp.dot(moved[...], window, preferred_element_type=F32)
-
-    out[...] = out[...] * scale
+            total[tap_row] += jnp.dot(moved[...], window, preferred_element_type=F32)
+
+    stores = []
+    for tap_row in range(3):
+        total[tap_row] = total[tap_row] * scale
+        for tap_col in range(3):
+            chosen = (tap_row, pl.ds(tap_col * filters, filters))
+            stores.append(pltpu.make_async_copy(total.at[chosen], out.at[chosen], cot_sems.at[steps + 3 * tap_row + tap_col]))
+            stores[-1].start()
+    for store in stores:
+        store.wait()
 
 
 def weight_gradient(depth, at, scale, cot, own, other):
-    width, chans_in = own[0].shape[1:]
+    height, width, chans_in = own[0].shape
     rows, filters = cot.shape[0] - 2, cot.shape[1]
+    chunk = max(height, min(8, rows))
     return pl.pallas_call(
         functools.partial(weight_kernel, depth, scale),
         out_shape=jax.ShapeDtypeStruct((3, 3 * filters, chans_in), F32),
-        in_specs=[SMEM, VMEM] + [HBM] * (len(own) + len(other)),
-        out_specs=VMEM,
+        in_specs=[SMEM, HBM] + [HBM] * (len(own) + len(other)),
+        out_specs=HBM,
         scratch_shapes=[
             pltpu.VMEM((rows + 2, width, chans_in), BF16),
-            pltpu.VMEM((3 * filters, min(8, rows) * width), BF16),
+            pltpu.VMEM((rows // chunk, chunk, filters, width), BF16),
+            pltpu.VMEM((3 * filters, chunk * width), BF16),
+            pltpu.VMEM((3, 3 * filters, chans_in), F32),
             pltpu.SemaphoreType.DMA((depth * PAIR,)),
+            pltpu.SemaphoreType.DMA((rows // chunk + 9,)),
         ],
         compiler_params=params(58),
         cost_estimate=cost(18 * rows * width * chans_in * filters, 2 * rows * width * (filters + chans_in)),
@@ -208,7 +255,7 @@
     )(same, cross)
 
 
-def input_kernel(chans, at, cot, kernels, keep, send, source, taps, stacked, sems):
+def input_kernel(chans, at, cot, kernels, keep, send, source, taps, stacked, made, sems, out_sems):
     side, far, core = at[1], at[2], at[3]
     depth, rows, width, filters = source.shape
     rows = rows - 2
@@ -218,10 +265,19 @@
         copies.append(
             (
                 pltpu.make_async_copy(kernels.at[n], taps.at[n], sems.at[n, 0]),
-                pltpu.make_async_copy(cot.at[n], source.at[n], sems.at[n, 1]),
+                [
+                    pltpu.make_async_copy(
+                        cot.at[n, pl.ds(first, (rows + 2) // 2)],
+                        source.at[n, pl.ds(first, (rows + 2) // 2)],
+                        sems.at[n, 1 + (first > 0)],
+                    )
+                    for first in (0, (rows + 2) // 2)
+                ],
             )
         )
-        for copy in copies[n]:
+        copies[n][0].start()
+    for n in range(depth):
+        for copy in copies[n][1]:
             copy.start()
     part = filters // chans
     places = chans if part % 16 == 0 else 1
@@ -237,15 +293,18 @@
                         pl.ds((n * 3 + i) * filters + place * size, size), pl.ds(j * chans_in, chans_in)
                     ] = taps[n, 3 * i + j, of_chan]
     for n in range(depth):
-        copies[n][1].wait()
+        for copy in copies[n][1]:
+            copy.wait()
     half = rows // PAIR
-    chunk = min(8, half)
+    chunk = min(4, half)
     lanes = lax.broadcasted_iota(jnp.int32, (width, chans_in), 0)
 
-    for out, of_side in ((send, 1 - side), (keep, side)):
-
-        @pl.loop(0, half // chunk)
-        def _(step):
+    def result(place, step):
+        chosen = pl.ds(step * chunk, chunk)
+        return pltpu.make_async_copy(made.at[place, chosen], (send, keep)[place].at[chosen], out_sems.at[place, step])
+
+    for place, of_side in enumerate((1 - side, side)):
+        for step in range(half // chunk):
             first = of_side * half + step * chunk
             window = [
                 source[n, pl.ds(first + 2 - i, chunk)].reshape(chunk * width, filters)
@@ -265,7 +324,12 @@
                 ]
                 before_it = jnp.where(lanes < width - 1, pltpu.roll(here[0], width - 1, 0), 0.0)
                 behind_it = jnp.where(lanes >= 1, pltpu.roll(here[2], 1, 0), 0.0)
-                out[step * chunk + row] = here[1] + before_it + behind_it
+                made[place, step * chunk + row] = here[1] + before_it + behind_it
+            result(place, step).start()
+
+    for place in range(2):
+        for step in range(half // chunk):
+            result(place, step).wait()
 
 
 def input_partial(chans, at, cot, kernels):
@@ -277,12 +341,14 @@
         functools.partial(input_kernel, chans),
         out_shape=(half, half),
         in_specs=[SMEM, HBM, HBM],
-        out_specs=(VMEM, VMEM),
+        out_specs=(HBM, HBM),
         scratch_shapes=[
             pltpu.VMEM(cot.shape, BF16),
             pltpu.VMEM(kernels.shape, BF16),
             pltpu.VMEM((depth * 3 * filters, 3 * chans_in), BF16),
-            pltpu.SemaphoreType.DMA((depth, 2)),
+            pltpu.VMEM((PAIR, rows // PAIR, width, chans_in), F32),
+            pltpu.SemaphoreType.DMA((depth, 3)),
+            pltpu.SemaphoreType.DMA((PAIR, rows // PAIR // min(4, rows // PAIR))),
         ],
         compiler_params=params(58),
         cost_estimate=cost(

time: 173 us -> 172 us (level)
  Pallas kernels: 45.1 us -> 43.1 us
  transfers between devices with their start and end apart: 21 -> 21, of which waited for: 7 -> 7; matrix products, arithmetic and copies ran while one was open for 8% -> 8% of each run, Pallas kernels for 26% -> 25%
where the time goes in v2:
time: 172 us; the launch traced here: 171 us
  waiting for transfers between devices  65.9 us (38%)
  Pallas kernels  43.1 us (25%)
  starting transfers between devices  30.5 us (18%)
  between operations  14.4 us (8%)
  other arithmetic  9.94 us (6%)
  local copies, waits for them, and re-layouts  7.27 us (4%)
    ppermute x2, waiting for transfers between devices, line_step(): along[step] = lax.ppermute(along[step - 1], 'filt', down)  30.6 us
    pallas_call x2, Pallas kernels, forward_partial(): pl.pallas_call(functools.partial(forward_kernel, depth, chans, which), ou...  14.2 us
    pallas_call x2, Pallas kernels, input_partial(): pl.pallas_call(functools.partial(input_kernel, chans), out_shape=(half, h...  13.7 us
    ppermute x1, waiting for transfers between devices, line_step(): along[depth - 1] = along[1 - depth] = lax.ppermute(along[0], 'filt', across)  11.8 us
    all_to_all x1, waiting for transfers between devices, exchange(): lax.all_to_all(pieces, 'filt', 0, 0, axis_index_groups=lines(depth), tile...  11 us
    pallas_call x1, Pallas kernels, weight_gradient(): pl.pallas_call(functools.partial(weight_kernel, depth, scale), out_shape=...  10.8 us
    ppermute x6, starting transfers between devices, pair_swap(): return lax.ppermute(value, 'filt', pairs)  8.46 us
    ppermute x2, waiting for transfers between devices, fars_gather(): lax.ppermute(value, 'chan', [(c, (c + 2 * step) % chans) for c in range(c...  7.05 us
  transfers between devices with their start and end apart: 21, of which 7 were waited for; matrix products, arithmetic and copies ran while one was open for 8% of the time, Pallas kernels for 25%

profile of v2, /device:TPU:0, one launch (start us, length us, event | category | flops | bytes accessed | tf_op | source)
XLA Modules:
  0.0 171.1 jit_solution(7321644859081787199)
XLA Ops:
  7.2 3.0 %collective-permute-start.4 = (bf16[16,128,128]{2,1,0:T(8,128)(2,1)}, bf16[16,128,128]{2,1,0:T(8,128)(2,1)S(1)}, u32[]{:S(2)}, u32[]{:S(2)}) collective-permute-start(bf16[16,128,128]{2,1,0:T(8,128)(2,1)} %bitcast.42), channel_id=1, source_target_pairs={{0,16},{8,24},{16,0},{24,8},{1,17},{9,25},{17,1},{25,9},{2,18},{10... | collective-permute-start | bytes 1572872 | tf_op jit(solution)/shard_map/ppermute | solution.py:364
  10.2 4.3 %collective-permute-start = (bf16[8,128,256]{2,1,0:T(8,128)(2,1)}, bf16[8,128,256]{2,1,0:T(8,128)(2,1)}, u32[]{:S(2)}, u32[]{:S(2)}) collective-permute-start(bf16[8,128,256]{2,1,0:T(8,128)(2,1)} %bitcast.44), channel_id=1, source_target_pairs={{0,2},{1,3},{2,4},{3,5},{4,6},{5,7},{8,10},{9,11},{10,12},{11,13},... | collective-permute-start | bytes 1572872 | tf_op jit(solution)/shard_map/ppermute | solution.py:376
  14.5 1.3 collective-permute-start.1
  15.8 6.6 %collective-permute-start.2 = (bf16[8,128,256]{2,1,0:T(8,128)(2,1)}, bf16[8,128,256]{2,1,0:T(8,128)(2,1)S(1)}, u32[]{:S(2)}, u32[]{:S(2)}) collective-permute-start(bf16[8,128,256]{2,1,0:T(8,128)(2,1)} %bitcast.46), channel_id=1, source_target_pairs={{0,6},{1,7},{6,0},{7,1},{8,14},{9,15},{14,8},{15,9},{16,22},{17,23... | collective-permute-start | bytes 1572872 | tf_op jit(solution)/shard_map/ppermute | solution.py:381
  22.4 1.6 collective-permute-start.3
  24.0 1.1 pad_maximum_fusion.1
  25.1 1.2 collective-permute-done
  26.4 4.0 %collective-permute-done.1 = bf16[8,128,256]{2,1,0:T(8,128)(2,1)} collective-permute-done((bf16[8,128,256]{2,1,0:T(8,128)(2,1)}, bf16[8,128,256]{2,1,0:T(8,128)(2,1)}, u32[]{:S(2)}, u32[]{:S(2)}) %collective-permute-start.1) | collective-permute-done | bytes 524320 | tf_op jit(solution)/shard_map/ppermute | solution.py:377
  30.3 11.8 %collective-permute-done.2 = bf16[8,128,256]{2,1,0:T(8,128)(2,1)S(1)} collective-permute-done((bf16[8,128,256]{2,1,0:T(8,128)(2,1)}, bf16[8,128,256]{2,1,0:T(8,128)(2,1)S(1)}, u32[]{:S(2)}, u32[]{:S(2)}) %collective-permute-start.2) | collective-permute-done | bytes 524320 | tf_op jit(solution)/shard_map/ppermute | solution.py:381
  43.3 1.5 collective-permute-start.5
  44.8 1.3 collective-permute-start.6
  46.1 1.3 fusion
  47.5 1.6 collective-permute-start.7
  50.2 1.1 fusion.3
  51.4 1.1 fusion.2.cot
  53.6 26.6 %collective-permute-done.6 = bf16[8,128,256]{2,1,0:T(8,128)(2,1)} collective-permute-done((bf16[8,128,256]{2,1,0:T(8,128)(2,1)}, bf16[8,128,256]{2,1,0:T(8,128)(2,1)}, u32[]{:S(2)}, u32[]{:S(2)}) %collective-permute-start.6) | collective-permute-done | bytes 524320 | tf_op jit(solution)/shard_map/ppermute | solution.py:377
  81.1 3.5 %all-to-all-start = ((bf16[4,18,32,128]{3,2,1,0:T(8,128)(2,1)}), bf16[4,18,32,128]{3,2,1,0:T(8,128)(2,1)S(1)}, u32[]{:S(2)}, u32[]{:S(2)}) async-start(bf16[4,18,32,128]{3,2,1,0:T(8,128)(2,1)} %pad_maximum_fusion.2), calls=%async_computation | async-start | bytes 1179648 | tf_op jit(solution)/shard_map/all_to_all | solution.py:424
  84.6 2.0 %select_select_fusion.refs_3_ = bf16[8,128,256]{2,1,0:T(8,128)(2,1)} fusion(bf16[8,128,256]{2,1,0:T(8,128)(2,1)} %collective-permute-done.5, bf16[8,128,256]{2,1,0:T(8,128)(2,1)} %collective-permute-done.6, pred[]{:T(512)S(6)} %eq.18, pred[]{:T(512)S(6)} %eq.9), kind=kLoop, calls=%fused_computation.3 | loop fusion | flops 524288 | bytes 1572866 | tf_op jit(solution)/shard_map/jit(_where)/select_n | solution.py:50
  86.7 1.5 collective-permute-start.10
  89.5 11.0 %all-to-all-done = bf16[4,18,32,128]{3,2,1,0:T(8,128)(2,1)S(1)} async-done(((bf16[4,18,32,128]{3,2,1,0:T(8,128)(2,1)}), bf16[4,18,32,128]{3,2,1,0:T(8,128)(2,1)S(1)}, u32[]{:S(2)}, u32[]{:S(2)}) %all-to-all-start) | async-done | bytes 589856 | tf_op jit(solution)/shard_map/all_to_all | solution.py:424
  100.5 7.1 %forward.2 = (f32[16,128,128]{2,1,0:T(8,128)}, f32[16,128,128]{2,1,0:T(8,128)}) custom-call(s32[8]{0:T(128)} %concatenate.6.at, bf16[3,3,128,256]{3,2,1,0:T(8,128)(2,1)} %weights.3, bf16[8,128,256]{2,1,0:T(8,128)(2,1)} %bitcast.48, bf16[8,128,256]{2,1,0:T(8,128)(2,1)} %copy-done.9, bf16[8,128,256]{2,1,0:T(8,128)(2,1)} %copy-done.8, ...), custom_call_target="tpu_custom_call" | custom-call | flops 2415919104 | bytes 6291456 | tf_op jit(solution)/shard_map/forward/pallas_call | solution.py:136
  107.8 7.0 %collective-permute-done.14 = bf16[4,18,32,128]{3,2,1,0:T(8,128)(2,1)S(1)} collective-permute-done((bf16[4,18,32,128]{3,2,1,0:T(8,128)(2,1)S(1)}, bf16[4,18,32,128]{3,2,1,0:T(8,128)(2,1)S(1)}, u32[]{:S(2)}, u32[]{:S(2)}) %collective-permute-start.14) | collective-permute-done | bytes 589856 | tf_op jit(solution)/shard_map/ppermute | solution.py:364
  115.0 1.3 add.101
  116.6 7.0 %forward.3 = (f32[16,128,128]{2,1,0:T(8,128)}, f32[16,128,128]{2,1,0:T(8,128)}) custom-call(s32[8]{0:T(128)} %concatenate.6.at, bf16[3,3,128,256]{3,2,1,0:T(8,128)(2,1)} %weights.3, bf16[8,128,256]{2,1,0:T(8,128)(2,1)} %bitcast.49, bf16[8,128,256]{2,1,0:T(8,128)(2,1)} %copy-done.9, bf16[8,128,256]{2,1,0:T(8,128)(2,1)} %copy-done.8, ...), custom_call_target="tpu_custom_call" | custom-call | flops 2415919104 | bytes 6291456 | tf_op jit(solution)/shard_map/forward/pallas_call | solution.py:136
  124.8 4.4 %turned.1.cot = bf16[4,18,128,128]{3,2,1,0:T(8,128)(2,1)} custom-call(bf16[2,4,18,32,128]{4,3,2,1,0:T(8,128)(2,1)} %copy-done, bf16[2,4,18,32,128]{4,3,2,1,0:T(8,128)(2,1)} %copy-done.2), custom_call_target="tpu_custom_call" | custom-call | bytes 4718592 | tf_op jit(solution)/shard_map/turned/pallas_call | solution.py:246
  129.3 6.9 %input_gradient.2 = (f32[8,128,128]{2,1,0:T(8,128)}, f32[8,128,128]{2,1,0:T(8,128)}) custom-call(s32[8]{0:T(128)} %concatenate.6.at, bf16[4,18,128,128]{3,2,1,0:T(8,128)(2,1)} %turned.1.cot, bf16[4,9,128,128]{3,2,1,0:T(8,128)(2,1)} %all-gather.3.cloned.1.call-done.kernels), custom_call_target="tpu_custom_call" | custom-call | flops 2415919104 | bytes 3538944 | tf_op jit(solution)/shard_map/input_gradient/pallas_call | solution.py:340
  136.1 1.7 collective-permute-start.16
  137.8 4.1 %collective-permute-done.12 = f32[16,128,128]{2,1,0:T(8,128)S(1)} collective-permute-done((f32[16,128,128]{2,1,0:T(8,128)}, f32[16,128,128]{2,1,0:T(8,128)S(1)}, u32[]{:S(2)}, u32[]{:S(2)}) %collective-permute-start.12) | collective-permute-done | bytes 1048608 | tf_op jit(solution)/shard_map/ppermute | solution.py:471
  141.9 6.9 %input_gradient.3 = (f32[8,128,128]{2,1,0:T(8,128)}, f32[8,128,128]{2,1,0:T(8,128)}) custom-call(s32[8]{0:T(128)} %concatenate.6.at, bf16[4,18,128,128]{3,2,1,0:T(8,128)(2,1)} %turned.1.cot, bf16[4,9,128,128]{3,2,1,0:T(8,128)(2,1)} %all-gather.5.cloned.1.call-done.kernels), custom_call_target="tpu_custom_call" | custom-call | flops 2415919104 | bytes 3538944 | tf_op jit(solution)/shard_map/input_gradient/pallas_call | solution.py:340
  148.8 1.6 collective-permute-start.17
  151.4 1.1 add_convert_fusion.2
  152.5 10.8 %weight_gradient.1 = f32[3,384,256]{2,1,0:T(8,128)} custom-call(s32[8]{0:T(128)} %concatenate.6.at, bf16[66,128,128]{2,1,0:T(8,128)(2,1)} %copy-done.1, bf16[8,128,256]{2,1,0:T(8,128)(2,1)} %bitcast.50, bf16[8,128,256]{2,1,0:T(8,128)(2,1)} %copy-done.9, bf16[8,128,256]{2,1,0:T(8,128)(2,1)} %copy-done.8, bf16[8,128,256]{2,1,0:T(8,128)(2,1)} %select_select_fusion.refs_3_, ...), custom_call_target="tpu_custom_call" | custom-call | flops 4831838208 | bytes 6291456 | tf_op jit(solution)/shard_map/weight_gradient/pallas_call | solution.py:212
  (61 shorter events, 9.3 us)
Async XLA Ops:
  7.2 35.0 %copy-start.5 = (bf16[3,3,128,256]{3,2,1,0:T(8,128)(2,1)S(1)}, bf16[3,3,128,256]{3,2,1,0:T(8,128)(2,1)}, u32[]{:S(2)}) copy-start(bf16[3,3,128,256]{3,2,1,0:T(8,128)(2,1)} %weights.3) | copy-start | bytes 1769476
  7.2 82.3 %all-gather.3.cloned.1.call-start = ((), (), s32[]{:S(2)}) async-start(), calls=%async_computation.1 | async-start | bytes 1474560 | tf_op jit(solution)/shard_map/all_gather | solution.py:430
  7.2 16.8 %collective-permute-start.4 = (bf16[16,128,128]{2,1,0:T(8,128)(2,1)}, bf16[16,128,128]{2,1,0:T(8,128)(2,1)S(1)}, u32[]{:S(2)}, u32[]{:S(2)}) collective-permute-start(bf16[16,128,128]{2,1,0:T(8,128)(2,1)} %bitcast.42), channel_id=1, source_target_pairs={{0,16},{8,24},{16,0},{24,8},{1,17},{9,25},{17,1},{25,9},{2,18},{10... | collective-permute-start | bytes 1572872 | tf_op jit(solution)/shard_map/ppermute | solution.py:364
  10.2 16.1 %collective-permute-start = (bf16[8,128,256]{2,1,0:T(8,128)(2,1)}, bf16[8,128,256]{2,1,0:T(8,128)(2,1)}, u32[]{:S(2)}, u32[]{:S(2)}) collective-permute-start(bf16[8,128,256]{2,1,0:T(8,128)(2,1)} %bitcast.44), channel_id=1, source_target_pairs={{0,2},{1,3},{2,4},{3,5},{4,6},{5,7},{8,10},{9,11},{10,12},{11,13},... | collective-permute-start | bytes 1572872 | tf_op jit(solution)/shard_map/ppermute | solution.py:376
  14.5 15.8 %collective-permute-start.1 = (bf16[8,128,256]{2,1,0:T(8,128)(2,1)}, bf16[8,128,256]{2,1,0:T(8,128)(2,1)}, u32[]{:S(2)}, u32[]{:S(2)}) collective-permute-start(bf16[8,128,256]{2,1,0:T(8,128)(2,1)} %bitcast.45), channel_id=1, source_target_pairs={{2,0},{3,1},{4,2},{5,3},{6,4},{7,5},{10,8},{11,9},{12,10},{13,11},... | collective-permute-start | bytes 1572872 | tf_op jit(solution)/shard_map/ppermute | solution.py:377
  15.8 26.4 %collective-permute-start.2 = (bf16[8,128,256]{2,1,0:T(8,128)(2,1)}, bf16[8,128,256]{2,1,0:T(8,128)(2,1)S(1)}, u32[]{:S(2)}, u32[]{:S(2)}) collective-permute-start(bf16[8,128,256]{2,1,0:T(8,128)(2,1)} %bitcast.46), channel_id=1, source_target_pairs={{0,6},{1,7},{6,0},{7,1},{8,14},{9,15},{14,8},{15,9},{16,22},{17,23... | collective-permute-start | bytes 1572872 | tf_op jit(solution)/shard_map/ppermute | solution.py:381
  22.4 19.8 %collective-permute-start.3 = (bf16[8,128,256]{2,1,0:T(8,128)(2,1)}, bf16[8,128,256]{2,1,0:T(8,128)(2,1)S(1)}, u32[]{:S(2)}, u32[]{:S(2)}) collective-permute-start(bf16[8,128,256]{2,1,0:T(8,128)(2,1)} %bitcast.47), channel_id=1, source_target_pairs={{0,1},{1,0},{2,3},{3,2},{4,5},{5,4},{6,7},{7,6},{8,9},{9,8},{10,11... | collective-permute-start | bytes 1572872 | tf_op jit(solution)/shard_map/ppermute | solution.py:391
  42.2 1.0 copy-start.10
  42.2 8.0 %collective-permute-start.9 = (bf16[2,16,128,128]{3,2,1,0:T(8,128)(2,1)S(1)}, bf16[2,16,128,128]{3,2,1,0:T(8,128)(2,1)}, u32[]{:S(2)}, u32[]{:S(2)}) collective-permute-start(bf16[2,16,128,128]{3,2,1,0:T(8,128)(2,1)S(1)} %pad_maximum_fusion.1), channel_id=1, source_target_pairs={{0,8},{8,0},{16,24},{24,16},{1,9},{9,1},{17,25},{25,17},{2,10},{10... | collective-permute-start | bytes 3145736 | tf_op jit(solution)/shard_map/ppermute | solution.py:386
  43.3 10.3 %collective-permute-start.5 = (bf16[8,128,256]{2,1,0:T(8,128)(2,1)}, bf16[8,128,256]{2,1,0:T(8,128)(2,1)}, u32[]{:S(2)}, u32[]{:S(2)}) collective-permute-start(bf16[8,128,256]{2,1,0:T(8,128)(2,1)} %collective-permute-done), channel_id=1, source_target_pairs={{2,4},{3,5},{4,6},{5,7},{10,12},{11,13},{12,14},{13,15},{18,20},{1... | collective-permute-start | bytes 1572872 | tf_op jit(solution)/shard_map/ppermute | solution.py:376
  44.8 35.5 %collective-permute-start.6 = (bf16[8,128,256]{2,1,0:T(8,128)(2,1)}, bf16[8,128,256]{2,1,0:T(8,128)(2,1)}, u32[]{:S(2)}, u32[]{:S(2)}) collective-permute-start(bf16[8,128,256]{2,1,0:T(8,128)(2,1)} %collective-permute-done.1), channel_id=1, source_target_pairs={{2,0},{3,1},{4,2},{5,3},{10,8},{11,9},{12,10},{13,11},{18,16},{19,... | collective-permute-start | bytes 1572872 | tf_op jit(solution)/shard_map/ppermute | solution.py:377
  47.4 3.9 %copy-start.8 = (bf16[8,128,256]{2,1,0:T(8,128)(2,1)}, bf16[8,128,256]{2,1,0:T(8,128)(2,1)S(1)}, u32[]{:S(2)}) copy-start(bf16[8,128,256]{2,1,0:T(8,128)(2,1)S(1)} %get-tuple-element.55.refs_2_) | copy-start | bytes 1572868
  47.4 3.9 %copy-start.9 = (bf16[8,128,256]{2,1,0:T(8,128)(2,1)}, bf16[8,128,256]{2,1,0:T(8,128)(2,1)S(1)}, u32[]{:S(2)}) copy-start(bf16[8,128,256]{2,1,0:T(8,128)(2,1)S(1)} %get-tuple-element.56.refs_1_) | copy-start | bytes 1572868
  47.5 32.8 %collective-permute-start.7 = (bf16[8,128,256]{2,1,0:T(8,128)(2,1)S(1)}, bf16[8,128,256]{2,1,0:T(8,128)(2,1)S(1)}, u32[]{:S(2)}, u32[]{:S(2)}) collective-permute-start(bf16[8,128,256]{2,1,0:T(8,128)(2,1)S(1)} %get-tuple-element.56.refs_1_), channel_id=1, source_target_pairs={{0,1},{1,0},{2,3},{3,2},{4,5},{5,4},{6,7},{7,6},{8,9},{9,8},{10,11... | collective-permute-start | bytes 1572872 | tf_op jit(solution)/shard_map/ppermute | solution.py:391
  49.0 32.1 %collective-permute-start.8 = (bf16[8,128,256]{2,1,0:T(8,128)(2,1)S(1)}, bf16[8,128,256]{2,1,0:T(8,128)(2,1)}, u32[]{:S(2)}, u32[]{:S(2)}) collective-permute-start(bf16[8,128,256]{2,1,0:T(8,128)(2,1)S(1)} %get-tuple-element.55.refs_2_), channel_id=1, source_target_pairs={{0,1},{1,0},{2,3},{3,2},{4,5},{5,4},{6,7},{7,6},{8,9},{9,8},{10,11... | collective-permute-start | bytes 1572872 | tf_op jit(solution)/shard_map/ppermute | solution.py:391
  52.5 34.1 %copy-start.1 = (bf16[66,128,128]{2,1,0:T(8,128)(2,1)}, bf16[66,128,128]{2,1,0:T(8,128)(2,1)S(1)}, u32[]{:S(2)}) copy-start(bf16[66,128,128]{2,1,0:T(8,128)(2,1)S(1)} %fusion.2.cot) | copy-start | bytes 6488068
  81.1 19.4 %all-to-all-start = ((bf16[4,18,32,128]{3,2,1,0:T(8,128)(2,1)}), bf16[4,18,32,128]{3,2,1,0:T(8,128)(2,1)S(1)}, u32[]{:S(2)}, u32[]{:S(2)}) async-start(bf16[4,18,32,128]{3,2,1,0:T(8,128)(2,1)} %pad_maximum_fusion.2), calls=%async_computation | async-start | bytes 1179648 | tf_op jit(solution)/shard_map/all_to_all | solution.py:424
  84.6 57.3 %all-gather.5.cloned.1.call-start = ((), (), s32[]{:S(2)}) async-start(), calls=%async_computation.2 | async-start | bytes 1474560 | tf_op jit(solution)/shard_map/all_gather | solution.py:430
  86.7 13.9 %collective-permute-start.10 = (bf16[8,128,256]{2,1,0:T(8,128)(2,1)}, bf16[8,128,256]{2,1,0:T(8,128)(2,1)}, u32[]{:S(2)}, u32[]{:S(2)}) collective-permute-start(bf16[8,128,256]{2,1,0:T(8,128)(2,1)} %select_select_fusion.refs_3_), channel_id=1, source_target_pairs={{0,1},{1,0},{2,3},{3,2},{4,5},{5,4},{6,7},{7,6},{8,9},{9,8},{10,11... | collective-permute-start | bytes 1572872 | tf_op jit(solution)/shard_map/ppermute | solution.py:391
  100.5 14.3 %collective-permute-start.14 = (bf16[4,18,32,128]{3,2,1,0:T(8,128)(2,1)S(1)}, bf16[4,18,32,128]{3,2,1,0:T(8,128)(2,1)S(1)}, u32[]{:S(2)}, u32[]{:S(2)}) collective-permute-start(bf16[4,18,32,128]{3,2,1,0:T(8,128)(2,1)S(1)} %all-to-all-done), channel_id=1, source_target_pairs={{0,16},{8,24},{16,0},{24,8},{1,17},{9,25},{17,1},{25,9},{2,18},{10... | collective-permute-start | bytes 1769480 | tf_op jit(solution)/shard_map/ppermute | solution.py:364
  107.7 7.4 %copy-start.4 = (f32[16,128,128]{2,1,0:T(8,128)S(1)}, f32[16,128,128]{2,1,0:T(8,128)}, u32[]{:S(2)}) copy-start(f32[16,128,128]{2,1,0:T(8,128)} %get-tuple-element.35) | copy-start | bytes 3145732
  107.7 7.4 %collective-permute-start.11 = (f32[16,128,128]{2,1,0:T(8,128)}, f32[16,128,128]{2,1,0:T(8,128)S(1)}, u32[]{:S(2)}, u32[]{:S(2)}) collective-permute-start(f32[16,128,128]{2,1,0:T(8,128)} %get-tuple-element.36), channel_id=1, source_target_pairs={{0,8},{8,0},{16,24},{24,16},{1,9},{9,1},{17,25},{25,17},{2,10},{10... | collective-permute-start | bytes 3145736 | tf_op jit(solution)/shard_map/ppermute | solution.py:386
  114.9 8.7 %copy-start = (bf16[2,4,18,32,128]{4,3,2,1,0:T(8,128)(2,1)}, bf16[2,4,18,32,128]{4,3,2,1,0:T(8,128)(2,1)S(1)}, u32[]{:S(2)}) copy-start(bf16[2,4,18,32,128]{4,3,2,1,0:T(8,128)(2,1)S(1)} %pad_maximum_fusion.same) | copy-start | bytes 3538948
  114.9 8.8 %collective-permute-start.15 = (bf16[2,4,18,32,128]{4,3,2,1,0:T(8,128)(2,1)S(1)}, bf16[2,4,18,32,128]{4,3,2,1,0:T(8,128)(2,1)S(1)}, u32[]{:S(2)}, u32[]{:S(2)}) collective-permute-start(bf16[2,4,18,32,128]{4,3,2,1,0:T(8,128)(2,1)S(1)} %pad_maximum_fusion.same), channel_id=1, source_target_pairs={{0,8},{8,0},{16,24},{24,16},{1,9},{9,1},{17,25},{25,17},{2,10},{10... | collective-permute-start | bytes 3538952 | tf_op jit(solution)/shard_map/ppermute | solution.py:386
  116.3 25.6 %collective-permute-start.12 = (f32[16,128,128]{2,1,0:T(8,128)}, f32[16,128,128]{2,1,0:T(8,128)S(1)}, u32[]{:S(2)}, u32[]{:S(2)}) collective-permute-start(f32[16,128,128]{2,1,0:T(8,128)} %add.101), channel_id=1, source_target_pairs={{0,16},{8,24},{16,0},{24,8},{1,17},{9,25},{17,1},{25,9},{2,18},{10... | collective-permute-start | bytes 3145736 | tf_op jit(solution)/shard_map/ppermute | solution.py:471
  123.6 26.8 %collective-permute-start.13 = (f32[16,128,128]{2,1,0:T(8,128)}, f32[16,128,128]{2,1,0:T(8,128)S(1)}, u32[]{:S(2)}, u32[]{:S(2)}) collective-permute-start(f32[16,128,128]{2,1,0:T(8,128)} %get-tuple-element.40), channel_id=1, source_target_pairs={{0,8},{8,0},{16,24},{24,16},{1,9},{9,1},{17,25},{25,17},{2,10},{10... | collective-permute-start | bytes 3145736 | tf_op jit(solution)/shard_map/ppermute | solution.py:386
  123.7 1.1 copy-start.2
  136.1 14.3 %copy-start.3 = (f32[16,128,128]{2,1,0:T(8,128)S(1)}, f32[16,128,128]{2,1,0:T(8,128)}, u32[]{:S(2)}) copy-start(f32[16,128,128]{2,1,0:T(8,128)} %get-tuple-element.39) | copy-start | bytes 3145732
  136.1 15.2 %collective-permute-start.16 = (f32[8,128,128]{2,1,0:T(8,128)}, f32[8,128,128]{2,1,0:T(8,128)}, u32[]{:S(2)}, u32[]{:S(2)}) collective-permute-start(f32[8,128,128]{2,1,0:T(8,128)} %get-tuple-element.43), channel_id=1, source_target_pairs={{0,1},{1,0},{2,3},{3,2},{4,5},{5,4},{6,7},{7,6},{8,9},{9,8},{10,11... | collective-permute-start | bytes 1572872 | tf_op jit(solution)/shard_map/ppermute | solution.py:391
  148.8 2.6 %copy-start.7 = (f32[8,128,128]{2,1,0:T(8,128)S(1)}, f32[8,128,128]{2,1,0:T(8,128)}, u32[]{:S(2)}) copy-start(f32[8,128,128]{2,1,0:T(8,128)} %get-tuple-element.42) | copy-start | bytes 1572868
  148.8 14.5 %collective-permute-start.17 = (f32[8,128,128]{2,1,0:T(8,128)}, f32[8,128,128]{2,1,0:T(8,128)S(1)}, u32[]{:S(2)}, u32[]{:S(2)}) collective-permute-start(f32[8,128,128]{2,1,0:T(8,128)} %get-tuple-element.46), channel_id=1, source_target_pairs={{0,1},{1,0},{2,3},{3,2},{4,5},{5,4},{6,7},{7,6},{8,9},{9,8},{10,11... | collective-permute-start | bytes 1572872 | tf_op jit(solution)/shard_map/ppermute | solution.py:391
  152.5 10.8 %copy-start.6 = (f32[8,128,128]{2,1,0:T(8,128)S(1)}, f32[8,128,128]{2,1,0:T(8,128)}, u32[]{:S(2)}) copy-start(f32[8,128,128]{2,1,0:T(8,128)} %get-tuple-element.45) | copy-start | bytes 1572868
  (1 other events, 0.8 us)
Sparse Core Ops, SparseCore 0:
  43.3 36.4 all-gather.2
  107.9 30.6 all-gather.4

commit v3 on v2

--- a/solution.py
+++ b/solution.py
@@ -255,7 +255,7 @@
     )(same, cross)
 
 
-def input_kernel(chans, at, cot, kernels, keep, send, source, taps, stacked, made, sems, out_sems):
+def input_kernel(chans, index, at, cot, kernels, keep, send, source, taps, stacked, made, sems, out_sems):
     side, far, core = at[1], at[2], at[3]
     depth, rows, width, filters = source.shape
     rows = rows - 2
@@ -264,7 +264,9 @@
     for n in range(depth):
         copies.append(
             (
-                pltpu.make_async_copy(kernels.at[n], taps.at[n], sems.at[n, 0]),
+                pltpu.make_async_copy(
+                    kernels.at[n, :, :, pl.ds(index * chans_in, chans_in)], taps.at[n], sems.at[n, 0]
+                ),
                 [
                     pltpu.make_async_copy(
                         cot.at[n, pl.ds(first, (rows + 2) // 2)],
@@ -332,19 +334,19 @@
             result(place, step).wait()
 
 
-def input_partial(chans, at, cot, kernels):
+def input_partial(chans, at, cot, kernels, index, halves):
     depth, rows, width, filters = cot.shape
     rows = rows - 2
-    chans_in = kernels.shape[3]
+    chans_in = kernels.shape[3] // halves
     half = jax.ShapeDtypeStruct((rows // PAIR, width, chans_in), F32)
     return pl.pallas_call(
-        functools.partial(input_kernel, chans),
+        functools.partial(input_kernel, chans, index),
         out_shape=(half, half),
         in_specs=[SMEM, HBM, HBM],
         out_specs=(HBM, HBM),
         scratch_shapes=[
             pltpu.VMEM(cot.shape, BF16),
-            pltpu.VMEM(kernels.shape, BF16),
+            pltpu.VMEM(kernels.shape[:3] + (chans_in,), BF16),
             pltpu.VMEM((depth * 3 * filters, 3 * chans_in), BF16),
             pltpu.VMEM((PAIR, rows // PAIR, width, chans_in), F32),
             pltpu.SemaphoreType.DMA((depth, 3)),
@@ -424,24 +426,21 @@
         return lax.all_to_all(pieces, "filt", 0, 0, axis_index_groups=lines(depth), tiled=True)
 
     halves = PAIR if chans_in % (PAIR * 128) == 0 else 1
-    kernels = []
-    for half in jnp.split(weights, halves, axis=3):
-        half = half.reshape((9,) + half.shape[2:])
-        kernels.append(lax.all_gather(half, "filt", axis=0, axis_index_groups=lines(depth)))
+    kernels = lax.all_gather(weights, "filt", axis=0, axis_index_groups=lines(depth))
+    kernels = kernels.reshape((depth, 9) + weights.shape[2:])
 
     mine, theirs = [inputs[0]], [pair_swap(inputs[0], depth)]
     same = fars_gather(cotangent[0], chans)
     along = line_step({0: inputs[0]}, 1, depth)
-    fresh = theirs + [same]
+    padded = all_rows(after(same, along[-1], along[1], *theirs))
+    pieces = line_pieces(padded)
+    fresh = theirs + [pieces]
     stages = max(2, depth - 1)
     for stage in range(2, stages + 1):
         ways = list(along)
         ready = lax.optimization_barrier([along[way] for way in ways] + fresh)
         along = dict(zip(ways, ready))
         if stage == 2:
-            padded = all_rows(ready[-1])
-            pieces = line_pieces(padded)
-        elif stage == 3:
             pieces = exchange(ready[-1])
         fresh = []
         if stage < stages:
@@ -450,36 +449,36 @@
             mine.append(arrival(along, depth, line, len(theirs) - 1))
             theirs.append(pair_swap(mine[-1], depth))
             fresh.append(theirs[-1])
-        fresh.append(pieces)
-    if stages < 3:
-        pieces = exchange(pieces)
     same = fars_gather(pieces, chans)
     sources = turned(same, core_swap(same, chans))
 
     if part % 16:
         order = [(far - c // 2 + chans // 2) % (chans // 2) * 2 + (core + c) % 2 for c in range(chans)]
-        split = [half.reshape((depth, 9, chans, part, -1)) for half in kernels]
-        kernels = [jnp.take(half, jnp.stack(order), axis=2).reshape(kernels[0].shape) for half in split]
-
-    outputs, came, at_next = None, [], after(at, kernels[0], pieces)
+        split = kernels.reshape((depth, 9, chans, part, chans_in))
+        kernels = jnp.take(split, jnp.stack(order), axis=2).reshape(kernels.shape)
+
+    outputs, input_grad, at_next = None, [], after(at, kernels)
+
+    def next_half(at_next):
+        kept, sent = input_partial(chans, at_next, sources, kernels, len(input_grad), halves)
+        input_grad.append((kept + pair_swap(sent, depth)).astype(BF16))
+        return after(at, sent)
+
     for which in [*range(1, chans // 2), 0]:
         keep, send = forward_partial(depth, chans, which, at_next, weights, mine, theirs)
         at_next = after(at, send)
         moving = keep + core_swap(send, chans)
         if which:
+            if not input_grad:
+                at_next = next_half(at_next)
             at_next = after(at_next, moving)
             moving = lax.ppermute(moving, "chan", [(c, (c + 2 * which) % chans) for c in range(chans)])
-            came.append(moving)
         outputs = moving if outputs is None else outputs + moving
     outputs = outputs.astype(BF16)[None]
-
-    input_grad = []
-    for half in kernels:
-        kept, sent = input_partial(chans, at_next, sources, half)
-        at_next = after(at_next, sent, *came)
-        input_grad.append((kept + pair_swap(sent, depth)).astype(BF16))
-    at_next = after(at_next, *input_grad[:-1])
+    while len(input_grad) < halves:
+        at_next = next_half(at_next)
     input_grad = jnp.concatenate(input_grad, axis=2)[None]
+
     weight_grad = weight_gradient(depth, at_next, scale, padded, mine, theirs)
     weight_grad = weight_grad.reshape((3, 3, filters, chans_in))
     return (outputs, input_grad, weight_grad)

time: 172 us -> 183 us (1.064)
  waiting for transfers between devices: 65.9 us -> 75.4 us
    ppermute x2, waiting for transfers between devices: 30.6 us -> 14.3 us  [line_step(): along[step] = lax.ppermute(along[step - 1], 'filt', down)]
    all_to_all x1, waiting for transfers between devices: 11 us -> 25.4 us  [exchange(): lax.all_to_all(pieces, 'filt', 0, 0, axis_index_groups=lines(depth), tile...]
    ppermute x6, waiting for transfers between devices: 0.02 us -> 12.4 us  [pair_swap(): return lax.ppermute(value, 'filt', pairs)]
    ppermute x1, waiting for transfers between devices: 11.8 us -> 17.9 us  [line_step(): along[depth - 1] = along[1 - depth] = lax.ppermute(along[0], 'filt', across)]
    ppermute x1, waiting for transfers between devices: 4.08 us -> 0.01 us  [body(): lax.ppermute(moving, 'chan', [(c, (c + 2 * which) % chans) for c in range...]
    ppermute x2, waiting for transfers between devices: 7.05 us -> 4.74 us  [fars_gather(): lax.ppermute(value, 'chan', [(c, (c + 2 * step) % chans) for c in range(c...]
    ppermute x6, starting transfers between devices: 8.46 us -> 6.36 us  [pair_swap(): return lax.ppermute(value, 'filt', pairs)]
    all_to_all x1, starting transfers between devices: 3.48 us -> 5.55 us  [exchange(): lax.all_to_all(pieces, 'filt', 0, 0, axis_index_groups=lines(depth), tile...]
  transfers between devices with their start and end apart: 21 -> 20, of which waited for: 7 -> 9; matrix products, arithmetic and copies ran while one was open for 8% -> 7% of each run, Pallas kernels for 25% -> 24%
where the time goes in v3:
time: 183 us; the launch traced here: 181 us
  waiting for transfers between devices  75.4 us (41%)
  Pallas kernels  43.1 us (24%)
  starting transfers between devices  30.7 us (17%)
  between operations  14.4 us (8%)
  other arithmetic  9.35 us (5%)
  local copies, waits for them, and re-layouts  7.9 us (4%)
    all_to_all x1, waiting for transfers between devices, exchange(): lax.all_to_all(pieces, 'filt', 0, 0, axis_index_groups=lines(depth), tile...  25.4 us
    ppermute x1, waiting for transfers between devices, line_step(): along[depth - 1] = along[1 - depth] = lax.ppermute(along[0], 'filt', across)  17.9 us
    ppermute x2, waiting for transfers between devices, line_step(): along[step] = lax.ppermute(along[step - 1], 'filt', down)  14.3 us
    pallas_call x2, Pallas kernels, forward_partial(): pl.pallas_call(functools.partial(forward_kernel, depth, chans, which), ou...  14.1 us
    pallas_call x2, Pallas kernels, input_partial(): pl.pallas_call(functools.partial(input_kernel, chans, index), out_shape=(...  13.9 us
    ppermute x6, waiting for transfers between devices, pair_swap(): return lax.ppermute(value, 'filt', pairs)  12.4 us
    pallas_call x1, Pallas kernels, weight_gradient(): pl.pallas_call(functools.partial(weight_kernel, depth, scale), out_shape=...  10.6 us
    ppermute x1, starting transfers between devices, line_step(): along[depth - 1] = along[1 - depth] = lax.ppermute(along[0], 'filt', across)  6.37 us
  transfers between devices with their start and end apart: 20, of which 9 were waited for; matrix products, arithmetic and copies ran while one was open for 7% of the time, Pallas kernels for 24%

profile of v3, /device:TPU:0, one launch (start us, length us, event | category | flops | bytes accessed | tf_op | source)
XLA Modules:
  0.0 180.8 jit_solution(14203616736436582846)
XLA Ops:
  7.2 3.0 %collective-permute-start.4 = (bf16[16,128,128]{2,1,0:T(8,128)(2,1)}, bf16[16,128,128]{2,1,0:T(8,128)(2,1)S(1)}, u32[]{:S(2)}, u32[]{:S(2)}) collective-permute-start(bf16[16,128,128]{2,1,0:T(8,128)(2,1)} %bitcast.39), channel_id=1, source_target_pairs={{0,16},{8,24},{16,0},{24,8},{1,17},{9,25},{17,1},{25,9},{2,18},{10... | collective-permute-start | bytes 1572872 | tf_op jit(solution)/shard_map/ppermute | solution.py:366
  10.2 1.5 collective-permute-start.3
  11.7 1.3 collective-permute-start.1
  13.0 4.6 %collective-permute-start = (bf16[8,128,256]{2,1,0:T(8,128)(2,1)}, bf16[8,128,256]{2,1,0:T(8,128)(2,1)S(1)}, u32[]{:S(2)}, u32[]{:S(2)}) collective-permute-start(bf16[8,128,256]{2,1,0:T(8,128)(2,1)} %bitcast.6.refs_0_), channel_id=1, source_target_pairs={{0,2},{1,3},{2,4},{3,5},{4,6},{5,7},{8,10},{9,11},{10,12},{11,13},... | collective-permute-start | bytes 1572872 | tf_op jit(solution)/shard_map/ppermute | solution.py:378
  17.6 4.7 %collective-permute-done.4 = bf16[16,128,128]{2,1,0:T(8,128)(2,1)S(1)} collective-permute-done((bf16[16,128,128]{2,1,0:T(8,128)(2,1)}, bf16[16,128,128]{2,1,0:T(8,128)(2,1)S(1)}, u32[]{:S(2)}, u32[]{:S(2)}) %collective-permute-start.4) | collective-permute-done | bytes 524320 | tf_op jit(solution)/shard_map/ppermute | solution.py:366
  22.3 1.1 pad_maximum_fusion.1
  23.8 3.1 %collective-permute-done.1 = bf16[8,128,256]{2,1,0:T(8,128)(2,1)S(1)} collective-permute-done((bf16[8,128,256]{2,1,0:T(8,128)(2,1)}, bf16[8,128,256]{2,1,0:T(8,128)(2,1)S(1)}, u32[]{:S(2)}, u32[]{:S(2)}) %collective-permute-start.1) | collective-permute-done | bytes 524320 | tf_op jit(solution)/shard_map/ppermute | solution.py:379
  29.0 6.4 %collective-permute-start.2 = (bf16[8,128,256]{2,1,0:T(8,128)(2,1)}, bf16[8,128,256]{2,1,0:T(8,128)(2,1)}, u32[]{:S(2)}, u32[]{:S(2)}) collective-permute-start(bf16[8,128,256]{2,1,0:T(8,128)(2,1)} %bitcast.6.refs_0_), channel_id=1, source_target_pairs={{0,6},{1,7},{6,0},{7,1},{8,14},{9,15},{14,8},{15,9},{16,22},{17,23... | collective-permute-start | bytes 1572872 | tf_op jit(solution)/shard_map/ppermute | solution.py:383
  36.1 1.2 fusion.3
  37.4 1.1 fusion.2.cot
  38.6 1.0 pad_maximum_fusion.2
  39.6 17.9 %collective-permute-done.2 = bf16[8,128,256]{2,1,0:T(8,128)(2,1)} collective-permute-done((bf16[8,128,256]{2,1,0:T(8,128)(2,1)}, bf16[8,128,256]{2,1,0:T(8,128)(2,1)}, u32[]{:S(2)}, u32[]{:S(2)}) %collective-permute-start.2) | collective-permute-done | bytes 524320 | tf_op jit(solution)/shard_map/ppermute | solution.py:383
  57.5 5.6 %all-to-all-start = ((bf16[4,18,32,128]{3,2,1,0:T(8,128)(2,1)}), bf16[4,18,32,128]{3,2,1,0:T(8,128)(2,1)S(1)}, u32[]{:S(2)}, u32[]{:S(2)}) async-start(bf16[4,18,32,128]{3,2,1,0:T(8,128)(2,1)} %pad_maximum_fusion.2), calls=%async_computation | async-start | bytes 1179648 | tf_op jit(solution)/shard_map/all_to_all | solution.py:426
  63.1 1.5 collective-permute-start.6
  64.5 1.3 collective-permute-start.7
  65.8 2.5 %fusion = (bf16[8,128,256]{2,1,0:T(8,128)(2,1)}, bf16[8,128,256]{2,1,0:T(8,128)(2,1)}) fusion(bf16[8,128,256]{2,1,0:T(8,128)(2,1)} %collective-permute-done.2, bf16[8,128,256]{2,1,0:T(8,128)(2,1)} %copy-done.8, pred[]{:T(512)S(6)} %eq.19, pred[]{:T(512)S(6)} %eq.18, pred[]{:T(512)S(6)} %eq.9, bf16[8,128,256]{2,1,0:T(8,128)(2,1)} %copy-done.9), kind=kLoop, calls=%fused_computation.7 | loop fusion | flops 1572864 | bytes 2621443 | tf_op jit(solution)/shard_map/jit(_where)/select_n | solution.py:50
  68.3 2.0 %collective-permute-start.8 = (bf16[8,128,256]{2,1,0:T(8,128)(2,1)}, bf16[8,128,256]{2,1,0:T(8,128)(2,1)S(1)}, u32[]{:S(2)}, u32[]{:S(2)}) collective-permute-start(bf16[8,128,256]{2,1,0:T(8,128)(2,1)} %get-tuple-element.52.refs_1_), channel_id=1, source_target_pairs={{0,1},{1,0},{2,3},{3,2},{4,5},{5,4},{6,7},{7,6},{8,9},{9,8},{10,11... | collective-permute-start | bytes 1572872 | tf_op jit(solution)/shard_map/ppermute | solution.py:393
  70.3 25.4 %all-to-all-done = bf16[4,18,32,128]{3,2,1,0:T(8,128)(2,1)S(1)} async-done(((bf16[4,18,32,128]{3,2,1,0:T(8,128)(2,1)}), bf16[4,18,32,128]{3,2,1,0:T(8,128)(2,1)S(1)}, u32[]{:S(2)}, u32[]{:S(2)}) %all-to-all-start) | async-done | bytes 589856 | tf_op jit(solution)/shard_map/all_to_all | solution.py:426
  95.7 11.2 %collective-permute-done.7 = bf16[8,128,256]{2,1,0:T(8,128)(2,1)} collective-permute-done((bf16[8,128,256]{2,1,0:T(8,128)(2,1)}, bf16[8,128,256]{2,1,0:T(8,128)(2,1)}, u32[]{:S(2)}, u32[]{:S(2)}) %collective-permute-start.7) | collective-permute-done | bytes 524320 | tf_op jit(solution)/shard_map/ppermute | solution.py:379
  107.7 1.4 select_select_fusion.refs_3_
  109.8 1.2 pad_maximum_fusion.same
  112.4 10.3 %collective-permute-done.10.refs_7_ = bf16[8,128,256]{2,1,0:T(8,128)(2,1)} collective-permute-done((bf16[8,128,256]{2,1,0:T(8,128)(2,1)S(1)}, bf16[8,128,256]{2,1,0:T(8,128)(2,1)}, u32[]{:S(2)}, u32[]{:S(2)}) %collective-permute-start.10) | collective-permute-done | bytes 524320 | tf_op jit(solution)/shard_map/ppermute | solution.py:393
  122.8 7.1 %forward.2 = (f32[16,128,128]{2,1,0:T(8,128)}, f32[16,128,128]{2,1,0:T(8,128)}) custom-call(s32[8]{0:T(128)} %concatenate.6.at, bf16[3,3,128,256]{3,2,1,0:T(8,128)(2,1)} %weights.3, bf16[8,128,256]{2,1,0:T(8,128)(2,1)} %bitcast.6.refs_0_, bf16[8,128,256]{2,1,0:T(8,128)(2,1)} %get-tuple-element.52.refs_1_, bf16[8,128,256]{2,1,0:T(8,128)(2,1)} %get-tuple-element.51.refs_2_, ...), custom_call_target="tpu_custom_call" | custom-call | flops 2415919104 | bytes 6291456 | tf_op jit(solution)/shard_map/forward/pallas_call | solution.py:136
  130.0 1.1 copy-done.3
  131.1 4.4 %turned.1.cot = bf16[4,18,128,128]{3,2,1,0:T(8,128)(2,1)} custom-call(bf16[2,4,18,32,128]{4,3,2,1,0:T(8,128)(2,1)} %copy-done, bf16[2,4,18,32,128]{4,3,2,1,0:T(8,128)(2,1)} %copy-done.3), custom_call_target="tpu_custom_call" | custom-call | bytes 4718592 | tf_op jit(solution)/shard_map/turned/pallas_call | solution.py:246
  135.5 7.0 %input_gradient.2 = (f32[8,128,128]{2,1,0:T(8,128)}, f32[8,128,128]{2,1,0:T(8,128)}) custom-call(s32[8]{0:T(128)} %concatenate.6.at, bf16[4,18,128,128]{3,2,1,0:T(8,128)(2,1)} %turned.1.cot, bf16[4,9,128,256]{3,2,1,0:T(8,128)(2,1)} %bitcast.41), custom_call_target="tpu_custom_call" | custom-call | flops 2415919104 | bytes 3538944 | tf_op jit(solution)/shard_map/input_gradient/pallas_call | solution.py:342
  144.0 7.0 %forward.3 = (f32[16,128,128]{2,1,0:T(8,128)}, f32[16,128,128]{2,1,0:T(8,128)}) custom-call(s32[8]{0:T(128)} %concatenate.6.at, bf16[3,3,128,256]{3,2,1,0:T(8,128)(2,1)} %weights.3, bf16[8,128,256]{2,1,0:T(8,128)(2,1)} %bitcast.6.refs_0_, bf16[8,128,256]{2,1,0:T(8,128)(2,1)} %get-tuple-element.52.refs_1_, bf16[8,128,256]{2,1,0:T(8,128)(2,1)} %get-tuple-element.51.refs_2_, ...), custom_call_target="tpu_custom_call" | custom-call | flops 2415919104 | bytes 6291456 | tf_op jit(solution)/shard_map/forward/pallas_call | solution.py:136
  151.1 6.9 %input_gradient.3 = (f32[8,128,128]{2,1,0:T(8,128)}, f32[8,128,128]{2,1,0:T(8,128)}) custom-call(s32[8]{0:T(128)} %concatenate.6.at, bf16[4,18,128,128]{3,2,1,0:T(8,128)(2,1)} %turned.1.cot, bf16[4,9,128,256]{3,2,1,0:T(8,128)(2,1)} %bitcast.42), custom_call_target="tpu_custom_call" | custom-call | flops 2415919104 | bytes 3538944 | tf_op jit(solution)/shard_map/input_gradient/pallas_call | solution.py:342
  158.0 1.5 collective-permute-start.17
  159.5 10.6 %weight_gradient.1 = f32[3,384,256]{2,1,0:T(8,128)} custom-call(s32[8]{0:T(128)} %concatenate.6.at, bf16[66,128,128]{2,1,0:T(8,128)(2,1)} %copy-done.1, bf16[8,128,256]{2,1,0:T(8,128)(2,1)} %bitcast.6.refs_0_, bf16[8,128,256]{2,1,0:T(8,128)(2,1)} %get-tuple-element.52.refs_1_, bf16[8,128,256]{2,1,0:T(8,128)(2,1)} %get-tuple-element.51.refs_2_, ...), custom_call_target="tpu_custom_call" | custom-call | flops 4831838208 | bytes 6291456 | tf_op jit(solution)/shard_map/weight_gradient/pallas_call | solution.py:212
  170.2 1.8 collective-permute-done.17
  172.9 1.0 fusion.1
  (61 shorter events, 8.6 us)
Async XLA Ops:
  7.2 105.3 %all-gather.3.cloned.1.call-start = ((), (), s32[]{:S(2)}) async-start(), calls=%async_computation.1 | async-start | bytes 2949120 | tf_op jit(solution)/shard_map/all_gather | solution.py:429
  7.2 15.1 %collective-permute-start.4 = (bf16[16,128,128]{2,1,0:T(8,128)(2,1)}, bf16[16,128,128]{2,1,0:T(8,128)(2,1)S(1)}, u32[]{:S(2)}, u32[]{:S(2)}) collective-permute-start(bf16[16,128,128]{2,1,0:T(8,128)(2,1)} %bitcast.39), channel_id=1, source_target_pairs={{0,16},{8,24},{16,0},{24,8},{1,17},{9,25},{17,1},{25,9},{2,18},{10... | collective-permute-start | bytes 1572872 | tf_op jit(solution)/shard_map/ppermute | solution.py:366
  10.2 13.6 %collective-permute-start.3 = (bf16[8,128,256]{2,1,0:T(8,128)(2,1)}, bf16[8,128,256]{2,1,0:T(8,128)(2,1)S(1)}, u32[]{:S(2)}, u32[]{:S(2)}) collective-permute-start(bf16[8,128,256]{2,1,0:T(8,128)(2,1)} %bitcast.6.refs_0_), channel_id=1, source_target_pairs={{0,1},{1,0},{2,3},{3,2},{4,5},{5,4},{6,7},{7,6},{8,9},{9,8},{10,11... | collective-permute-start | bytes 1572872 | tf_op jit(solution)/shard_map/ppermute | solution.py:393
  11.7 15.2 %collective-permute-start.1 = (bf16[8,128,256]{2,1,0:T(8,128)(2,1)}, bf16[8,128,256]{2,1,0:T(8,128)(2,1)S(1)}, u32[]{:S(2)}, u32[]{:S(2)}) collective-permute-start(bf16[8,128,256]{2,1,0:T(8,128)(2,1)} %bitcast.6.refs_0_), channel_id=1, source_target_pairs={{2,0},{3,1},{4,2},{5,3},{6,4},{7,5},{10,8},{11,9},{12,10},{13,11},... | collective-permute-start | bytes 1572872 | tf_op jit(solution)/shard_map/ppermute | solution.py:379
  13.0 15.2 %collective-permute-start = (bf16[8,128,256]{2,1,0:T(8,128)(2,1)}, bf16[8,128,256]{2,1,0:T(8,128)(2,1)S(1)}, u32[]{:S(2)}, u32[]{:S(2)}) collective-permute-start(bf16[8,128,256]{2,1,0:T(8,128)(2,1)} %bitcast.6.refs_0_), channel_id=1, source_target_pairs={{0,2},{1,3},{2,4},{3,5},{4,6},{5,7},{8,10},{9,11},{10,12},{11,13},... | collective-permute-start | bytes 1572872 | tf_op jit(solution)/shard_map/ppermute | solution.py:378
  23.8 4.4 %copy-start.11 = (bf16[8,128,256]{2,1,0:T(8,128)(2,1)}, bf16[8,128,256]{2,1,0:T(8,128)(2,1)S(1)}, u32[]{:S(2)}) copy-start(bf16[8,128,256]{2,1,0:T(8,128)(2,1)S(1)} %collective-permute-done.3.refs_4_) | copy-start | bytes 1572868
  29.0 7.1 %collective-permute-start.5 = (bf16[2,16,128,128]{3,2,1,0:T(8,128)(2,1)S(1)}, bf16[2,16,128,128]{3,2,1,0:T(8,128)(2,1)}, u32[]{:S(2)}, u32[]{:S(2)}) collective-permute-start(bf16[2,16,128,128]{3,2,1,0:T(8,128)(2,1)S(1)} %pad_maximum_fusion.1), channel_id=1, source_target_pairs={{0,8},{8,0},{16,24},{24,16},{1,9},{9,1},{17,25},{25,17},{2,10},{10... | collective-permute-start | bytes 3145736 | tf_op jit(solution)/shard_map/ppermute | solution.py:388
  29.0 28.5 %collective-permute-start.2 = (bf16[8,128,256]{2,1,0:T(8,128)(2,1)}, bf16[8,128,256]{2,1,0:T(8,128)(2,1)}, u32[]{:S(2)}, u32[]{:S(2)}) collective-permute-start(bf16[8,128,256]{2,1,0:T(8,128)(2,1)} %bitcast.6.refs_0_), channel_id=1, source_target_pairs={{0,6},{1,7},{6,0},{7,1},{8,14},{9,15},{14,8},{15,9},{16,22},{17,23... | collective-permute-start | bytes 1572872 | tf_op jit(solution)/shard_map/ppermute | solution.py:383
  38.5 29.8 %copy-start.1 = (bf16[66,128,128]{2,1,0:T(8,128)(2,1)}, bf16[66,128,128]{2,1,0:T(8,128)(2,1)S(1)}, u32[]{:S(2)}) copy-start(bf16[66,128,128]{2,1,0:T(8,128)(2,1)S(1)} %fusion.2.cot) | copy-start | bytes 6488068
  57.5 38.2 %all-to-all-start = ((bf16[4,18,32,128]{3,2,1,0:T(8,128)(2,1)}), bf16[4,18,32,128]{3,2,1,0:T(8,128)(2,1)S(1)}, u32[]{:S(2)}, u32[]{:S(2)}) async-start(bf16[4,18,32,128]{3,2,1,0:T(8,128)(2,1)} %pad_maximum_fusion.2), calls=%async_computation | async-start | bytes 1179648 | tf_op jit(solution)/shard_map/all_to_all | solution.py:426
  63.1 32.7 %collective-permute-start.6 = (bf16[8,128,256]{2,1,0:T(8,128)(2,1)}, bf16[8,128,256]{2,1,0:T(8,128)(2,1)}, u32[]{:S(2)}, u32[]{:S(2)}) collective-permute-start(bf16[8,128,256]{2,1,0:T(8,128)(2,1)} %copy-done.9), channel_id=1, source_target_pairs={{2,4},{3,5},{4,6},{5,7},{10,12},{11,13},{12,14},{13,15},{18,20},{1... | collective-permute-start | bytes 1572872 | tf_op jit(solution)/shard_map/ppermute | solution.py:378
  64.5 42.4 %collective-permute-start.7 = (bf16[8,128,256]{2,1,0:T(8,128)(2,1)}, bf16[8,128,256]{2,1,0:T(8,128)(2,1)}, u32[]{:S(2)}, u32[]{:S(2)}) collective-permute-start(bf16[8,128,256]{2,1,0:T(8,128)(2,1)} %copy-done.8), channel_id=1, source_target_pairs={{2,0},{3,1},{4,2},{5,3},{10,8},{11,9},{12,10},{13,11},{18,16},{19,... | collective-permute-start | bytes 1572872 | tf_op jit(solution)/shard_map/ppermute | solution.py:379
  68.3 38.6 %collective-permute-start.9 = (bf16[8,128,256]{2,1,0:T(8,128)(2,1)}, bf16[8,128,256]{2,1,0:T(8,128)(2,1)S(1)}, u32[]{:S(2)}, u32[]{:S(2)}) collective-permute-start(bf16[8,128,256]{2,1,0:T(8,128)(2,1)} %get-tuple-element.51.refs_2_), channel_id=1, source_target_pairs={{0,1},{1,0},{2,3},{3,2},{4,5},{5,4},{6,7},{7,6},{8,9},{9,8},{10,11... | collective-permute-start | bytes 1572872 | tf_op jit(solution)/shard_map/ppermute | solution.py:393
  68.3 39.5 %collective-permute-start.8 = (bf16[8,128,256]{2,1,0:T(8,128)(2,1)}, bf16[8,128,256]{2,1,0:T(8,128)(2,1)S(1)}, u32[]{:S(2)}, u32[]{:S(2)}) collective-permute-start(bf16[8,128,256]{2,1,0:T(8,128)(2,1)} %get-tuple-element.52.refs_1_), channel_id=1, source_target_pairs={{0,1},{1,0},{2,3},{3,2},{4,5},{5,4},{6,7},{7,6},{8,9},{9,8},{10,11... | collective-permute-start | bytes 1572872 | tf_op jit(solution)/shard_map/ppermute | solution.py:393
  95.7 14.1 %copy-start.2 = (bf16[4,18,32,128]{3,2,1,0:T(8,128)(2,1)}, bf16[4,18,32,128]{3,2,1,0:T(8,128)(2,1)S(1)}, u32[]{:S(2)}) copy-start(bf16[4,18,32,128]{3,2,1,0:T(8,128)(2,1)S(1)} %all-to-all-done) | copy-start | bytes 1769476
  95.7 14.0 %collective-permute-start.13 = (bf16[4,18,32,128]{3,2,1,0:T(8,128)(2,1)S(1)}, bf16[4,18,32,128]{3,2,1,0:T(8,128)(2,1)S(1)}, u32[]{:S(2)}, u32[]{:S(2)}) collective-permute-start(bf16[4,18,32,128]{3,2,1,0:T(8,128)(2,1)S(1)} %all-to-all-done), channel_id=1, source_target_pairs={{0,16},{8,24},{16,0},{24,8},{1,17},{9,25},{17,1},{25,9},{2,18},{10... | collective-permute-start | bytes 1769480 | tf_op jit(solution)/shard_map/ppermute | solution.py:366
  106.9 0.8 copy-start.12
  107.7 2.0 %copy-start.13 = (bf16[8,128,256]{2,1,0:T(8,128)(2,1)}, bf16[8,128,256]{2,1,0:T(8,128)(2,1)S(1)}, u32[]{:S(2)}) copy-start(bf16[8,128,256]{2,1,0:T(8,128)(2,1)S(1)} %collective-permute-done.8.refs_5_) | copy-start | bytes 1572868
  109.2 13.6 %copy-start.10 = (bf16[8,128,256]{2,1,0:T(8,128)(2,1)}, bf16[8,128,256]{2,1,0:T(8,128)(2,1)S(1)}, u32[]{:S(2)}) copy-start(bf16[8,128,256]{2,1,0:T(8,128)(2,1)S(1)} %select_select_fusion.refs_3_) | copy-start | bytes 1572868
  109.2 13.6 %collective-permute-start.10 = (bf16[8,128,256]{2,1,0:T(8,128)(2,1)S(1)}, bf16[8,128,256]{2,1,0:T(8,128)(2,1)}, u32[]{:S(2)}, u32[]{:S(2)}) collective-permute-start(bf16[8,128,256]{2,1,0:T(8,128)(2,1)S(1)} %select_select_fusion.refs_3_), channel_id=1, source_target_pairs={{0,1},{1,0},{2,3},{3,2},{4,5},{5,4},{6,7},{7,6},{8,9},{9,8},{10,11... | collective-permute-start | bytes 1572872 | tf_op jit(solution)/shard_map/ppermute | solution.py:393
  111.0 18.9 %copy-start = (bf16[2,4,18,32,128]{4,3,2,1,0:T(8,128)(2,1)}, bf16[2,4,18,32,128]{4,3,2,1,0:T(8,128)(2,1)S(1)}, u32[]{:S(2)}) copy-start(bf16[2,4,18,32,128]{4,3,2,1,0:T(8,128)(2,1)S(1)} %pad_maximum_fusion.same) | copy-start | bytes 3538948
  111.0 19.0 %collective-permute-start.14 = (bf16[2,4,18,32,128]{4,3,2,1,0:T(8,128)(2,1)S(1)}, bf16[2,4,18,32,128]{4,3,2,1,0:T(8,128)(2,1)S(1)}, u32[]{:S(2)}, u32[]{:S(2)}) collective-permute-start(bf16[2,4,18,32,128]{4,3,2,1,0:T(8,128)(2,1)S(1)} %pad_maximum_fusion.same), channel_id=1, source_target_pairs={{0,8},{8,0},{16,24},{24,16},{1,9},{9,1},{17,25},{25,17},{2,10},{10... | collective-permute-start | bytes 3538952 | tf_op jit(solution)/shard_map/ppermute | solution.py:388
  129.9 13.3 %collective-permute-start.11 = (f32[16,128,128]{2,1,0:T(8,128)}, f32[16,128,128]{2,1,0:T(8,128)S(1)}, u32[]{:S(2)}, u32[]{:S(2)}) collective-permute-start(f32[16,128,128]{2,1,0:T(8,128)} %get-tuple-element.34), channel_id=1, source_target_pairs={{0,8},{8,0},{16,24},{24,16},{1,9},{9,1},{17,25},{25,17},{2,10},{10... | collective-permute-start | bytes 3145736 | tf_op jit(solution)/shard_map/ppermute | solution.py:388
  130.0 1.1 copy-start.3
  135.5 7.7 %copy-start.5 = (f32[16,128,128]{2,1,0:T(8,128)S(1)}, f32[16,128,128]{2,1,0:T(8,128)}, u32[]{:S(2)}) copy-start(f32[16,128,128]{2,1,0:T(8,128)} %get-tuple-element.33) | copy-start | bytes 3145732
  142.5 27.6 %collective-permute-start.16 = (f32[8,128,128]{2,1,0:T(8,128)}, f32[8,128,128]{2,1,0:T(8,128)S(1)}, u32[]{:S(2)}, u32[]{:S(2)}) collective-permute-start(f32[8,128,128]{2,1,0:T(8,128)} %get-tuple-element.37), channel_id=1, source_target_pairs={{0,1},{1,0},{2,3},{3,2},{4,5},{5,4},{6,7},{7,6},{8,9},{9,8},{10,11... | collective-permute-start | bytes 1572872 | tf_op jit(solution)/shard_map/ppermute | solution.py:393
  143.4 29.6 %collective-permute-start.12 = (f32[16,128,128]{2,1,0:T(8,128)S(1)}, f32[16,128,128]{2,1,0:T(8,128)S(1)}, u32[]{:S(2)}, u32[]{:S(2)}) collective-permute-start(f32[16,128,128]{2,1,0:T(8,128)S(1)} %add.101), channel_id=1, source_target_pairs={{0,16},{8,24},{16,0},{24,8},{1,17},{9,25},{17,1},{25,9},{2,18},{10... | collective-permute-start | bytes 3145736 | tf_op jit(solution)/shard_map/ppermute | solution.py:475
  157.9 12.2 %copy-start.6 = (f32[8,128,128]{2,1,0:T(8,128)S(1)}, f32[8,128,128]{2,1,0:T(8,128)}, u32[]{:S(2)}) copy-start(f32[8,128,128]{2,1,0:T(8,128)} %get-tuple-element.42) | copy-start | bytes 1572868
  157.9 14.0 %copy-start.7 = (f32[8,128,128]{2,1,0:T(8,128)S(1)}, f32[8,128,128]{2,1,0:T(8,128)}, u32[]{:S(2)}) copy-start(f32[8,128,128]{2,1,0:T(8,128)} %get-tuple-element.44) | copy-start | bytes 1572868
  158.0 14.0 %collective-permute-start.17 = (f32[8,128,128]{2,1,0:T(8,128)}, f32[8,128,128]{2,1,0:T(8,128)S(1)}, u32[]{:S(2)}, u32[]{:S(2)}) collective-permute-start(f32[8,128,128]{2,1,0:T(8,128)} %get-tuple-element.45), channel_id=1, source_target_pairs={{0,1},{1,0},{2,3},{3,2},{4,5},{5,4},{6,7},{7,6},{8,9},{9,8},{10,11... | collective-permute-start | bytes 1572872 | tf_op jit(solution)/shard_map/ppermute | solution.py:393
  159.5 13.5 %collective-permute-start.15 = (f32[16,128,128]{2,1,0:T(8,128)}, f32[16,128,128]{2,1,0:T(8,128)S(1)}, u32[]{:S(2)}, u32[]{:S(2)}) collective-permute-start(f32[16,128,128]{2,1,0:T(8,128)} %get-tuple-element.41), channel_id=1, source_target_pairs={{0,8},{8,0},{16,24},{24,16},{1,9},{9,1},{17,25},{25,17},{2,10},{10... | collective-permute-start | bytes 3145736 | tf_op jit(solution)/shard_map/ppermute | solution.py:388
  170.1 2.8 %copy-start.4 = (f32[16,128,128]{2,1,0:T(8,128)S(1)}, f32[16,128,128]{2,1,0:T(8,128)}, u32[]{:S(2)}) copy-start(f32[16,128,128]{2,1,0:T(8,128)} %get-tuple-element.40) | copy-start | bytes 3145732
  (2 other events, 1.6 us)
Sparse Core Ops, SparseCore 0:
  29.2 74.3 all-gather.2

commit v4 on v2

--- a/solution.py
+++ b/solution.py
@@ -441,8 +441,6 @@
         if stage == 2:
             padded = all_rows(ready[-1])
             pieces = line_pieces(padded)
-        elif stage == 3:
-            pieces = exchange(ready[-1])
         fresh = []
         if stage < stages:
             along = line_step(along, stage, depth)
@@ -451,8 +449,7 @@
             theirs.append(pair_swap(mine[-1], depth))
             fresh.append(theirs[-1])
         fresh.append(pieces)
-    if stages < 3:
-        pieces = exchange(pieces)
+    pieces = exchange(pieces)
     same = fars_gather(pieces, chans)
     sources = turned(same, core_swap(same, chans))
 

time: 172 us -> 163 us (0.948)
  waiting for transfers between devices: 65.9 us -> 55.6 us
    all_to_all x1, waiting for transfers between devices: 11 us -> 3.93 us  [exchange(): lax.all_to_all(pieces, 'filt', 0, 0, axis_index_groups=lines(depth), tile...]
    ppermute x2, waiting for transfers between devices: 7.05 us -> 2.65 us  [fars_gather(): lax.ppermute(value, 'chan', [(c, (c + 2 * step) % chans) for c in range(c...]
    ppermute x6, waiting for transfers between devices: 0.02 us -> 4.2 us  [pair_swap(): return lax.ppermute(value, 'filt', pairs)]
    ppermute x2, waiting for transfers between devices: 30.6 us -> 26.4 us  [line_step(): along[step] = lax.ppermute(along[step - 1], 'filt', down)]
  transfers between devices with their start and end apart: 21 -> 21, of which waited for: 7 -> 9; matrix products, arithmetic and copies ran while one was open for 8% -> 9% of each run, Pallas kernels for 25% -> 27%
where the time goes in v4:
time: 163 us; the launch traced here: 162 us
  waiting for transfers between devices  55.6 us (34%)
  Pallas kernels  43.2 us (27%)
  starting transfers between devices  31.5 us (19%)
  between operations  14.4 us (9%)
  other arithmetic  10.9 us (7%)
  local copies, waits for them, and re-layouts  6.4 us (4%)
    ppermute x2, waiting for transfers between devices, line_step(): along[step] = lax.ppermute(along[step - 1], 'filt', down)  26.4 us
    pallas_call x2, Pallas kernels, forward_partial(): pl.pallas_call(functools.partial(forward_kernel, depth, chans, which), ou...  14.3 us
    pallas_call x2, Pallas kernels, input_partial(): pl.pallas_call(functools.partial(input_kernel, chans), out_shape=(half, h...  13.7 us
    ppermute x1, waiting for transfers between devices, line_step(): along[depth - 1] = along[1 - depth] = lax.ppermute(along[0], 'filt', across)  11.8 us
    pallas_call x1, Pallas kernels, weight_gradient(): pl.pallas_call(functools.partial(weight_kernel, depth, scale), out_shape=...  10.8 us
    ppermute x6, starting transfers between devices, pair_swap(): return lax.ppermute(value, 'filt', pairs)  8.37 us
    ppermute x1, starting transfers between devices, line_step(): along[depth - 1] = along[1 - depth] = lax.ppermute(along[0], 'filt', across)  6.56 us
    ppermute x2, starting transfers between devices, line_step(): along[-step] = lax.ppermute(along[1 - step], 'filt', up)  5.76 us
  transfers between devices with their start and end apart: 21, of which 9 were waited for; matrix products, arithmetic and copies ran while one was open for 9% of the time, Pallas kernels for 27%

profile of v4, /device:TPU:0, one launch (start us, length us, event | category | flops | bytes accessed | tf_op | source)
XLA Modules:
  0.0 162.1 jit_solution(13057109727544532350)
XLA Ops:
  7.2 3.0 %collective-permute-start.4 = (bf16[16,128,128]{2,1,0:T(8,128)(2,1)}, bf16[16,128,128]{2,1,0:T(8,128)(2,1)S(1)}, u32[]{:S(2)}, u32[]{:S(2)}) collective-permute-start(bf16[16,128,128]{2,1,0:T(8,128)(2,1)} %bitcast.42), channel_id=1, source_target_pairs={{0,16},{8,24},{16,0},{24,8},{1,17},{9,25},{17,1},{25,9},{2,18},{10... | collective-permute-start | bytes 1572872 | tf_op jit(solution)/shard_map/ppermute | solution.py:364
  10.2 4.3 %collective-permute-start = (bf16[8,128,256]{2,1,0:T(8,128)(2,1)}, bf16[8,128,256]{2,1,0:T(8,128)(2,1)}, u32[]{:S(2)}, u32[]{:S(2)}) collective-permute-start(bf16[8,128,256]{2,1,0:T(8,128)(2,1)} %bitcast.44), channel_id=1, source_target_pairs={{0,2},{1,3},{2,4},{3,5},{4,6},{5,7},{8,10},{9,11},{10,12},{11,13},... | collective-permute-start | bytes 1572872 | tf_op jit(solution)/shard_map/ppermute | solution.py:376
  14.5 1.3 collective-permute-start.1
  15.8 6.6 %collective-permute-start.2 = (bf16[8,128,256]{2,1,0:T(8,128)(2,1)}, bf16[8,128,256]{2,1,0:T(8,128)(2,1)S(1)}, u32[]{:S(2)}, u32[]{:S(2)}) collective-permute-start(bf16[8,128,256]{2,1,0:T(8,128)(2,1)} %bitcast.46), channel_id=1, source_target_pairs={{0,6},{1,7},{6,0},{7,1},{8,14},{9,15},{14,8},{15,9},{16,22},{17,23... | collective-permute-start | bytes 1572872 | tf_op jit(solution)/shard_map/ppermute | solution.py:381
  22.4 1.6 collective-permute-start.3
  24.0 1.1 pad_maximum_fusion.1
  25.1 1.3 collective-permute-done
  26.4 4.0 %collective-permute-done.1 = bf16[8,128,256]{2,1,0:T(8,128)(2,1)} collective-permute-done((bf16[8,128,256]{2,1,0:T(8,128)(2,1)}, bf16[8,128,256]{2,1,0:T(8,128)(2,1)}, u32[]{:S(2)}, u32[]{:S(2)}) %collective-permute-start.1) | collective-permute-done | bytes 524320 | tf_op jit(solution)/shard_map/ppermute | solution.py:377
  30.3 11.8 %collective-permute-done.2 = bf16[8,128,256]{2,1,0:T(8,128)(2,1)S(1)} collective-permute-done((bf16[8,128,256]{2,1,0:T(8,128)(2,1)}, bf16[8,128,256]{2,1,0:T(8,128)(2,1)S(1)}, u32[]{:S(2)}, u32[]{:S(2)}) %collective-permute-start.2) | collective-permute-done | bytes 524320 | tf_op jit(solution)/shard_map/ppermute | solution.py:381
  43.3 1.5 collective-permute-start.6
  44.8 1.3 collective-permute-start.7
  46.1 2.3 %fusion = (bf16[8,128,256]{2,1,0:T(8,128)(2,1)}, bf16[8,128,256]{2,1,0:T(8,128)(2,1)}) fusion(bf16[8,128,256]{2,1,0:T(8,128)(2,1)S(1)} %collective-permute-done.2, bf16[8,128,256]{2,1,0:T(8,128)(2,1)} %collective-permute-done.1, pred[]{:T(512)S(6)} %eq.19, pred[]{:T(512)S(6)} %eq.18, pred[]{:T(512)S(6)} %eq.9, bf16[8,128,256]{2,1,0:T(8,128)(2,1)} %collective-permute-done), kind=kLoop, calls=%fused_computation.7 | loop fusion | flops 1572864 | bytes 2621443 | tf_op jit(solution)/shard_map/jit(_where)/select_n | solution.py:50
  48.4 1.5 collective-permute-start.8
  52.3 1.1 fusion.2.cot
  54.5 3.9 %all-to-all-start = ((bf16[4,18,32,128]{3,2,1,0:T(8,128)(2,1)}), bf16[4,18,32,128]{3,2,1,0:T(8,128)(2,1)S(1)}, u32[]{:S(2)}, u32[]{:S(2)}) async-start(bf16[4,18,32,128]{3,2,1,0:T(8,128)(2,1)} %pad_maximum_fusion.2), calls=%async_computation | async-start | bytes 1179648 | tf_op jit(solution)/shard_map/all_to_all | solution.py:424
  58.4 22.5 %collective-permute-done.7 = bf16[8,128,256]{2,1,0:T(8,128)(2,1)} collective-permute-done((bf16[8,128,256]{2,1,0:T(8,128)(2,1)}, bf16[8,128,256]{2,1,0:T(8,128)(2,1)}, u32[]{:S(2)}, u32[]{:S(2)}) %collective-permute-start.7) | collective-permute-done | bytes 524320 | tf_op jit(solution)/shard_map/ppermute | solution.py:377
  80.9 2.1 %select_select_fusion.refs_3_ = bf16[8,128,256]{2,1,0:T(8,128)(2,1)} fusion(bf16[8,128,256]{2,1,0:T(8,128)(2,1)} %collective-permute-done.6, bf16[8,128,256]{2,1,0:T(8,128)(2,1)} %collective-permute-done.7, pred[]{:T(512)S(6)} %eq.18, pred[]{:T(512)S(6)} %eq.9), kind=kLoop, calls=%fused_computation.3 | loop fusion | flops 524288 | bytes 1572866 | tf_op jit(solution)/shard_map/jit(_where)/select_n | solution.py:50
  83.0 1.5 collective-permute-start.10
  85.8 1.5 all-gather.3.cloned.1.call-done.kernels
  87.3 3.9 %all-to-all-done = bf16[4,18,32,128]{3,2,1,0:T(8,128)(2,1)S(1)} async-done(((bf16[4,18,32,128]{3,2,1,0:T(8,128)(2,1)}), bf16[4,18,32,128]{3,2,1,0:T(8,128)(2,1)S(1)}, u32[]{:S(2)}, u32[]{:S(2)}) %all-to-all-start) | async-done | bytes 589856 | tf_op jit(solution)/shard_map/all_to_all | solution.py:424
  91.8 4.2 %collective-permute-done.10.refs_7_ = bf16[8,128,256]{2,1,0:T(8,128)(2,1)} collective-permute-done((bf16[8,128,256]{2,1,0:T(8,128)(2,1)}, bf16[8,128,256]{2,1,0:T(8,128)(2,1)}, u32[]{:S(2)}, u32[]{:S(2)}) %collective-permute-start.10) | collective-permute-done | bytes 524320 | tf_op jit(solution)/shard_map/ppermute | solution.py:391
  96.0 7.1 %forward.2 = (f32[16,128,128]{2,1,0:T(8,128)}, f32[16,128,128]{2,1,0:T(8,128)}) custom-call(s32[8]{0:T(128)} %concatenate.6.at, bf16[3,3,128,256]{3,2,1,0:T(8,128)(2,1)} %weights.3, bf16[8,128,256]{2,1,0:T(8,128)(2,1)} %bitcast.48, bf16[8,128,256]{2,1,0:T(8,128)(2,1)} %get-tuple-element.54.refs_1_, bf16[8,128,256]{2,1,0:T(8,128)(2,1)} %get-tuple-element.53.refs_2_, ...), custom_call_target="tpu_custom_call" | custom-call | flops 2415919104 | bytes 6291456 | tf_op jit(solution)/shard_map/forward/pallas_call | solution.py:136
  103.2 2.6 %collective-permute-done.14 = bf16[4,18,32,128]{3,2,1,0:T(8,128)(2,1)S(1)} collective-permute-done((bf16[4,18,32,128]{3,2,1,0:T(8,128)(2,1)S(1)}, bf16[4,18,32,128]{3,2,1,0:T(8,128)(2,1)S(1)}, u32[]{:S(2)}, u32[]{:S(2)}) %collective-permute-start.14) | collective-permute-done | bytes 589856 | tf_op jit(solution)/shard_map/ppermute | solution.py:364
  106.1 1.3 add.101
  107.9 7.2 %forward.3 = (f32[16,128,128]{2,1,0:T(8,128)}, f32[16,128,128]{2,1,0:T(8,128)}) custom-call(s32[8]{0:T(128)} %concatenate.6.at, bf16[3,3,128,256]{3,2,1,0:T(8,128)(2,1)} %weights.3, bf16[8,128,256]{2,1,0:T(8,128)(2,1)} %bitcast.49, bf16[8,128,256]{2,1,0:T(8,128)(2,1)} %get-tuple-element.54.refs_1_, bf16[8,128,256]{2,1,0:T(8,128)(2,1)} %get-tuple-element.53.refs_2_, ...), custom_call_target="tpu_custom_call" | custom-call | flops 2415919104 | bytes 6291456 | tf_op jit(solution)/shard_map/forward/pallas_call | solution.py:136
  116.3 4.4 %turned.1.cot = bf16[4,18,128,128]{3,2,1,0:T(8,128)(2,1)} custom-call(bf16[2,4,18,32,128]{4,3,2,1,0:T(8,128)(2,1)} %copy-done, bf16[2,4,18,32,128]{4,3,2,1,0:T(8,128)(2,1)} %copy-done.2), custom_call_target="tpu_custom_call" | custom-call | bytes 4718592 | tf_op jit(solution)/shard_map/turned/pallas_call | solution.py:246
  120.7 6.9 %input_gradient.2 = (f32[8,128,128]{2,1,0:T(8,128)}, f32[8,128,128]{2,1,0:T(8,128)}) custom-call(s32[8]{0:T(128)} %concatenate.6.at, bf16[4,18,128,128]{3,2,1,0:T(8,128)(2,1)} %turned.1.cot, bf16[4,9,128,128]{3,2,1,0:T(8,128)(2,1)} %all-gather.3.cloned.1.call-done.kernels), custom_call_target="tpu_custom_call" | custom-call | flops 2415919104 | bytes 3538944 | tf_op jit(solution)/shard_map/input_gradient/pallas_call | solution.py:340
  127.5 1.6 %collective-permute-start.16 = (f32[8,128,128]{2,1,0:T(8,128)}, f32[8,128,128]{2,1,0:T(8,128)}, u32[]{:S(2)}, u32[]{:S(2)}) collective-permute-start(f32[8,128,128]{2,1,0:T(8,128)} %get-tuple-element.41), channel_id=1, source_target_pairs={{0,1},{1,0},{2,3},{3,2},{4,5},{5,4},{6,7},{7,6},{8,9},{9,8},{10,11... | collective-permute-start | bytes 1572872 | tf_op jit(solution)/shard_map/ppermute | solution.py:391
  129.2 3.7 %collective-permute-done.12 = f32[16,128,128]{2,1,0:T(8,128)S(1)} collective-permute-done((f32[16,128,128]{2,1,0:T(8,128)}, f32[16,128,128]{2,1,0:T(8,128)S(1)}, u32[]{:S(2)}, u32[]{:S(2)}) %collective-permute-start.12) | collective-permute-done | bytes 1048608 | tf_op jit(solution)/shard_map/ppermute | solution.py:468
  132.9 6.9 %input_gradient.3 = (f32[8,128,128]{2,1,0:T(8,128)}, f32[8,128,128]{2,1,0:T(8,128)}) custom-call(s32[8]{0:T(128)} %concatenate.6.at, bf16[4,18,128,128]{3,2,1,0:T(8,128)(2,1)} %turned.1.cot, bf16[4,9,128,128]{3,2,1,0:T(8,128)(2,1)} %all-gather.5.cloned.1.call-done.kernels), custom_call_target="tpu_custom_call" | custom-call | flops 2415919104 | bytes 3538944 | tf_op jit(solution)/shard_map/input_gradient/pallas_call | solution.py:340
  139.8 1.6 collective-permute-start.17
  143.5 10.8 %weight_gradient.1 = f32[3,384,256]{2,1,0:T(8,128)} custom-call(s32[8]{0:T(128)} %concatenate.6.at, bf16[66,128,128]{2,1,0:T(8,128)(2,1)} %copy-done.1, bf16[8,128,256]{2,1,0:T(8,128)(2,1)} %bitcast.50, bf16[8,128,256]{2,1,0:T(8,128)(2,1)} %get-tuple-element.54.refs_1_, bf16[8,128,256]{2,1,0:T(8,128)(2,1)} %get-tuple-element.53.refs_2_, ...), custom_call_target="tpu_custom_call" | custom-call | flops 4831838208 | bytes 6291456 | tf_op jit(solution)/shard_map/weight_gradient/pallas_call | solution.py:212
  (55 shorter events, 11.4 us)
Async XLA Ops:
  7.2 35.0 %copy-start.5 = (bf16[3,3,128,256]{3,2,1,0:T(8,128)(2,1)S(1)}, bf16[3,3,128,256]{3,2,1,0:T(8,128)(2,1)}, u32[]{:S(2)}) copy-start(bf16[3,3,128,256]{3,2,1,0:T(8,128)(2,1)} %weights.3) | copy-start | bytes 1769476
  7.2 80.2 %all-gather.3.cloned.1.call-start = ((), (), s32[]{:S(2)}) async-start(), calls=%async_computation.1 | async-start | bytes 1474560 | tf_op jit(solution)/shard_map/all_gather | solution.py:430
  7.2 16.7 %collective-permute-start.4 = (bf16[16,128,128]{2,1,0:T(8,128)(2,1)}, bf16[16,128,128]{2,1,0:T(8,128)(2,1)S(1)}, u32[]{:S(2)}, u32[]{:S(2)}) collective-permute-start(bf16[16,128,128]{2,1,0:T(8,128)(2,1)} %bitcast.42), channel_id=1, source_target_pairs={{0,16},{8,24},{16,0},{24,8},{1,17},{9,25},{17,1},{25,9},{2,18},{10... | collective-permute-start | bytes 1572872 | tf_op jit(solution)/shard_map/ppermute | solution.py:364
  10.2 16.1 %collective-permute-start = (bf16[8,128,256]{2,1,0:T(8,128)(2,1)}, bf16[8,128,256]{2,1,0:T(8,128)(2,1)}, u32[]{:S(2)}, u32[]{:S(2)}) collective-permute-start(bf16[8,128,256]{2,1,0:T(8,128)(2,1)} %bitcast.44), channel_id=1, source_target_pairs={{0,2},{1,3},{2,4},{3,5},{4,6},{5,7},{8,10},{9,11},{10,12},{11,13},... | collective-permute-start | bytes 1572872 | tf_op jit(solution)/shard_map/ppermute | solution.py:376
  14.5 15.8 %collective-permute-start.1 = (bf16[8,128,256]{2,1,0:T(8,128)(2,1)}, bf16[8,128,256]{2,1,0:T(8,128)(2,1)}, u32[]{:S(2)}, u32[]{:S(2)}) collective-permute-start(bf16[8,128,256]{2,1,0:T(8,128)(2,1)} %bitcast.45), channel_id=1, source_target_pairs={{2,0},{3,1},{4,2},{5,3},{6,4},{7,5},{10,8},{11,9},{12,10},{13,11},... | collective-permute-start | bytes 1572872 | tf_op jit(solution)/shard_map/ppermute | solution.py:377
  15.8 26.4 %collective-permute-start.2 = (bf16[8,128,256]{2,1,0:T(8,128)(2,1)}, bf16[8,128,256]{2,1,0:T(8,128)(2,1)S(1)}, u32[]{:S(2)}, u32[]{:S(2)}) collective-permute-start(bf16[8,128,256]{2,1,0:T(8,128)(2,1)} %bitcast.46), channel_id=1, source_target_pairs={{0,6},{1,7},{6,0},{7,1},{8,14},{9,15},{14,8},{15,9},{16,22},{17,23... | collective-permute-start | bytes 1572872 | tf_op jit(solution)/shard_map/ppermute | solution.py:381
  22.4 19.8 %collective-permute-start.3 = (bf16[8,128,256]{2,1,0:T(8,128)(2,1)}, bf16[8,128,256]{2,1,0:T(8,128)(2,1)S(1)}, u32[]{:S(2)}, u32[]{:S(2)}) collective-permute-start(bf16[8,128,256]{2,1,0:T(8,128)(2,1)} %bitcast.47), channel_id=1, source_target_pairs={{0,1},{1,0},{2,3},{3,2},{4,5},{5,4},{6,7},{7,6},{8,9},{9,8},{10,11... | collective-permute-start | bytes 1572872 | tf_op jit(solution)/shard_map/ppermute | solution.py:391
  42.2 1.0 copy-start.8
  42.2 8.8 %collective-permute-start.5 = (bf16[2,16,128,128]{3,2,1,0:T(8,128)(2,1)S(1)}, bf16[2,16,128,128]{3,2,1,0:T(8,128)(2,1)}, u32[]{:S(2)}, u32[]{:S(2)}) collective-permute-start(bf16[2,16,128,128]{3,2,1,0:T(8,128)(2,1)S(1)} %pad_maximum_fusion.1), channel_id=1, source_target_pairs={{0,8},{8,0},{16,24},{24,16},{1,9},{9,1},{17,25},{25,17},{2,10},{10... | collective-permute-start | bytes 3145736 | tf_op jit(solution)/shard_map/ppermute | solution.py:386
  43.3 15.1 %collective-permute-start.6 = (bf16[8,128,256]{2,1,0:T(8,128)(2,1)}, bf16[8,128,256]{2,1,0:T(8,128)(2,1)}, u32[]{:S(2)}, u32[]{:S(2)}) collective-permute-start(bf16[8,128,256]{2,1,0:T(8,128)(2,1)} %collective-permute-done), channel_id=1, source_target_pairs={{2,4},{3,5},{4,6},{5,7},{10,12},{11,13},{12,14},{13,15},{18,20},{1... | collective-permute-start | bytes 1572872 | tf_op jit(solution)/shard_map/ppermute | solution.py:376
  44.8 36.1 %collective-permute-start.7 = (bf16[8,128,256]{2,1,0:T(8,128)(2,1)}, bf16[8,128,256]{2,1,0:T(8,128)(2,1)}, u32[]{:S(2)}, u32[]{:S(2)}) collective-permute-start(bf16[8,128,256]{2,1,0:T(8,128)(2,1)} %collective-permute-done.1), channel_id=1, source_target_pairs={{2,0},{3,1},{4,2},{5,3},{10,8},{11,9},{12,10},{13,11},{18,16},{19,... | collective-permute-start | bytes 1572872 | tf_op jit(solution)/shard_map/ppermute | solution.py:377
  48.4 32.5 %collective-permute-start.8 = (bf16[8,128,256]{2,1,0:T(8,128)(2,1)}, bf16[8,128,256]{2,1,0:T(8,128)(2,1)}, u32[]{:S(2)}, u32[]{:S(2)}) collective-permute-start(bf16[8,128,256]{2,1,0:T(8,128)(2,1)} %get-tuple-element.54.refs_1_), channel_id=1, source_target_pairs={{0,1},{1,0},{2,3},{3,2},{4,5},{5,4},{6,7},{7,6},{8,9},{9,8},{10,11... | collective-permute-start | bytes 1572872 | tf_op jit(solution)/shard_map/ppermute | solution.py:391
  49.9 31.0 %collective-permute-start.9 = (bf16[8,128,256]{2,1,0:T(8,128)(2,1)}, bf16[8,128,256]{2,1,0:T(8,128)(2,1)}, u32[]{:S(2)}, u32[]{:S(2)}) collective-permute-start(bf16[8,128,256]{2,1,0:T(8,128)(2,1)} %get-tuple-element.53.refs_2_), channel_id=1, source_target_pairs={{0,1},{1,0},{2,3},{3,2},{4,5},{5,4},{6,7},{7,6},{8,9},{9,8},{10,11... | collective-permute-start | bytes 1572872 | tf_op jit(solution)/shard_map/ppermute | solution.py:391
  53.4 29.6 %copy-start.1 = (bf16[66,128,128]{2,1,0:T(8,128)(2,1)}, bf16[66,128,128]{2,1,0:T(8,128)(2,1)S(1)}, u32[]{:S(2)}) copy-start(bf16[66,128,128]{2,1,0:T(8,128)(2,1)S(1)} %fusion.2.cot) | copy-start | bytes 6488068
  54.5 36.8 %all-to-all-start = ((bf16[4,18,32,128]{3,2,1,0:T(8,128)(2,1)}), bf16[4,18,32,128]{3,2,1,0:T(8,128)(2,1)S(1)}, u32[]{:S(2)}, u32[]{:S(2)}) async-start(bf16[4,18,32,128]{3,2,1,0:T(8,128)(2,1)} %pad_maximum_fusion.2), calls=%async_computation | async-start | bytes 1179648 | tf_op jit(solution)/shard_map/all_to_all | solution.py:424
  58.4 74.5 %all-gather.5.cloned.1.call-start = ((), (), s32[]{:S(2)}) async-start(), calls=%async_computation.2 | async-start | bytes 1474560 | tf_op jit(solution)/shard_map/all_gather | solution.py:430
  83.0 13.0 %collective-permute-start.10 = (bf16[8,128,256]{2,1,0:T(8,128)(2,1)}, bf16[8,128,256]{2,1,0:T(8,128)(2,1)}, u32[]{:S(2)}, u32[]{:S(2)}) collective-permute-start(bf16[8,128,256]{2,1,0:T(8,128)(2,1)} %select_select_fusion.refs_3_), channel_id=1, source_target_pairs={{0,1},{1,0},{2,3},{3,2},{4,5},{5,4},{6,7},{7,6},{8,9},{9,8},{10,11... | collective-permute-start | bytes 1572872 | tf_op jit(solution)/shard_map/ppermute | solution.py:391
  91.3 14.6 %collective-permute-start.14 = (bf16[4,18,32,128]{3,2,1,0:T(8,128)(2,1)S(1)}, bf16[4,18,32,128]{3,2,1,0:T(8,128)(2,1)S(1)}, u32[]{:S(2)}, u32[]{:S(2)}) collective-permute-start(bf16[4,18,32,128]{3,2,1,0:T(8,128)(2,1)S(1)} %all-to-all-done), channel_id=1, source_target_pairs={{0,16},{8,24},{16,0},{24,8},{1,17},{9,25},{17,1},{25,9},{2,18},{10... | collective-permute-start | bytes 1769480 | tf_op jit(solution)/shard_map/ppermute | solution.py:364
  103.1 3.0 %copy-start.4 = (f32[16,128,128]{2,1,0:T(8,128)S(1)}, f32[16,128,128]{2,1,0:T(8,128)}, u32[]{:S(2)}) copy-start(f32[16,128,128]{2,1,0:T(8,128)} %get-tuple-element.33) | copy-start | bytes 3145732
  103.1 3.0 %collective-permute-start.11 = (f32[16,128,128]{2,1,0:T(8,128)}, f32[16,128,128]{2,1,0:T(8,128)S(1)}, u32[]{:S(2)}, u32[]{:S(2)}) collective-permute-start(f32[16,128,128]{2,1,0:T(8,128)} %get-tuple-element.34), channel_id=1, source_target_pairs={{0,8},{8,0},{16,24},{24,16},{1,9},{9,1},{17,25},{25,17},{2,10},{10... | collective-permute-start | bytes 3145736 | tf_op jit(solution)/shard_map/ppermute | solution.py:386
  106.0 9.1 %copy-start = (bf16[2,4,18,32,128]{4,3,2,1,0:T(8,128)(2,1)}, bf16[2,4,18,32,128]{4,3,2,1,0:T(8,128)(2,1)S(1)}, u32[]{:S(2)}) copy-start(bf16[2,4,18,32,128]{4,3,2,1,0:T(8,128)(2,1)S(1)} %pad_maximum_fusion.same) | copy-start | bytes 3538948
  106.0 9.2 %collective-permute-start.15 = (bf16[2,4,18,32,128]{4,3,2,1,0:T(8,128)(2,1)S(1)}, bf16[2,4,18,32,128]{4,3,2,1,0:T(8,128)(2,1)S(1)}, u32[]{:S(2)}, u32[]{:S(2)}) collective-permute-start(bf16[2,4,18,32,128]{4,3,2,1,0:T(8,128)(2,1)S(1)} %pad_maximum_fusion.same), channel_id=1, source_target_pairs={{0,8},{8,0},{16,24},{24,16},{1,9},{9,1},{17,25},{25,17},{2,10},{10... | collective-permute-start | bytes 3538952 | tf_op jit(solution)/shard_map/ppermute | solution.py:386
  107.3 25.6 %collective-permute-start.12 = (f32[16,128,128]{2,1,0:T(8,128)}, f32[16,128,128]{2,1,0:T(8,128)S(1)}, u32[]{:S(2)}, u32[]{:S(2)}) collective-permute-start(f32[16,128,128]{2,1,0:T(8,128)} %add.101), channel_id=1, source_target_pairs={{0,16},{8,24},{16,0},{24,8},{1,17},{9,25},{17,1},{25,9},{2,18},{10... | collective-permute-start | bytes 3145736 | tf_op jit(solution)/shard_map/ppermute | solution.py:468
  115.1 26.3 %collective-permute-start.13 = (f32[16,128,128]{2,1,0:T(8,128)}, f32[16,128,128]{2,1,0:T(8,128)S(1)}, u32[]{:S(2)}, u32[]{:S(2)}) collective-permute-start(f32[16,128,128]{2,1,0:T(8,128)} %get-tuple-element.38), channel_id=1, source_target_pairs={{0,8},{8,0},{16,24},{24,16},{1,9},{9,1},{17,25},{25,17},{2,10},{10... | collective-permute-start | bytes 3145736 | tf_op jit(solution)/shard_map/ppermute | solution.py:386
  115.2 1.1 copy-start.2
  127.5 13.9 %copy-start.3 = (f32[16,128,128]{2,1,0:T(8,128)S(1)}, f32[16,128,128]{2,1,0:T(8,128)}, u32[]{:S(2)}) copy-start(f32[16,128,128]{2,1,0:T(8,128)} %get-tuple-element.37) | copy-start | bytes 3145732
  127.5 14.9 %collective-permute-start.16 = (f32[8,128,128]{2,1,0:T(8,128)}, f32[8,128,128]{2,1,0:T(8,128)}, u32[]{:S(2)}, u32[]{:S(2)}) collective-permute-start(f32[8,128,128]{2,1,0:T(8,128)} %get-tuple-element.41), channel_id=1, source_target_pairs={{0,1},{1,0},{2,3},{3,2},{4,5},{5,4},{6,7},{7,6},{8,9},{9,8},{10,11... | collective-permute-start | bytes 1572872 | tf_op jit(solution)/shard_map/ppermute | solution.py:391
  139.8 2.6 %copy-start.7 = (f32[8,128,128]{2,1,0:T(8,128)S(1)}, f32[8,128,128]{2,1,0:T(8,128)}, u32[]{:S(2)}) copy-start(f32[8,128,128]{2,1,0:T(8,128)} %get-tuple-element.40) | copy-start | bytes 1572868
  139.8 14.5 %collective-permute-start.17 = (f32[8,128,128]{2,1,0:T(8,128)}, f32[8,128,128]{2,1,0:T(8,128)S(1)}, u32[]{:S(2)}, u32[]{:S(2)}) collective-permute-start(f32[8,128,128]{2,1,0:T(8,128)} %get-tuple-element.44), channel_id=1, source_target_pairs={{0,1},{1,0},{2,3},{3,2},{4,5},{5,4},{6,7},{7,6},{8,9},{9,8},{10,11... | collective-permute-start | bytes 1572872 | tf_op jit(solution)/shard_map/ppermute | solution.py:391
  143.5 10.8 %copy-start.6 = (f32[8,128,128]{2,1,0:T(8,128)S(1)}, f32[8,128,128]{2,1,0:T(8,128)}, u32[]{:S(2)}) copy-start(f32[8,128,128]{2,1,0:T(8,128)} %get-tuple-element.43) | copy-start | bytes 1572868
Sparse Core Ops, SparseCore 0:
  43.3 43.9 all-gather.2
  103.3 29.1 all-gather.4

commit v5 on v4

--- a/solution.py
+++ b/solution.py
@@ -102,7 +102,7 @@
         def _():
             wait(first + spot)
 
-    group = min(4, block)
+    group = min(8, block)
 
     def result(step, place):
         chosen = pl.ds(step * group, group)
@@ -144,7 +144,7 @@
             pltpu.VMEM((2, rows // chans, filters, width), F32),
             pltpu.SemaphoreType.DMA((depth * PAIR,)),
             pltpu.SemaphoreType.DMA((3, 3)),
-            pltpu.SemaphoreType.DMA((2, rows // chans // min(4, rows // chans))),
+            pltpu.SemaphoreType.DMA((2, rows // chans // min(8, rows // chans))),
         ],
         compiler_params=params(58),
         cost_estimate=cost(
@@ -296,7 +296,7 @@
         for copy in copies[n][1]:
             copy.wait()
     half = rows // PAIR
-    chunk = min(4, half)
+    chunk = min(8, half)
     lanes = lax.broadcasted_iota(jnp.int32, (width, chans_in), 0)
 
     def result(place, step):
@@ -348,7 +348,7 @@
             pltpu.VMEM((depth * 3 * filters, 3 * chans_in), BF16),
             pltpu.VMEM((PAIR, rows // PAIR, width, chans_in), F32),
             pltpu.SemaphoreType.DMA((depth, 3)),
-            pltpu.SemaphoreType.DMA((PAIR, rows // PAIR // min(4, rows // PAIR))),
+            pltpu.SemaphoreType.DMA((PAIR, rows // PAIR // min(8, rows // PAIR))),
         ],
         compiler_params=params(58),
         cost_estimate=cost(

time: 163 us -> 163 us (level)
  transfers between devices with their start and end apart: 21 -> 21, of which waited for: 9 -> 9; matrix products, arithmetic and copies ran while one was open for 9% -> 9% of each run, Pallas kernels for 27% -> 26%
where the time goes in v5:
time: 163 us; the launch traced here: 162 us
  waiting for transfers between devices  56.6 us (35%)
  Pallas kernels  42.3 us (26%)
  starting transfers between devices  31.6 us (19%)
  between operations  14.4 us (9%)
  other arithmetic  10.9 us (7%)
  local copies, waits for them, and re-layouts  6.4 us (4%)
    ppermute x2, waiting for transfers between devices, line_step(): along[step] = lax.ppermute(along[step - 1], 'filt', down)  26.4 us
    pallas_call x2, Pallas kernels, input_partial(): pl.pallas_call(functools.partial(input_kernel, chans), out_shape=(half, h...  13.9 us
    pallas_call x2, Pallas kernels, forward_partial(): pl.pallas_call(functools.partial(forward_kernel, depth, chans, which), ou...  13.2 us
    ppermute x1, waiting for transfers between devices, line_step(): along[depth - 1] = along[1 - depth] = lax.ppermute(along[0], 'filt', across)  11.8 us
    pallas_call x1, Pallas kernels, weight_gradient(): pl.pallas_call(functools.partial(weight_kernel, depth, scale), out_shape=...  10.8 us
    ppermute x6, starting transfers between devices, pair_swap(): return lax.ppermute(value, 'filt', pairs)  8.38 us
    ppermute x1, starting transfers between devices, line_step(): along[depth - 1] = along[1 - depth] = lax.ppermute(along[0], 'filt', across)  6.56 us
    ppermute x2, starting transfers between devices, line_step(): along[-step] = lax.ppermute(along[1 - step], 'filt', up)  5.76 us
  transfers between devices with their start and end apart: 21, of which 9 were waited for; matrix products, arithmetic and copies ran while one was open for 9% of the time, Pallas kernels for 26%

profile of v5, /device:TPU:0, one launch (start us, length us, event | category | flops | bytes accessed | tf_op | source)
XLA Modules:
  0.0 162.2 jit_solution(904753405703318608)
XLA Ops:
  7.2 3.0 %collective-permute-start.4 = (bf16[16,128,128]{2,1,0:T(8,128)(2,1)}, bf16[16,128,128]{2,1,0:T(8,128)(2,1)S(1)}, u32[]{:S(2)}, u32[]{:S(2)}) collective-permute-start(bf16[16,128,128]{2,1,0:T(8,128)(2,1)} %bitcast.42), channel_id=1, source_target_pairs={{0,16},{8,24},{16,0},{24,8},{1,17},{9,25},{17,1},{25,9},{2,18},{10... | collective-permute-start | bytes 1572872 | tf_op jit(solution)/shard_map/ppermute | solution.py:364
  10.2 4.3 %collective-permute-start = (bf16[8,128,256]{2,1,0:T(8,128)(2,1)}, bf16[8,128,256]{2,1,0:T(8,128)(2,1)}, u32[]{:S(2)}, u32[]{:S(2)}) collective-permute-start(bf16[8,128,256]{2,1,0:T(8,128)(2,1)} %bitcast.44), channel_id=1, source_target_pairs={{0,2},{1,3},{2,4},{3,5},{4,6},{5,7},{8,10},{9,11},{10,12},{11,13},... | collective-permute-start | bytes 1572872 | tf_op jit(solution)/shard_map/ppermute | solution.py:376
  14.5 1.3 collective-permute-start.1
  15.8 6.6 %collective-permute-start.2 = (bf16[8,128,256]{2,1,0:T(8,128)(2,1)}, bf16[8,128,256]{2,1,0:T(8,128)(2,1)S(1)}, u32[]{:S(2)}, u32[]{:S(2)}) collective-permute-start(bf16[8,128,256]{2,1,0:T(8,128)(2,1)} %bitcast.46), channel_id=1, source_target_pairs={{0,6},{1,7},{6,0},{7,1},{8,14},{9,15},{14,8},{15,9},{16,22},{17,23... | collective-permute-start | bytes 1572872 | tf_op jit(solution)/shard_map/ppermute | solution.py:381
  22.4 1.6 collective-permute-start.3
  24.0 1.1 pad_maximum_fusion.1
  25.1 1.3 collective-permute-done
  26.4 4.0 %collective-permute-done.1 = bf16[8,128,256]{2,1,0:T(8,128)(2,1)} collective-permute-done((bf16[8,128,256]{2,1,0:T(8,128)(2,1)}, bf16[8,128,256]{2,1,0:T(8,128)(2,1)}, u32[]{:S(2)}, u32[]{:S(2)}) %collective-permute-start.1) | collective-permute-done | bytes 524320 | tf_op jit(solution)/shard_map/ppermute | solution.py:377
  30.3 11.8 %collective-permute-done.2 = bf16[8,128,256]{2,1,0:T(8,128)(2,1)S(1)} collective-permute-done((bf16[8,128,256]{2,1,0:T(8,128)(2,1)}, bf16[8,128,256]{2,1,0:T(8,128)(2,1)S(1)}, u32[]{:S(2)}, u32[]{:S(2)}) %collective-permute-start.2) | collective-permute-done | bytes 524320 | tf_op jit(solution)/shard_map/ppermute | solution.py:381
  43.3 1.5 collective-permute-start.6
  44.8 1.3 collective-permute-start.7
  46.1 2.3 %fusion = (bf16[8,128,256]{2,1,0:T(8,128)(2,1)}, bf16[8,128,256]{2,1,0:T(8,128)(2,1)}) fusion(bf16[8,128,256]{2,1,0:T(8,128)(2,1)S(1)} %collective-permute-done.2, bf16[8,128,256]{2,1,0:T(8,128)(2,1)} %collective-permute-done.1, pred[]{:T(512)S(6)} %eq.19, pred[]{:T(512)S(6)} %eq.18, pred[]{:T(512)S(6)} %eq.9, bf16[8,128,256]{2,1,0:T(8,128)(2,1)} %collective-permute-done), kind=kLoop, calls=%fused_computation.7 | loop fusion | flops 1572864 | bytes 2621443 | tf_op jit(solution)/shard_map/jit(_where)/select_n | solution.py:50
  48.4 1.5 collective-permute-start.8
  52.3 1.1 fusion.2.cot
  54.5 3.9 %all-to-all-start = ((bf16[4,18,32,128]{3,2,1,0:T(8,128)(2,1)}), bf16[4,18,32,128]{3,2,1,0:T(8,128)(2,1)S(1)}, u32[]{:S(2)}, u32[]{:S(2)}) async-start(bf16[4,18,32,128]{3,2,1,0:T(8,128)(2,1)} %pad_maximum_fusion.2), calls=%async_computation | async-start | bytes 1179648 | tf_op jit(solution)/shard_map/all_to_all | solution.py:424
  58.4 22.5 %collective-permute-done.7 = bf16[8,128,256]{2,1,0:T(8,128)(2,1)} collective-permute-done((bf16[8,128,256]{2,1,0:T(8,128)(2,1)}, bf16[8,128,256]{2,1,0:T(8,128)(2,1)}, u32[]{:S(2)}, u32[]{:S(2)}) %collective-permute-start.7) | collective-permute-done | bytes 524320 | tf_op jit(solution)/shard_map/ppermute | solution.py:377
  80.9 2.1 %select_select_fusion.refs_3_ = bf16[8,128,256]{2,1,0:T(8,128)(2,1)} fusion(bf16[8,128,256]{2,1,0:T(8,128)(2,1)} %collective-permute-done.6, bf16[8,128,256]{2,1,0:T(8,128)(2,1)} %collective-permute-done.7, pred[]{:T(512)S(6)} %eq.18, pred[]{:T(512)S(6)} %eq.9), kind=kLoop, calls=%fused_computation.3 | loop fusion | flops 524288 | bytes 1572866 | tf_op jit(solution)/shard_map/jit(_where)/select_n | solution.py:50
  83.0 1.5 collective-permute-start.10
  85.8 1.5 all-gather.3.cloned.1.call-done.kernels
  87.3 3.9 %all-to-all-done = bf16[4,18,32,128]{3,2,1,0:T(8,128)(2,1)S(1)} async-done(((bf16[4,18,32,128]{3,2,1,0:T(8,128)(2,1)}), bf16[4,18,32,128]{3,2,1,0:T(8,128)(2,1)S(1)}, u32[]{:S(2)}, u32[]{:S(2)}) %all-to-all-start) | async-done | bytes 589856 | tf_op jit(solution)/shard_map/all_to_all | solution.py:424
  91.8 4.2 %collective-permute-done.10.refs_7_ = bf16[8,128,256]{2,1,0:T(8,128)(2,1)} collective-permute-done((bf16[8,128,256]{2,1,0:T(8,128)(2,1)}, bf16[8,128,256]{2,1,0:T(8,128)(2,1)}, u32[]{:S(2)}, u32[]{:S(2)}) %collective-permute-start.10) | collective-permute-done | bytes 524320 | tf_op jit(solution)/shard_map/ppermute | solution.py:391
  96.0 6.6 %forward.2 = (f32[16,128,128]{2,1,0:T(8,128)}, f32[16,128,128]{2,1,0:T(8,128)}) custom-call(s32[8]{0:T(128)} %concatenate.6.at, bf16[3,3,128,256]{3,2,1,0:T(8,128)(2,1)} %weights.3, bf16[8,128,256]{2,1,0:T(8,128)(2,1)} %bitcast.48, bf16[8,128,256]{2,1,0:T(8,128)(2,1)} %get-tuple-element.54.refs_1_, bf16[8,128,256]{2,1,0:T(8,128)(2,1)} %get-tuple-element.53.refs_2_, ...), custom_call_target="tpu_custom_call" | custom-call | flops 2415919104 | bytes 6291456 | tf_op jit(solution)/shard_map/forward/pallas_call | solution.py:136
  102.7 3.2 %collective-permute-done.14 = bf16[4,18,32,128]{3,2,1,0:T(8,128)(2,1)S(1)} collective-permute-done((bf16[4,18,32,128]{3,2,1,0:T(8,128)(2,1)S(1)}, bf16[4,18,32,128]{3,2,1,0:T(8,128)(2,1)S(1)}, u32[]{:S(2)}, u32[]{:S(2)}) %collective-permute-start.14) | collective-permute-done | bytes 589856 | tf_op jit(solution)/shard_map/ppermute | solution.py:364
  106.1 1.3 add.101
  107.9 6.6 %forward.3 = (f32[16,128,128]{2,1,0:T(8,128)}, f32[16,128,128]{2,1,0:T(8,128)}) custom-call(s32[8]{0:T(128)} %concatenate.6.at, bf16[3,3,128,256]{3,2,1,0:T(8,128)(2,1)} %weights.3, bf16[8,128,256]{2,1,0:T(8,128)(2,1)} %bitcast.49, bf16[8,128,256]{2,1,0:T(8,128)(2,1)} %get-tuple-element.54.refs_1_, bf16[8,128,256]{2,1,0:T(8,128)(2,1)} %get-tuple-element.53.refs_2_, ...), custom_call_target="tpu_custom_call" | custom-call | flops 2415919104 | bytes 6291456 | tf_op jit(solution)/shard_map/forward/pallas_call | solution.py:136
  115.8 4.4 %turned.1.cot = bf16[4,18,128,128]{3,2,1,0:T(8,128)(2,1)} custom-call(bf16[2,4,18,32,128]{4,3,2,1,0:T(8,128)(2,1)} %copy-done, bf16[2,4,18,32,128]{4,3,2,1,0:T(8,128)(2,1)} %copy-done.2), custom_call_target="tpu_custom_call" | custom-call | bytes 4718592 | tf_op jit(solution)/shard_map/turned/pallas_call | solution.py:246
  120.2 6.9 %input_gradient.2 = (f32[8,128,128]{2,1,0:T(8,128)}, f32[8,128,128]{2,1,0:T(8,128)}) custom-call(s32[8]{0:T(128)} %concatenate.6.at, bf16[4,18,128,128]{3,2,1,0:T(8,128)(2,1)} %turned.1.cot, bf16[4,9,128,128]{3,2,1,0:T(8,128)(2,1)} %all-gather.3.cloned.1.call-done.kernels), custom_call_target="tpu_custom_call" | custom-call | flops 2415919104 | bytes 3538944 | tf_op jit(solution)/shard_map/input_gradient/pallas_call | solution.py:340
  127.1 1.6 %collective-permute-start.16 = (f32[8,128,128]{2,1,0:T(8,128)}, f32[8,128,128]{2,1,0:T(8,128)}, u32[]{:S(2)}, u32[]{:S(2)}) collective-permute-start(f32[8,128,128]{2,1,0:T(8,128)} %get-tuple-element.41), channel_id=1, source_target_pairs={{0,1},{1,0},{2,3},{3,2},{4,5},{5,4},{6,7},{7,6},{8,9},{9,8},{10,11... | collective-permute-start | bytes 1572872 | tf_op jit(solution)/shard_map/ppermute | solution.py:391
  128.8 4.2 %collective-permute-done.12 = f32[16,128,128]{2,1,0:T(8,128)S(1)} collective-permute-done((f32[16,128,128]{2,1,0:T(8,128)}, f32[16,128,128]{2,1,0:T(8,128)S(1)}, u32[]{:S(2)}, u32[]{:S(2)}) %collective-permute-start.12) | collective-permute-done | bytes 1048608 | tf_op jit(solution)/shard_map/ppermute | solution.py:468
  132.9 6.9 %input_gradient.3 = (f32[8,128,128]{2,1,0:T(8,128)}, f32[8,128,128]{2,1,0:T(8,128)}) custom-call(s32[8]{0:T(128)} %concatenate.6.at, bf16[4,18,128,128]{3,2,1,0:T(8,128)(2,1)} %turned.1.cot, bf16[4,9,128,128]{3,2,1,0:T(8,128)(2,1)} %all-gather.5.cloned.1.call-done.kernels), custom_call_target="tpu_custom_call" | custom-call | flops 2415919104 | bytes 3538944 | tf_op jit(solution)/shard_map/input_gradient/pallas_call | solution.py:340
  139.9 1.6 collective-permute-start.17
  143.6 10.8 %weight_gradient.1 = f32[3,384,256]{2,1,0:T(8,128)} custom-call(s32[8]{0:T(128)} %concatenate.6.at, bf16[66,128,128]{2,1,0:T(8,128)(2,1)} %copy-done.1, bf16[8,128,256]{2,1,0:T(8,128)(2,1)} %bitcast.50, bf16[8,128,256]{2,1,0:T(8,128)(2,1)} %get-tuple-element.54.refs_1_, bf16[8,128,256]{2,1,0:T(8,128)(2,1)} %get-tuple-element.53.refs_2_, ...), custom_call_target="tpu_custom_call" | custom-call | flops 4831838208 | bytes 6291456 | tf_op jit(solution)/shard_map/weight_gradient/pallas_call | solution.py:212
  (55 shorter events, 11.4 us)
Async XLA Ops:
  7.2 35.0 %copy-start.5 = (bf16[3,3,128,256]{3,2,1,0:T(8,128)(2,1)S(1)}, bf16[3,3,128,256]{3,2,1,0:T(8,128)(2,1)}, u32[]{:S(2)}) copy-start(bf16[3,3,128,256]{3,2,1,0:T(8,128)(2,1)} %weights.3) | copy-start | bytes 1769476
  7.2 80.2 %all-gather.3.cloned.1.call-start = ((), (), s32[]{:S(2)}) async-start(), calls=%async_computation.1 | async-start | bytes 1474560 | tf_op jit(solution)/shard_map/all_gather | solution.py:430
  7.2 16.7 %collective-permute-start.4 = (bf16[16,128,128]{2,1,0:T(8,128)(2,1)}, bf16[16,128,128]{2,1,0:T(8,128)(2,1)S(1)}, u32[]{:S(2)}, u32[]{:S(2)}) collective-permute-start(bf16[16,128,128]{2,1,0:T(8,128)(2,1)} %bitcast.42), channel_id=1, source_target_pairs={{0,16},{8,24},{16,0},{24,8},{1,17},{9,25},{17,1},{25,9},{2,18},{10... | collective-permute-start | bytes 1572872 | tf_op jit(solution)/shard_map/ppermute | solution.py:364
  10.2 16.1 %collective-permute-start = (bf16[8,128,256]{2,1,0:T(8,128)(2,1)}, bf16[8,128,256]{2,1,0:T(8,128)(2,1)}, u32[]{:S(2)}, u32[]{:S(2)}) collective-permute-start(bf16[8,128,256]{2,1,0:T(8,128)(2,1)} %bitcast.44), channel_id=1, source_target_pairs={{0,2},{1,3},{2,4},{3,5},{4,6},{5,7},{8,10},{9,11},{10,12},{11,13},... | collective-permute-start | bytes 1572872 | tf_op jit(solution)/shard_map/ppermute | solution.py:376
  14.5 15.8 %collective-permute-start.1 = (bf16[8,128,256]{2,1,0:T(8,128)(2,1)}, bf16[8,128,256]{2,1,0:T(8,128)(2,1)}, u32[]{:S(2)}, u32[]{:S(2)}) collective-permute-start(bf16[8,128,256]{2,1,0:T(8,128)(2,1)} %bitcast.45), channel_id=1, source_target_pairs={{2,0},{3,1},{4,2},{5,3},{6,4},{7,5},{10,8},{11,9},{12,10},{13,11},... | collective-permute-start | bytes 1572872 | tf_op jit(solution)/shard_map/ppermute | solution.py:377
  15.8 26.4 %collective-permute-start.2 = (bf16[8,128,256]{2,1,0:T(8,128)(2,1)}, bf16[8,128,256]{2,1,0:T(8,128)(2,1)S(1)}, u32[]{:S(2)}, u32[]{:S(2)}) collective-permute-start(bf16[8,128,256]{2,1,0:T(8,128)(2,1)} %bitcast.46), channel_id=1, source_target_pairs={{0,6},{1,7},{6,0},{7,1},{8,14},{9,15},{14,8},{15,9},{16,22},{17,23... | collective-permute-start | bytes 1572872 | tf_op jit(solution)/shard_map/ppermute | solution.py:381
  22.4 19.8 %collective-permute-start.3 = (bf16[8,128,256]{2,1,0:T(8,128)(2,1)}, bf16[8,128,256]{2,1,0:T(8,128)(2,1)S(1)}, u32[]{:S(2)}, u32[]{:S(2)}) collective-permute-start(bf16[8,128,256]{2,1,0:T(8,128)(2,1)} %bitcast.47), channel_id=1, source_target_pairs={{0,1},{1,0},{2,3},{3,2},{4,5},{5,4},{6,7},{7,6},{8,9},{9,8},{10,11... | collective-permute-start | bytes 1572872 | tf_op jit(solution)/shard_map/ppermute | solution.py:391
  42.2 1.0 copy-start.8
  42.2 8.8 %collective-permute-start.5 = (bf16[2,16,128,128]{3,2,1,0:T(8,128)(2,1)S(1)}, bf16[2,16,128,128]{3,2,1,0:T(8,128)(2,1)}, u32[]{:S(2)}, u32[]{:S(2)}) collective-permute-start(bf16[2,16,128,128]{3,2,1,0:T(8,128)(2,1)S(1)} %pad_maximum_fusion.1), channel_id=1, source_target_pairs={{0,8},{8,0},{16,24},{24,16},{1,9},{9,1},{17,25},{25,17},{2,10},{10... | collective-permute-start | bytes 3145736 | tf_op jit(solution)/shard_map/ppermute | solution.py:386
  43.3 15.1 %collective-permute-start.6 = (bf16[8,128,256]{2,1,0:T(8,128)(2,1)}, bf16[8,128,256]{2,1,0:T(8,128)(2,1)}, u32[]{:S(2)}, u32[]{:S(2)}) collective-permute-start(bf16[8,128,256]{2,1,0:T(8,128)(2,1)} %collective-permute-done), channel_id=1, source_target_pairs={{2,4},{3,5},{4,6},{5,7},{10,12},{11,13},{12,14},{13,15},{18,20},{1... | collective-permute-start | bytes 1572872 | tf_op jit(solution)/shard_map/ppermute | solution.py:376
  44.8 36.1 %collective-permute-start.7 = (bf16[8,128,256]{2,1,0:T(8,128)(2,1)}, bf16[8,128,256]{2,1,0:T(8,128)(2,1)}, u32[]{:S(2)}, u32[]{:S(2)}) collective-permute-start(bf16[8,128,256]{2,1,0:T(8,128)(2,1)} %collective-permute-done.1), channel_id=1, source_target_pairs={{2,0},{3,1},{4,2},{5,3},{10,8},{11,9},{12,10},{13,11},{18,16},{19,... | collective-permute-start | bytes 1572872 | tf_op jit(solution)/shard_map/ppermute | solution.py:377
  48.4 32.5 %collective-permute-start.8 = (bf16[8,128,256]{2,1,0:T(8,128)(2,1)}, bf16[8,128,256]{2,1,0:T(8,128)(2,1)}, u32[]{:S(2)}, u32[]{:S(2)}) collective-permute-start(bf16[8,128,256]{2,1,0:T(8,128)(2,1)} %get-tuple-element.54.refs_1_), channel_id=1, source_target_pairs={{0,1},{1,0},{2,3},{3,2},{4,5},{5,4},{6,7},{7,6},{8,9},{9,8},{10,11... | collective-permute-start | bytes 1572872 | tf_op jit(solution)/shard_map/ppermute | solution.py:391
  49.9 31.0 %collective-permute-start.9 = (bf16[8,128,256]{2,1,0:T(8,128)(2,1)}, bf16[8,128,256]{2,1,0:T(8,128)(2,1)}, u32[]{:S(2)}, u32[]{:S(2)}) collective-permute-start(bf16[8,128,256]{2,1,0:T(8,128)(2,1)} %get-tuple-element.53.refs_2_), channel_id=1, source_target_pairs={{0,1},{1,0},{2,3},{3,2},{4,5},{5,4},{6,7},{7,6},{8,9},{9,8},{10,11... | collective-permute-start | bytes 1572872 | tf_op jit(solution)/shard_map/ppermute | solution.py:391
  53.4 29.6 %copy-start.1 = (bf16[66,128,128]{2,1,0:T(8,128)(2,1)}, bf16[66,128,128]{2,1,0:T(8,128)(2,1)S(1)}, u32[]{:S(2)}) copy-start(bf16[66,128,128]{2,1,0:T(8,128)(2,1)S(1)} %fusion.2.cot) | copy-start | bytes 6488068
  54.5 36.8 %all-to-all-start = ((bf16[4,18,32,128]{3,2,1,0:T(8,128)(2,1)}), bf16[4,18,32,128]{3,2,1,0:T(8,128)(2,1)S(1)}, u32[]{:S(2)}, u32[]{:S(2)}) async-start(bf16[4,18,32,128]{3,2,1,0:T(8,128)(2,1)} %pad_maximum_fusion.2), calls=%async_computation | async-start | bytes 1179648 | tf_op jit(solution)/shard_map/all_to_all | solution.py:424
  58.4 74.5 %all-gather.5.cloned.1.call-start = ((), (), s32[]{:S(2)}) async-start(), calls=%async_computation.2 | async-start | bytes 1474560 | tf_op jit(solution)/shard_map/all_gather | solution.py:430
  83.0 13.0 %collective-permute-start.10 = (bf16[8,128,256]{2,1,0:T(8,128)(2,1)}, bf16[8,128,256]{2,1,0:T(8,128)(2,1)}, u32[]{:S(2)}, u32[]{:S(2)}) collective-permute-start(bf16[8,128,256]{2,1,0:T(8,128)(2,1)} %select_select_fusion.refs_3_), channel_id=1, source_target_pairs={{0,1},{1,0},{2,3},{3,2},{4,5},{5,4},{6,7},{7,6},{8,9},{9,8},{10,11... | collective-permute-start | bytes 1572872 | tf_op jit(solution)/shard_map/ppermute | solution.py:391
  91.3 14.6 %collective-permute-start.14 = (bf16[4,18,32,128]{3,2,1,0:T(8,128)(2,1)S(1)}, bf16[4,18,32,128]{3,2,1,0:T(8,128)(2,1)S(1)}, u32[]{:S(2)}, u32[]{:S(2)}) collective-permute-start(bf16[4,18,32,128]{3,2,1,0:T(8,128)(2,1)S(1)} %all-to-all-done), channel_id=1, source_target_pairs={{0,16},{8,24},{16,0},{24,8},{1,17},{9,25},{17,1},{25,9},{2,18},{10... | collective-permute-start | bytes 1769480 | tf_op jit(solution)/shard_map/ppermute | solution.py:364
  102.6 3.5 %copy-start.4 = (f32[16,128,128]{2,1,0:T(8,128)S(1)}, f32[16,128,128]{2,1,0:T(8,128)}, u32[]{:S(2)}) copy-start(f32[16,128,128]{2,1,0:T(8,128)} %get-tuple-element.33) | copy-start | bytes 3145732
  102.6 3.5 %collective-permute-start.11 = (f32[16,128,128]{2,1,0:T(8,128)}, f32[16,128,128]{2,1,0:T(8,128)S(1)}, u32[]{:S(2)}, u32[]{:S(2)}) collective-permute-start(f32[16,128,128]{2,1,0:T(8,128)} %get-tuple-element.34), channel_id=1, source_target_pairs={{0,8},{8,0},{16,24},{24,16},{1,9},{9,1},{17,25},{25,17},{2,10},{10... | collective-permute-start | bytes 3145736 | tf_op jit(solution)/shard_map/ppermute | solution.py:386
  106.0 8.5 %copy-start = (bf16[2,4,18,32,128]{4,3,2,1,0:T(8,128)(2,1)}, bf16[2,4,18,32,128]{4,3,2,1,0:T(8,128)(2,1)S(1)}, u32[]{:S(2)}) copy-start(bf16[2,4,18,32,128]{4,3,2,1,0:T(8,128)(2,1)S(1)} %pad_maximum_fusion.same) | copy-start | bytes 3538948
  106.0 8.7 %collective-permute-start.15 = (bf16[2,4,18,32,128]{4,3,2,1,0:T(8,128)(2,1)S(1)}, bf16[2,4,18,32,128]{4,3,2,1,0:T(8,128)(2,1)S(1)}, u32[]{:S(2)}, u32[]{:S(2)}) collective-permute-start(bf16[2,4,18,32,128]{4,3,2,1,0:T(8,128)(2,1)S(1)} %pad_maximum_fusion.same), channel_id=1, source_target_pairs={{0,8},{8,0},{16,24},{24,16},{1,9},{9,1},{17,25},{25,17},{2,10},{10... | collective-permute-start | bytes 3538952 | tf_op jit(solution)/shard_map/ppermute | solution.py:386
  107.3 25.6 %collective-permute-start.12 = (f32[16,128,128]{2,1,0:T(8,128)}, f32[16,128,128]{2,1,0:T(8,128)S(1)}, u32[]{:S(2)}, u32[]{:S(2)}) collective-permute-start(f32[16,128,128]{2,1,0:T(8,128)} %add.101), channel_id=1, source_target_pairs={{0,16},{8,24},{16,0},{24,8},{1,17},{9,25},{17,1},{25,9},{2,18},{10... | collective-permute-start | bytes 3145736 | tf_op jit(solution)/shard_map/ppermute | solution.py:468
  114.5 27.0 %collective-permute-start.13 = (f32[16,128,128]{2,1,0:T(8,128)}, f32[16,128,128]{2,1,0:T(8,128)S(1)}, u32[]{:S(2)}, u32[]{:S(2)}) collective-permute-start(f32[16,128,128]{2,1,0:T(8,128)} %get-tuple-element.38), channel_id=1, source_target_pairs={{0,8},{8,0},{16,24},{24,16},{1,9},{9,1},{17,25},{25,17},{2,10},{10... | collective-permute-start | bytes 3145736 | tf_op jit(solution)/shard_map/ppermute | solution.py:386
  114.7 1.1 copy-start.2
  127.1 14.4 %copy-start.3 = (f32[16,128,128]{2,1,0:T(8,128)S(1)}, f32[16,128,128]{2,1,0:T(8,128)}, u32[]{:S(2)}) copy-start(f32[16,128,128]{2,1,0:T(8,128)} %get-tuple-element.37) | copy-start | bytes 3145732
  127.1 15.4 %collective-permute-start.16 = (f32[8,128,128]{2,1,0:T(8,128)}, f32[8,128,128]{2,1,0:T(8,128)}, u32[]{:S(2)}, u32[]{:S(2)}) collective-permute-start(f32[8,128,128]{2,1,0:T(8,128)} %get-tuple-element.41), channel_id=1, source_target_pairs={{0,1},{1,0},{2,3},{3,2},{4,5},{5,4},{6,7},{7,6},{8,9},{9,8},{10,11... | collective-permute-start | bytes 1572872 | tf_op jit(solution)/shard_map/ppermute | solution.py:391
  139.9 2.6 %copy-start.7 = (f32[8,128,128]{2,1,0:T(8,128)S(1)}, f32[8,128,128]{2,1,0:T(8,128)}, u32[]{:S(2)}) copy-start(f32[8,128,128]{2,1,0:T(8,128)} %get-tuple-element.40) | copy-start | bytes 1572868
  139.9 14.5 %collective-permute-start.17 = (f32[8,128,128]{2,1,0:T(8,128)}, f32[8,128,128]{2,1,0:T(8,128)S(1)}, u32[]{:S(2)}, u32[]{:S(2)}) collective-permute-start(f32[8,128,128]{2,1,0:T(8,128)} %get-tuple-element.44), channel_id=1, source_target_pairs={{0,1},{1,0},{2,3},{3,2},{4,5},{5,4},{6,7},{7,6},{8,9},{9,8},{10,11... | collective-permute-start | bytes 1572872 | tf_op jit(solution)/shard_map/ppermute | solution.py:391
  143.6 10.8 %copy-start.6 = (f32[8,128,128]{2,1,0:T(8,128)S(1)}, f32[8,128,128]{2,1,0:T(8,128)}, u32[]{:S(2)}) copy-start(f32[8,128,128]{2,1,0:T(8,128)} %get-tuple-element.43) | copy-start | bytes 1572868
Sparse Core Ops, SparseCore 0:
  43.3 43.9 all-gather.2
  102.8 29.7 all-gather.4
